TPU v7x, 32 devices: a whole 2x2x4 slice. The times are simulated.
32 devices in a mesh: dp: 8 (over z, y), tensor: 4 (over x, core).
Axes of the slice: x: 2, y: 2, z: 4, core: 2. Of those that a mesh axis runs over, the one named last changes fastest.
Arguments:
- tokens: bfloat16 [8192, 1024], P('dp'), may hold values from -6 to 6
- lengths: int32 [8], P('dp'), may hold values from 256 to 1024, as said below
- chosen: int32 [8192, 8], P('dp'), may hold values from 0 to 15, all different within a row
- gate_values: float32 [8192, 8], P('dp'), may hold values from 0.05 to 0.25
- cotangent: bfloat16 [8192, 1024], P('dp'), may hold values from -6 to 6
- norm_attn: float32 [1024], replicated, may hold values from 0.5 to 1.5
- w_query: bfloat16 [1024, 1024], P(None, 'tensor'), may hold values from -0.1875 to 0.1875
- w_key: bfloat16 [1024, 512], P(None, 'tensor'), may hold values from -0.1875 to 0.1875
- w_value: bfloat16 [1024, 512], P(None, 'tensor'), may hold values from -0.1875 to 0.1875
- w_out: bfloat16 [1024, 1024], P('tensor'), may hold values from -3 to 3
- norm_moe: float32 [1024], replicated, may hold values from 0.5 to 1.5
- w_gate: bfloat16 [16, 1024, 512], P(None, None, 'tensor'), may hold values from -0.1875 to 0.1875
- w_up: bfloat16 [16, 1024, 512], P(None, None, 'tensor'), may hold values from -0.1875 to 0.1875
- w_down: bfloat16 [16, 512, 1024], P(None, 'tensor'), may hold values from -1 to 1
Outputs:
- result: bfloat16 [8192, 1024], P('dp')
- grad_tokens: bfloat16 [8192, 1024], P('dp')
- grad_gates: float32 [8192, 8], P('dp')
- grad_norm_attn: float32 [1024], replicated
- grad_query: float32 [1024, 1024], P(None, 'tensor')
- grad_key: float32 [1024, 512], P(None, 'tensor')
- grad_value: float32 [1024, 512], P(None, 'tensor')
- grad_out: float32 [1024, 1024], P('tensor')
- grad_norm_moe: float32 [1024], replicated
- grad_gate: float32 [16, 1024, 512], P(None, None, 'tensor')
- grad_up: float32 [16, 1024, 512], P(None, None, 'tensor')
- grad_down: float32 [16, 512, 1024], P(None, 'tensor')
Inputs may be any that keep to these rules, and one draw needn't show every extreme that they name: `lengths`: valid length of each sequence, at least 256; some sequence fills all 1024 slots.
All inputs are finite; a program needn't handle non-finite values.
Results may differ from a plain program's by a relative error of at most 0.015.
Values sent between devices are 32-bit elements; how exact they have to be, the bound alone decides.
A program may use at most 320 MiB of HBM per device.

v0:
```python
import math

import jax
import jax.numpy as jnp
from jax import lax
from jax.sharding import PartitionSpec as P

HEAD_DIM = 64
TOP_K = 8
EXPERTS = 16
CAPACITY = 640


EPSILON = 1e-05
THETA = 10000.0
NEGATIVE = -1e30


def dot_f(left, right):
    return jnp.dot(left, right, preferred_element_type=jnp.float32)


def rms_norm(values, gain):
    return values * lax.rsqrt(jnp.mean(values * values, axis=-1, keepdims=True) + EPSILON) * gain


def rope_tables(positions, width):
    half_w = width // 2
    freqs = THETA ** (-jnp.arange(half_w, dtype=jnp.float32) * 2.0 / width)
    angles = jnp.arange(positions, dtype=jnp.float32)[:, None] * freqs[None, :]
    cosine = jnp.concatenate([jnp.cos(angles), jnp.cos(angles)], axis=1)
    sine = jnp.concatenate([jnp.sin(angles), jnp.sin(angles)], axis=1)
    return (cosine, sine)


def rotate(values, cosine, sine):
    half_w = values.shape[-1] // 2
    turned = jnp.concatenate([-values[..., half_w:], values[..., :half_w]], axis=-1)
    return values * cosine[:, None, :] + turned * sine[:, None, :]


def route_pairs(valid, chosen):
    tok_rows = chosen.shape[0]
    live_int = valid.astype(jnp.int32)
    expert_ids = jnp.arange(EXPERTS, dtype=jnp.int32)
    hits = (
        jnp.sum((chosen[:, :, None] == expert_ids[None, None, :]).astype(jnp.int32), axis=1)
        * live_int[:, None]
    )
    before = jnp.cumsum(hits, axis=0) - hits
    places = jnp.take_along_axis(before, chosen, axis=1)
    pairs = jnp.sum(live_int) * TOP_K
    limit = (5 * pairs + 4 * EXPERTS - 1) // (4 * EXPERTS)
    kept = (places < limit) & (live_int[:, None] > 0)
    dump_at = EXPERTS * CAPACITY
    target = jnp.where(kept, chosen * CAPACITY + places, dump_at)
    row_ids = jnp.broadcast_to(jnp.arange(tok_rows, dtype=jnp.int32)[:, None], chosen.shape)
    slot_token = (
        jnp.zeros((dump_at + 1,), jnp.int32)
        .at[target.reshape(-1)]
        .set(row_ids.reshape(-1))[:dump_at]
    )
    slot_live = jnp.zeros((dump_at + 1,), jnp.int32).at[target.reshape(-1)].set(1)[:dump_at]
    return (slot_token, slot_live, target, kept)


def block_scores(q_block, start, k_seq, length, scaling):
    rows_q = q_block.shape[0]
    kv_here = k_seq.shape[1]
    grouped = q_block.reshape(rows_q, kv_here, q_block.shape[1] // kv_here, q_block.shape[2])
    scores = (
        jnp.einsum("qkgd,skd->kgqs", grouped, k_seq, preferred_element_type=jnp.float32) * scaling
    )
    q_pos = start + jnp.arange(rows_q, dtype=jnp.int32)
    k_pos = jnp.arange(k_seq.shape[0], dtype=jnp.int32)
    allowed = (k_pos[None, :] <= q_pos[:, None]) & (k_pos[None, :] < length)
    return (jnp.where(allowed, scores, NEGATIVE), grouped)


def forward_block(q_block, start, k_seq, v_seq, length, scaling):
    scores, grouped = block_scores(q_block, start, k_seq, length, scaling)
    top_s = jnp.max(scores, axis=-1, keepdims=True)
    expo = jnp.exp(scores - top_s)
    total = jnp.sum(expo, axis=-1, keepdims=True)
    probs = (expo / total).astype(jnp.bfloat16)
    lse_part = (top_s + jnp.log(total))[..., 0]
    out_b = jnp.einsum("kgqs,skd->qkgd", probs, v_seq, preferred_element_type=jnp.float32)
    return (out_b.reshape(q_block.shape[0], -1), lse_part)


def backward_block(q_block, d_block, start, lse_block, k_seq, v_seq, length, scaling):
    scores, grouped = block_scores(q_block, start, k_seq, length, scaling)
    exact = jnp.exp(scores - lse_block[..., None])
    probs = exact.astype(jnp.bfloat16)
    d_grouped = d_block.reshape(grouped.shape)
    d_probs = jnp.einsum("qkgd,skd->kgqs", d_grouped, v_seq, preferred_element_type=jnp.float32)
    inner = jnp.sum(exact * d_probs, axis=-1, keepdims=True)
    d_scores = (exact * (d_probs - inner)).astype(jnp.bfloat16)
    d_query = (
        jnp.einsum("kgqs,skd->qkgd", d_scores, k_seq, preferred_element_type=jnp.float32) * scaling
    )
    d_key = (
        jnp.einsum("kgqs,qkgd->skd", d_scores, grouped, preferred_element_type=jnp.float32)
        * scaling
    )
    d_value = jnp.einsum("kgqs,qkgd->skd", probs, d_grouped, preferred_element_type=jnp.float32)
    return (d_query.reshape(q_block.shape), d_key, d_value)


def attend_forward(q_all, k_all, v_all, lengths, scaling):
    seq_len = q_all.shape[1]
    q_rows = min(512, seq_len)
    n_blocks = seq_len // q_rows

    def one_sequence(item):
        q_seq, k_seq, v_seq, length = item
        outs = []
        lses = []
        for block in range(n_blocks):
            start = block * q_rows
            finish = start + q_rows
            out_b, lse_b = forward_block(
                q_seq[start:finish], start, k_seq[:finish], v_seq[:finish], length, scaling
            )
            outs.append(out_b)
            lses.append(lse_b)
        return (jnp.concatenate(outs, axis=0), jnp.stack(lses, axis=0))

    return lax.map(one_sequence, (q_all, k_all, v_all, lengths))


def attend_backward(q_all, k_all, v_all, d_all, lse_all, lengths, scaling):
    seq_len = q_all.shape[1]
    q_rows = min(512, seq_len)
    n_blocks = seq_len // q_rows

    def one_sequence(item):
        q_seq, k_seq, v_seq, d_seq, lse_seq, length = item
        sum_key = jnp.zeros(k_seq.shape, jnp.float32)
        sum_value = jnp.zeros(k_seq.shape, jnp.float32)
        d_queries = []
        for block in range(n_blocks):
            start = block * q_rows
            finish = start + q_rows
            d_query, d_key, d_value = backward_block(
                q_seq[start:finish],
                d_seq[start:finish],
                start,
                lse_seq[block],
                k_seq[:finish],
                v_seq[:finish],
                length,
                scaling,
            )
            padding = ((0, seq_len - finish), (0, 0), (0, 0))
            sum_key = sum_key + jnp.pad(d_key, padding)
            sum_value = sum_value + jnp.pad(d_value, padding)
            d_queries.append(d_query)
        return (jnp.concatenate(d_queries, axis=0), sum_key, sum_value)

    return lax.map(one_sequence, (q_all, k_all, v_all, d_all, lse_all, lengths))


def per_device(
    tokens,
    lengths,
    chosen,
    gate_values,
    cotangent,
    norm_attn,
    w_query,
    w_key,
    w_value,
    w_out,
    norm_moe,
    w_gate,
    w_up,
    w_down,
):
    seq_count = lengths.shape[0]
    tok_rows = tokens.shape[0]
    seq_len = tok_rows // seq_count
    width = tokens.shape[1]
    heads_here = w_query.shape[1] // HEAD_DIM
    kv_here = w_key.shape[1] // HEAD_DIM
    scaling = 1.0 / math.sqrt(HEAD_DIM)
    valid = (jnp.arange(seq_len, dtype=jnp.int32)[None, :] < lengths[:, None]).reshape(-1)
    valid_f = valid.astype(jnp.float32)[:, None]
    cosine, sine = rope_tables(seq_len, HEAD_DIM)
    x_in = tokens.astype(jnp.float32)
    h_attn = rms_norm(x_in, norm_attn).astype(jnp.bfloat16)
    q_lin = dot_f(h_attn, w_query).reshape(seq_count, seq_len, heads_here, HEAD_DIM)
    k_lin = dot_f(h_attn, w_key).reshape(seq_count, seq_len, kv_here, HEAD_DIM)
    v_att = (
        dot_f(h_attn, w_value).astype(jnp.bfloat16).reshape(seq_count, seq_len, kv_here, HEAD_DIM)
    )
    q_rot = rotate(q_lin, cosine, sine).astype(jnp.bfloat16)
    k_rot = rotate(k_lin, cosine, sine).astype(jnp.bfloat16)
    attended, lse_all = attend_forward(q_rot, k_rot, v_att, lengths, scaling)
    attn_cat = attended.reshape(tok_rows, heads_here * HEAD_DIM).astype(jnp.bfloat16)
    attn_sum = lax.psum(dot_f(attn_cat, w_out), "tensor")
    resid = x_in + attn_sum
    h_moe = rms_norm(resid, norm_moe).astype(jnp.bfloat16)
    slot_token, slot_live, target, kept = route_pairs(valid, chosen)
    dump_at = EXPERTS * CAPACITY
    live_f = slot_live.astype(jnp.float32)[:, None]
    dispatched = (h_moe[slot_token] * slot_live.astype(jnp.bfloat16)[:, None]).reshape(
        EXPERTS, CAPACITY, -1
    )
    gate_act = jnp.einsum("ecd,edf->ecf", dispatched, w_gate, preferred_element_type=jnp.float32)
    up_act = jnp.einsum("ecd,edf->ecf", dispatched, w_up, preferred_element_type=jnp.float32)
    sigma = jax.nn.sigmoid(gate_act)
    silu_g = gate_act * sigma
    hidden_b = (silu_g * up_act).astype(jnp.bfloat16)
    produced = jnp.einsum(
        "ecf,efd->ecd", hidden_b, w_down, preferred_element_type=jnp.float32
    ).reshape(dump_at, -1)
    weights = jnp.where(kept, gate_values, 0.0)
    slot_weight = (
        jnp.zeros((dump_at + 1,), jnp.float32)
        .at[target.reshape(-1)]
        .set(weights.reshape(-1))[:dump_at]
    )
    moe_part = (
        jnp.zeros((tok_rows, width), jnp.float32)
        .at[slot_token]
        .add(produced * slot_weight[:, None])
    )
    moe_sum = lax.psum(moe_part, "tensor")
    result = ((resid + moe_sum) * valid_f).astype(jnp.bfloat16)
    d_out = cotangent.astype(jnp.float32) * valid_f
    slot_cot = cotangent[slot_token].astype(jnp.float32)
    slot_dot = jnp.sum(slot_cot * produced, axis=-1)
    slot_dot = jnp.concatenate([slot_dot, jnp.zeros((1,), jnp.float32)])
    d_gate_part = jnp.where(kept, slot_dot[target], 0.0)
    d_prod = (slot_weight[:, None] * slot_cot).astype(jnp.bfloat16).reshape(EXPERTS, CAPACITY, -1)
    grad_down = jnp.einsum("ecf,ecd->efd", hidden_b, d_prod, preferred_element_type=jnp.float32)
    d_hidden = jnp.einsum("ecd,efd->ecf", d_prod, w_down, preferred_element_type=jnp.float32)
    d_gate_b = (d_hidden * up_act * sigma * (1.0 + gate_act * (1.0 - sigma))).astype(jnp.bfloat16)
    d_up_b = (d_hidden * silu_g).astype(jnp.bfloat16)
    grad_gate = jnp.einsum("ecd,ecf->edf", dispatched, d_gate_b, preferred_element_type=jnp.float32)
    grad_up = jnp.einsum("ecd,ecf->edf", dispatched, d_up_b, preferred_element_type=jnp.float32)
    d_disp = jnp.einsum("ecf,edf->ecd", d_gate_b, w_gate, preferred_element_type=jnp.float32)
    d_disp = (
        d_disp + jnp.einsum("ecf,edf->ecd", d_up_b, w_up, preferred_element_type=jnp.float32)
    ).reshape(dump_at, -1)
    d_h_part = jnp.zeros((tok_rows, width), jnp.float32).at[slot_token].add(d_disp * live_f)
    d_h_moe, d_gates = lax.psum((d_h_part, d_gate_part), "tensor")
    unused_m, pull_moe = jax.vjp(rms_norm, resid, norm_moe)
    d_resid_n, grad_norm_moe = pull_moe(d_h_moe)
    d_resid = d_out + d_resid_n
    d_resid_b = d_resid.astype(jnp.bfloat16)
    grad_out = jnp.einsum("tf,td->fd", attn_cat, d_resid_b, preferred_element_type=jnp.float32)
    d_attn = jnp.einsum("td,fd->tf", d_resid_b, w_out, preferred_element_type=jnp.float32).astype(
        jnp.bfloat16
    )
    d_attn = d_attn.reshape(seq_count, seq_len, heads_here, HEAD_DIM)
    d_q_rot, d_k_rot, d_v_all = attend_backward(
        q_rot, k_rot, v_att, d_attn, lse_all, lengths, scaling
    )
    unused_q, pull_query = jax.vjp(lambda values: rotate(values, cosine, sine), q_lin)
    unused_k, pull_key = jax.vjp(lambda values: rotate(values, cosine, sine), k_lin)
    d_query = pull_query(d_q_rot)[0].astype(jnp.bfloat16).reshape(tok_rows, -1)
    d_key = pull_key(d_k_rot)[0].astype(jnp.bfloat16).reshape(tok_rows, -1)
    d_value = d_v_all.astype(jnp.bfloat16).reshape(tok_rows, -1)
    grad_query = jnp.einsum("td,tf->df", h_attn, d_query, preferred_element_type=jnp.float32)
    grad_key = jnp.einsum("td,tf->df", h_attn, d_key, preferred_element_type=jnp.float32)
    grad_value = jnp.einsum("td,tf->df", h_attn, d_value, preferred_element_type=jnp.float32)
    d_h_part_a = jnp.einsum("tf,df->td", d_query, w_query, preferred_element_type=jnp.float32)
    d_h_part_a = d_h_part_a + jnp.einsum(
        "tf,df->td", d_key, w_key, preferred_element_type=jnp.float32
    )
    d_h_part_a = d_h_part_a + jnp.einsum(
        "tf,df->td", d_value, w_value, preferred_element_type=jnp.float32
    )
    d_h_attn = lax.psum(d_h_part_a, "tensor")
    unused_a, pull_attn = jax.vjp(rms_norm, x_in, norm_attn)
    d_x_n, grad_norm_attn = pull_attn(d_h_attn)
    grad_tokens = (d_resid + d_x_n).astype(jnp.bfloat16)
    summed = (
        lax.psum_scatter(grad_norm_attn, "dp", scatter_dimension=0, tiled=True),
        lax.psum_scatter(grad_query, "dp", scatter_dimension=0, tiled=True),
        lax.psum_scatter(grad_key, "dp", scatter_dimension=0, tiled=True),
        lax.psum_scatter(grad_value, "dp", scatter_dimension=0, tiled=True),
        lax.psum_scatter(grad_out, "dp", scatter_dimension=1, tiled=True),
        lax.psum_scatter(grad_norm_moe, "dp", scatter_dimension=0, tiled=True),
        lax.psum_scatter(grad_gate, "dp", scatter_dimension=1, tiled=True),
        lax.psum_scatter(grad_up, "dp", scatter_dimension=1, tiled=True),
        lax.psum_scatter(grad_down, "dp", scatter_dimension=2, tiled=True),
    )
    full = (
        lax.all_gather(summed[0], "dp", axis=0, tiled=True),
        lax.all_gather(summed[1], "dp", axis=0, tiled=True),
        lax.all_gather(summed[2], "dp", axis=0, tiled=True),
        lax.all_gather(summed[3], "dp", axis=0, tiled=True),
        lax.all_gather(summed[4], "dp", axis=1, tiled=True),
        lax.all_gather(summed[5], "dp", axis=0, tiled=True),
        lax.all_gather(summed[6], "dp", axis=1, tiled=True),
        lax.all_gather(summed[7], "dp", axis=1, tiled=True),
        lax.all_gather(summed[8], "dp", axis=2, tiled=True),
    )
    return (
        result,
        grad_tokens,
        d_gates,
        full[0],
        full[1],
        full[2],
        full[3],
        full[4],
        full[5],
        full[6],
        full[7],
        full[8],
    )


def solution(mesh):
    placed = (
        P("dp", None),
        P("dp"),
        P("dp", None),
        P("dp", None),
        P("dp", None),
        P(),
        P(None, "tensor"),
        P(None, "tensor"),
        P(None, "tensor"),
        P("tensor", None),
        P(),
        P(None, None, "tensor"),
        P(None, None, "tensor"),
        P(None, "tensor", None),
    )
    return jax.shard_map(
        per_device,
        mesh=mesh,
        in_specs=placed,
        out_specs=(
            P("dp", None),
            P("dp", None),
            P("dp", None),
            P(),
            P(None, "tensor"),
            P(None, "tensor"),
            P(None, "tensor"),
            P("tensor", None),
            P(),
            P(None, None, "tensor"),
            P(None, None, "tensor"),
            P(None, "tensor", None),
        ),
        check_vma=False,
    )
```

profile of v0, /device:TPU:0, one launch (start us, length us, event | category | flops | bytes accessed | tf_op | source)
XLA Modules:
  0.0 2006.4 jit_solution(8211791717490124012)
XLA Ops:
  32.9 4.5 reduce-window.6
  38.3 65.5 %gather_fusion.3 = s32[8192]{0:T(1024)S(1)} fusion(s32[1024,16]{0,1:T(8,128)S(1)} %fusion.89, s32[8192]{0:T(1024)S(1)} %reshape.515), kind=kCustom, calls=%fused_computation.3 | custom fusion | bytes 131072 | tf_op jit(solution)/shard_map/jit(take_along_axis)/gather | solution.py:51
  105.8 30.5 %scatter_custom_fusion = s32[10241]{0:T(1024)S(1)} fusion(s32[8192]{0:T(1024)S(1)} %bitcast.245, s32[8192]{0:T(1024)S(1)} %reshape.525, s32[]{:T(128)} %constant.82.clone.1), kind=kCustom, calls=%fused_computation.165 | custom fusion | bytes 40968 | tf_op jit(solution)/shard_map/scatter | solution.py:61
  136.3 30.5 %scatter_custom_fusion.1 = s32[10241]{0:T(1024)S(1)} fusion(s32[8192]{0:T(1024)S(1)} %bitcast.246, s32[8192]{0:T(1024)S(1)} %broadcast.300, s32[]{:T(128)} %constant.82.clone.1), kind=kCustom, calls=%fused_computation.163 | custom fusion | bytes 40968 | tf_op jit(solution)/shard_map/scatter | solution.py:63
  167.9 30.5 %scatter_custom_fusion.2 = f32[10241]{0:T(1024)S(1)} fusion(s32[8192]{0:T(1024)S(1)} %bitcast.247, f32[8192]{0:T(1024)S(1)} %reshape.541, f32[]{:T(128)} %constant.73.clone.1), kind=kCustom, calls=%fused_computation.161 | custom fusion | bytes 40968 | tf_op jit(solution)/shard_map/scatter | solution.py:222
  200.3 44.0 %gather_fusion.1 = bf16[10240,1024]{1,0:T(8,128)(2,1)} fusion(bf16[1024,1024]{1,0:T(8,128)(2,1)S(1)} %copy-done.2, s32[10240]{0:T(1024)S(1)} %get-tuple-element.131), kind=kCustom, calls=%fused_computation.1 | custom fusion | bytes 41984000 | tf_op jit(solution)/shard_map/gather | solution.py:232
  250.2 44.1 %gather_fusion = bf16[10240,1024]{1,0:T(8,128)(2,1)} fusion(bf16[1024,1024]{1,0:T(8,128)(2,1)S(1)} %multiply_convert_fusion.4, s32[10240]{0:T(1024)S(1)} %get-tuple-element.131), kind=kCustom, calls=%fused_computation | custom fusion | bytes 41984000 | tf_op jit(solution)/shard_map/gather | solution.py:207
  294.3 28.2 %copy.119 = bf16[16,640,1024]{1,2,0:T(8,128)(2,1)} copy(bf16[16,640,1024]{2,1,0:T(8,128)(2,1)} %bitcast.207) | data formatting | bytes 41943040 | tf_op jit(solution)/shard_map/gather | solution.py:207
  322.6 13.1 fusion.10
  335.7 12.2 fusion.12
  347.9 18.0 multiply_convert_fusion
  365.9 19.4 fusion.111
  385.3 28.9 %convolution_add_fusion = f32[16,640,1024]{2,1,0:T(8,128)} fusion(f32[16,640,1024]{2,1,0:T(8,128)} %fusion.111, bf16[16,640,128]{2,1,0:T(8,128)(2,1)} %get-tuple-element.112, bf16[16,1024,128]{2,1,0:T(8,128)(2,1)} %param.26), kind=kOutput, calls=%fused_computation.25 | convolution fusion | flops 2694840320 | bytes 90701824 | tf_op jit(solution)/shard_map/ecf,edf->ecd/dot_general | solution.py:245
  414.2 28.1 %bitcast_multiply_fusion = f32[10240,1024]{1,0:T(8,128)} fusion(f32[16,640,1024]{2,1,0:T(8,128)} %convolution_add_fusion, f32[10240]{0:T(1024)S(1)} %copy-done.57), kind=kLoop, calls=%fused_computation.13 | loop fusion | flops 10485760 | bytes 83927040 | tf_op jit(solution)/shard_map/mul | solution.py:247
  442.4 90.5 %scatter_custom_fusion.4 = f32[1024,1024]{1,0:T(8,128)} fusion(s32[10240]{0:T(1024)} %get-tuple-element.132, f32[10240,1024]{1,0:T(8,128)} %bitcast_multiply_fusion, f32[]{:T(128)} %constant.73.clone.1), kind=kCustom, calls=%fused_computation.84 | custom fusion | flops 10485760 | bytes 4194816 | tf_op jit(solution)/shard_map/scatter-add | solution.py:247
  533.1 88.2 %all-reduce.16.cloned.1.call-done = f32[1024,1024]{1,0:T(8,128)} async-done(((f32[1024,1024]{1,0:T(8,128)}), f32[1024,1024]{1,0:T(8,128)}) %all-reduce.16.cloned.1.call-update) | async-done | bytes 4194320 | tf_op jit(solution)/shard_map/psum | solution.py:248
  621.3 5.2 multiply_reduce_fusion
  640.3 5.3 fusion.18
  653.8 12.8 fusion.8
  666.7 13.3 fusion.6
  680.1 12.2 fusion.2
  699.3 4.9 fusion.60
  705.7 3.7 fusion.56
  711.9 24.6 %fusion.1 = (f32[16,640]{1,0:T(8,128)S(1)}, f32[16,640,1024]{2,1,0:T(8,128)}) fusion(bf16[16,640,1024]{2,1,0:T(8,128)(2,1)} %bitcast.204, bf16[16,640,128]{2,1,0:T(8,128)(2,1)} %get-tuple-element.114, bf16[16,128,1024]{2,1,0:T(8,128)(2,1)} %param.27), kind=kOutput, calls=%fused_computation.12 | convolution fusion | flops 2715801600 | bytes 69771264 | tf_op jit(solution)/shard_map/ecf,efd->ecd/dot_general | solution.py:215
  736.5 34.7 %reduce-scatter.8.cloned.1.call-done = f32[128,256]{1,0:T(8,128)} async-done(((f32[1024,256]{1,0:T(8,128)}), f32[128,256]{1,0:T(8,128)}) %reduce-scatter.8.cloned.1.call-update) | async-done | bytes 131088 | tf_op jit(solution)/shard_map/reduce_scatter | solution.py:282
  771.3 28.5 %bitcast_multiply_fusion.1 = f32[10240,1024]{1,0:T(8,128)} fusion(f32[16,640,1024]{2,1,0:T(8,128)} %get-tuple-element.144, f32[10240]{0:T(1024)S(1)} %copy-done.54), kind=kLoop, calls=%fused_computation.14 | loop fusion | flops 10485760 | bytes 83927040 | tf_op jit(solution)/shard_map/mul | solution.py:227
  799.8 90.7 %scatter_custom_fusion.3 = f32[1024,1024]{1,0:T(8,128)} fusion(s32[10240]{0:T(1024)} %get-tuple-element.132, f32[10240,1024]{1,0:T(8,128)} %bitcast_multiply_fusion.1, f32[]{:T(128)} %constant.73.clone.1), kind=kCustom, calls=%fused_computation.86 | custom fusion | flops 10485760 | bytes 4194816 | tf_op jit(solution)/shard_map/scatter-add | solution.py:227
  894.8 28.8 %reduce-scatter.16.cloned.1.call-done = f32[16,128,128]{2,1,0:T(8,128)} async-done(((f32[16,1024,128]{2,1,0:T(8,128)}), f32[16,128,128]{2,1,0:T(8,128)}) %reduce-scatter.16.cloned.1.call-update) | async-done | bytes 1048592 | tf_op jit(solution)/shard_map/reduce_scatter | solution.py:287
  923.7 152.8 %reduce-scatter.18.cloned.1.call-done = f32[16,128,128]{2,1,0:T(8,128)} async-done(((f32[16,1024,128]{2,1,0:T(8,128)}), f32[16,128,128]{2,1,0:T(8,128)}) %reduce-scatter.18.cloned.1.call-update) | async-done | bytes 1048592 | tf_op jit(solution)/shard_map/reduce_scatter | solution.py:288
  1076.6 152.0 %reduce-scatter.20.cloned.1.call-done = f32[16,128,128]{2,1,0:T(8,128)} async-done(((f32[16,128,1024]{2,1,0:T(8,128)}), f32[16,128,128]{2,1,0:T(8,128)}) %reduce-scatter.20.cloned.1.call-update) | async-done | bytes 1048592 | tf_op jit(solution)/shard_map/reduce_scatter | solution.py:289
  1230.4 45.5 %gather_fusion.2 = f32[8192]{0:T(1024)S(1)} fusion(f32[10241]{0:T(1024)S(1)} %pad_maximum_fusion.7, s32[8192]{0:T(1024)S(1)} %broadcast_clamp_fusion.1), kind=kCustom, calls=%fused_computation.2 | custom fusion | bytes 98304 | tf_op jit(solution)/shard_map/gather | solution.py:235
  1276.5 12.0 psum.39
  1288.4 5.4 reduce-scatter.12.cloned.1.call-done
  1293.9 32.2 %all_gather.30 = f32[1024,128]{1,0:T(8,128)S(1)} all-gather(f32[128,128]{1,0:T(8,128)} %reduce-scatter.12.cloned.1.call-done), channel_id=1, replica_groups=mesh['dp'=8,'tensor'=4] {'dp'}, dimensions={0}, use_global_device_ids=true | all-gather | bytes 589824 | tf_op jit(solution)/shard_map/all_gather | solution.py:295
  1326.0 32.7 %reduce-scatter.10.cloned.1.call-done = f32[128,128]{1,0:T(8,128)} async-done(((f32[1024,128]{1,0:T(8,128)}), f32[128,128]{1,0:T(8,128)}) %reduce-scatter.10.cloned.1.call-update) | async-done | bytes 65552 | tf_op jit(solution)/shard_map/reduce_scatter | solution.py:283
  1358.8 32.1 %all_gather.29 = f32[1024,128]{1,0:T(8,128)S(1)} all-gather(f32[128,128]{1,0:T(8,128)} %reduce-scatter.10.cloned.1.call-done), channel_id=1, replica_groups=mesh['dp'=8,'tensor'=4] {'dp'}, dimensions={0}, use_global_device_ids=true | all-gather | bytes 589824 | tf_op jit(solution)/shard_map/all_gather | solution.py:294
  1390.9 10.4 all-gather.10.cloned.1.call-done
  1401.3 41.8 %all-gather.8.cloned.1.call-done = f32[1024,256]{1,0:T(8,128)} async-done(((f32[128,256]{1,0:T(8,128)}), f32[1024,256]{1,0:T(8,128)}) %all-gather.8.cloned.1.call-update) | async-done | bytes 1048592 | tf_op jit(solution)/shard_map/all_gather | solution.py:293
  1443.1 155.2 %all-reduce.18.cloned.1.call-done = (f32[1024,1024]{1,0:T(8,128)}, f32[1024,1024]{1,0:T(8,128)}) async-done(((f32[1024,1024]{1,0:T(8,128)}, f32[1024,1024]{1,0:T(8,128)}), (f32[1024,1024]{1,0:T(8,128)}, f32[1024,1024]{1,0:T(8,128)})) %all-reduce.18.cloned.1.call-update) | async-done | bytes 8388624 | tf_op jit(solution)/shard_map/psum | solution.py:229
  1601.9 22.2 %all-reduce.8 = (f32[1024]{0:T(1024)S(1)}, f32[1024]{0:T(1024)S(1)}) all-reduce(f32[1024]{0:T(1024)S(1)} %get-tuple-element.101, f32[1024]{0:T(1024)S(1)} %copy-done.83), channel_id=2, replica_groups=mesh['dp'=8,'tensor'=4] {'dp'}, use_global_device_ids=true, to_apply=%region_26.27.clone | all-reduce | flops 2048 | bytes 16384
  1624.1 16.4 all-gather
  1640.6 18.2 all-gather.1
  1658.9 5.4 multiply_convert_fusion.3
  1667.9 58.3 %all-gather.12.cloned.1.call-done = f32[16,1024,128]{2,1,0:T(8,128)} async-done(((f32[16,128,128]{2,1,0:T(8,128)}), f32[16,1024,128]{2,1,0:T(8,128)}) %all-gather.12.cloned.1.call-update) | async-done | bytes 8388624 | tf_op jit(solution)/shard_map/all_gather | solution.py:298
  1726.2 125.4 %all-gather.14.cloned.1.call-done = f32[16,1024,128]{2,1,0:T(8,128)} async-done(((f32[16,128,128]{2,1,0:T(8,128)}), f32[16,1024,128]{2,1,0:T(8,128)}) %all-gather.14.cloned.1.call-update) | async-done | bytes 8388624 | tf_op jit(solution)/shard_map/all_gather | solution.py:299
  1851.6 125.7 %all-gather.16.cloned.1.call-done = f32[16,128,1024]{2,1,0:T(8,128)} async-done(((f32[16,128,128]{2,1,0:T(8,128)}), f32[16,128,1024]{2,1,0:T(8,128)}) %all-gather.16.cloned.1.call-update) | async-done | bytes 8388624 | tf_op jit(solution)/shard_map/all_gather | solution.py:300
  1983.3 7.7 copy.174
  1991.0 4.3 copy.175
  (332 shorter events, 92.2 us)
Async XLA Ops:
  7.2 21.1 %copy-start = (bf16[256,1024]{1,0:T(8,128)(2,1)S(1)}, bf16[256,1024]{1,0:T(8,128)(2,1)}, u32[]{:S(2)}) copy-start(bf16[256,1024]{1,0:T(8,128)(2,1)} %param.23) | copy-start | bytes 1572868
  7.2 237.1 %all-reduce.14.cloned.1.call-start = ((), (), s32[]{:S(2)}) async-start(), calls=%async_computation.7 | async-start | bytes 8388608 | tf_op jit(solution)/shard_map/psum | solution.py:201
  31.0 590.3 %all-reduce.16.cloned.1.call-start = ((), (), s32[]{:S(2)}) async-start(), calls=%async_computation.8 | async-start | bytes 8388608 | tf_op jit(solution)/shard_map/psum | solution.py:248
  38.3 66.1 %copy-start.56 = (s32[1024,8]{0,1:T(8,128)S(1)}, s32[1024,8]{0,1:T(8,128)}, u32[]{:S(2)}) copy-start(s32[1024,8]{0,1:T(8,128)} %param.16) | copy-start | bytes 98308
  38.3 66.1 %copy-start.84 = (pred[1024]{0:T(1024)(128)(4,1)S(1)}, pred[1024]{0:T(1024)(128)(4,1)}, u32[]{:S(2)}) copy-start(pred[1024]{0:T(1024)(128)(4,1)} %get-tuple-element.148) | copy-start | bytes 3076
  38.3 129.2 %copy-start.78 = (f32[1024,8]{0,1:T(8,128)S(1)}, f32[1024,8]{0,1:T(8,128)}, u32[]{:S(2)}) copy-start(f32[1024,8]{0,1:T(8,128)} %param.17) | copy-start | bytes 98308
  103.9 96.4 %copy-start.2 = (bf16[1024,1024]{1,0:T(8,128)(2,1)S(1)}, bf16[1024,1024]{1,0:T(8,128)(2,1)}, u32[]{:S(2)}) copy-start(bf16[1024,1024]{1,0:T(8,128)(2,1)} %param.18) | copy-start | bytes 6291460
  105.0 139.3 %copy-start.59 = (pred[1024,8]{0,1:T(8,128)(4,1)}, pred[1024,8]{0,1:T(8,128)(4,1)S(1)}, u32[]{:S(2)}) copy-start(pred[1024,8]{0,1:T(8,128)(4,1)S(1)} %get-tuple-element.109) | copy-start | bytes 24580
  322.6 13.1 copy-start.17
  335.7 12.2 copy-start.48
  365.9 19.4 copy-start.22
  385.3 28.9 %copy-start.57 = (f32[10240]{0:T(1024)S(1)}, f32[10240]{0:T(1024)}, u32[]{:S(2)}) copy-start(f32[10240]{0:T(1024)} %get-tuple-element.129) | copy-start | bytes 122884
  442.3 90.6 %copy-start.75 = (f32[2,2,512]{2,1,0:T(2,128)S(1)}, f32[2,2,512]{2,1,0:T(2,128)}, u32[]{:S(2)}) copy-start(f32[2,2,512]{2,1,0:T(2,128)} %copy-done.74) | copy-start | bytes 24580
  442.4 90.7 %copy-start.77 = (f32[2,2,512]{2,1,0:T(2,128)S(1)}, f32[2,2,512]{2,1,0:T(2,128)}, u32[]{:S(2)}) copy-start(f32[2,2,512]{2,1,0:T(2,128)} %copy-done.76) | copy-start | bytes 24580
  442.4 90.7 %copy-start.80 = (f32[2,2,512]{2,1,0:T(2,128)S(1)}, f32[2,2,512]{2,1,0:T(2,128)}, u32[]{:S(2)}) copy-start(f32[2,2,512]{2,1,0:T(2,128)} %copy-done.79) | copy-start | bytes 24580
  442.4 90.7 %copy-start.82 = (f32[2,2,512]{2,1,0:T(2,128)S(1)}, f32[2,2,512]{2,1,0:T(2,128)}, u32[]{:S(2)}) copy-start(f32[2,2,512]{2,1,0:T(2,128)} %copy-done.81) | copy-start | bytes 24580
  442.4 178.9 %copy-start.64 = (f32[1024]{0:T(1024)S(1)}, f32[1024]{0:T(1024)}, u32[]{:S(2)}) copy-start(f32[1024]{0:T(1024)} %copy-done.63) | copy-start | bytes 12292
  442.4 178.9 %copy-start.67 = (f32[1024]{0:T(1024)S(1)}, f32[1024]{0:T(1024)}, u32[]{:S(2)}) copy-start(f32[1024]{0:T(1024)} %param.24) | copy-start | bytes 12292
  532.9 178.4 %reduce-scatter.14.cloned.1.call-start = ((), (), s32[]{:S(2)}) async-start(), calls=%async_computation.13 | async-start | bytes 1179648 | tf_op jit(solution)/shard_map/reduce_scatter | solution.py:285
  533.0 93.5 %copy-start.68 = (f32[1024]{0:T(1024)}, f32[1024]{0:T(1024)S(1)}, u32[]{:S(2)}) copy-start(f32[1024]{0:T(1024)S(1)} %fusion.98) | copy-start | bytes 12292
  533.1 93.4 %copy-start.73 = (f32[1024]{0:T(1024)S(1)}, f32[1024]{0:T(1024)}, u32[]{:S(2)}) copy-start(f32[1024]{0:T(1024)} %copy-done.72) | copy-start | bytes 12292
  533.1 93.4 %copy-start.3 = (bf16[1024,1024]{1,0:T(8,128)(2,1)S(1)}, bf16[1024,1024]{1,0:T(8,128)(2,1)}, u32[]{:S(2)}) copy-start(bf16[1024,1024]{1,0:T(8,128)(2,1)} %param.18) | copy-start | bytes 6291460
  640.2 131.0 %reduce-scatter.8.cloned.1.call-start = ((), (), s32[]{:S(2)}) async-start(), calls=%async_computation.9 | async-start | bytes 1179648 | tf_op jit(solution)/shard_map/reduce_scatter | solution.py:282
  653.8 269.9 %reduce-scatter.16.cloned.1.call-start = ((), (), s32[]{:S(2)}) async-start(), calls=%async_computation.15 | async-start | bytes 9437184 | tf_op jit(solution)/shard_map/reduce_scatter | solution.py:287
  666.6 409.9 %reduce-scatter.18.cloned.1.call-start = ((), (), s32[]{:S(2)}) async-start(), calls=%async_computation.17 | async-start | bytes 9437184 | tf_op jit(solution)/shard_map/reduce_scatter | solution.py:288
  680.0 548.6 %reduce-scatter.20.cloned.1.call-start = ((), (), s32[]{:S(2)}) async-start(), calls=%async_computation.19 | async-start | bytes 9437184 | tf_op jit(solution)/shard_map/reduce_scatter | solution.py:289
  692.3 601.5 %reduce-scatter.12.cloned.1.call-start = ((), (), s32[]{:S(2)}) async-start(), calls=%async_computation.12 | async-start | bytes 589824 | tf_op jit(solution)/shard_map/reduce_scatter | solution.py:284
  709.4 649.4 %reduce-scatter.10.cloned.1.call-start = ((), (), s32[]{:S(2)}) async-start(), calls=%async_computation.11 | async-start | bytes 589824 | tf_op jit(solution)/shard_map/reduce_scatter | solution.py:283
  711.2 690.1 %all-gather.10.cloned.1.call-start = ((), (), s32[]{:S(2)}) async-start(), calls=%async_computation.14 | async-start | bytes 1179648 | tf_op jit(solution)/shard_map/all_gather | solution.py:296
  711.8 59.4 %copy-start.54 = (f32[10240]{0:T(1024)S(1)}, f32[10240]{0:T(1024)}, u32[]{:S(2)}) copy-start(f32[10240]{0:T(1024)} %copy-done.53) | copy-start | bytes 122884
  711.8 731.2 %all-gather.8.cloned.1.call-start = ((), (), s32[]{:S(2)}) async-start(), calls=%async_computation.10 | async-start | bytes 1179648 | tf_op jit(solution)/shard_map/all_gather | solution.py:293
  771.2 827.1 %all-reduce.18.cloned.1.call-start = ((), (), s32[]{:S(2)}) async-start(), calls=%async_computation.21 | async-start | bytes 16777216 | tf_op jit(solution)/shard_map/psum | solution.py:229
  799.8 90.7 %copy-start.47 = (bf16[1024,128]{1,0:T(8,128)(2,1)S(1)}, bf16[1024,128]{1,0:T(8,128)(2,1)}, u32[]{:S(2)}) copy-start(bf16[1024,128]{1,0:T(8,128)(2,1)} %param.21) | copy-start | bytes 786436
  799.8 91.4 %copy-start.24 = (bf16[1,1024,4,64]{1,3,2,0:T(8,128)(2,1)S(1)}, bf16[1,1024,4,64]{1,3,2,0:T(8,128)(2,1)}, u32[]{:S(2)}) copy-start(bf16[1,1024,4,64]{1,3,2,0:T(8,128)(2,1)} %copy-done.23) | copy-start | bytes 1572868
  799.8 91.4 %copy-start.30 = (bf16[1024,256]{1,0:T(8,128)(2,1)S(1)}, bf16[1024,256]{1,0:T(8,128)(2,1)}, u32[]{:S(2)}) copy-start(bf16[1024,256]{1,0:T(8,128)(2,1)} %param.20) | copy-start | bytes 1572868
  894.7 333.9 %copy-start.58 = (s32[1024,8]{0,1:T(8,128)S(1)}, s32[1024,8]{0,1:T(8,128)}, u32[]{:S(2)}) copy-start(s32[1024,8]{0,1:T(8,128)} %get-tuple-element.107) | copy-start | bytes 98308
  894.8 334.3 %copy-start.85 = (u32[32]{0:T(128)S(1)}, u32[32]{0:T(128)}, u32[]{:S(2)}) copy-start(u32[32]{0:T(128)} %constant.171) | copy-start | bytes 388
  894.8 831.4 %all-gather.12.cloned.1.call-start = ((), (), s32[]{:S(2)}) async-start(), calls=%async_computation.16 | async-start | bytes 9437184 | tf_op jit(solution)/shard_map/all_gather | solution.py:298
  923.7 927.9 %all-gather.14.cloned.1.call-start = ((), (), s32[]{:S(2)}) async-start(), calls=%async_computation.18 | async-start | bytes 9437184 | tf_op jit(solution)/shard_map/all_gather | solution.py:299
  1076.6 900.7 %all-gather.16.cloned.1.call-start = ((), (), s32[]{:S(2)}) async-start(), calls=%async_computation.20 | async-start | bytes 9437184 | tf_op jit(solution)/shard_map/all_gather | solution.py:300
  1230.4 46.1 %copy-start.60 = (pred[1024,8]{0,1:T(8,128)(4,1)S(1)}, pred[1024,8]{0,1:T(8,128)(4,1)}, u32[]{:S(2)}) copy-start(pred[1024,8]{0,1:T(8,128)(4,1)} %copy-done.59) | copy-start | bytes 24580
  1230.4 367.9 %copy-start.13 = (bf16[1024,1024]{1,0:T(8,128)(2,1)S(1)}, bf16[1024,1024]{1,0:T(8,128)(2,1)}, u32[]{:S(2)}) copy-start(bf16[1024,1024]{1,0:T(8,128)(2,1)} %param.14) | copy-start | bytes 6291460
  1230.4 367.9 %copy-start.62 = (f32[1024]{0:T(1024)S(1)}, f32[1024]{0:T(1024)}, u32[]{:S(2)}) copy-start(f32[1024]{0:T(1024)} %copy-done.61) | copy-start | bytes 12292
  1230.4 367.9 %copy-start.65 = (f32[1024]{0:T(1024)S(1)}, f32[1024]{0:T(1024)}, u32[]{:S(2)}) copy-start(f32[1024]{0:T(1024)} %param.19) | copy-start | bytes 12292
  1276.3 325.6 %copy-start.83 = (f32[1024]{0:T(1024)S(1)}, f32[1024]{0:T(1024)}, u32[]{:S(2)}) copy-start(f32[1024]{0:T(1024)} %get-tuple-element.99) | copy-start | bytes 12292
  1276.3 382.5 %copy-start.71 = (f32[1024]{0:T(1024)S(1)}, f32[1024]{0:T(1024)}, u32[]{:S(2)}) copy-start(f32[1024]{0:T(1024)} %copy-done.70) | copy-start | bytes 12292
  1276.3 382.6 %copy-start.69 = (f32[1024]{0:T(1024)S(1)}, f32[1024]{0:T(1024)}, u32[]{:S(2)}) copy-start(f32[1024]{0:T(1024)} %copy-done.68) | copy-start | bytes 12292
  1667.9 313.9 %copy-start.42 = (f32[256,1024]{1,0:T(8,128)S(1)}, f32[256,1024]{1,0:T(8,128)}, u32[]{:S(2)}) copy-start(f32[256,1024]{1,0:T(8,128)} %all-gather.10.cloned.1.call-done) | copy-start | bytes 3145732
  (59 other events, 198.0 us)
Sparse Core Ops, SparseCore 0:
  31.1 88.1 all-reduce.13
  533.0 88.1 all-reduce.15
  640.3 64.1 reduce-scatter.13
  708.7 62.4 reduce-scatter.7
  775.2 148.3 reduce-scatter.15
  928.1 148.3 reduce-scatter.17
  1080.2 148.3 reduce-scatter.19
  1232.9 60.9 reduce-scatter.11
  1297.8 60.9 reduce-scatter.9
  1360.9 40.3 all-gather.9
  1403.6 39.3 all-gather.7
  1446.2 151.9 all-reduce.17
  1600.7 125.4 all-gather.11
  1728.4 123.0 all-gather.13
  1853.7 123.5 all-gather.15
where the time goes:
time: 2020 us; the launch traced here: 2010 us
  waiting for transfers between devices  1010 us (50%)
  local copies, waits for them, and re-layouts  360 us (18%)
  other arithmetic  282 us (14%)
  matrix products  201 us (10%)
  blocking collectives  133 us (7%)
    psum x1, waiting for transfers between devices, per_device(): moe_sum = lax.psum(moe_part, 'tensor')  155 us
    reduce_scatter x1, waiting for transfers between devices, per_device(): lax.psum_scatter(grad_up, 'dp', scatter_dimension=1, tiled=True)  153 us
    reduce_scatter x1, waiting for transfers between devices, per_device(): lax.psum_scatter(grad_down, 'dp', scatter_dimension=2, tiled=True)  152 us
    all_gather x1, waiting for transfers between devices, per_device(): lax.all_gather(summed[8], 'dp', axis=2, tiled=True)  126 us
    all_gather x1, waiting for transfers between devices, per_device(): lax.all_gather(summed[7], 'dp', axis=1, tiled=True)  125 us
    scatter-add x1, other arithmetic, per_device(): moe_part = jnp.zeros((tok_rows, width), jnp.float32).at[slot_token].add(p...  90.7 us
    scatter-add x1, other arithmetic, per_device(): jnp.zeros((tok_rows, width), jnp.float32).at[slot_token]  90.5 us
    psum x1, waiting for transfers between devices, per_device(): d_h_moe, d_gates = lax.psum((d_h_part, d_gate_part), 'tensor')  88.2 us
  transfers between devices with their start and end apart: 15, of which 13 were waited for; matrix products, arithmetic and copies ran while one was open for 24% of the time, Pallas kernels for 0%

commit v1 on v0

--- a/solution.py
+++ b/solution.py
@@ -8,7 +8,6 @@
 HEAD_DIM = 64
 TOP_K = 8
 EXPERTS = 16
-CAPACITY = 640
 
 
 EPSILON = 1e-05
@@ -39,29 +38,21 @@
     return values * cosine[:, None, :] + turned * sine[:, None, :]
 
 
-def route_pairs(valid, chosen):
+def route_weights(valid, chosen, gate_values):
     tok_rows = chosen.shape[0]
     live_int = valid.astype(jnp.int32)
-    expert_ids = jnp.arange(EXPERTS, dtype=jnp.int32)
-    hits = (
-        jnp.sum((chosen[:, :, None] == expert_ids[None, None, :]).astype(jnp.int32), axis=1)
-        * live_int[:, None]
-    )
-    before = jnp.cumsum(hits, axis=0) - hits
-    places = jnp.take_along_axis(before, chosen, axis=1)
+    onehot = chosen[:, :, None] == jnp.arange(EXPERTS, dtype=jnp.int32)[None, None, :]
+    onehot_f = onehot.astype(jnp.float32)
+    hits = jnp.sum(onehot_f, axis=1) * valid.astype(jnp.float32)[:, None]
+    earlier = (
+        jnp.arange(tok_rows, dtype=jnp.int32)[None, :] < jnp.arange(tok_rows, dtype=jnp.int32)[:, None]
+    ).astype(jnp.bfloat16)
+    places = dot_f(earlier, hits.astype(jnp.bfloat16))
     pairs = jnp.sum(live_int) * TOP_K
-    limit = (5 * pairs + 4 * EXPERTS - 1) // (4 * EXPERTS)
-    kept = (places < limit) & (live_int[:, None] > 0)
-    dump_at = EXPERTS * CAPACITY
-    target = jnp.where(kept, chosen * CAPACITY + places, dump_at)
-    row_ids = jnp.broadcast_to(jnp.arange(tok_rows, dtype=jnp.int32)[:, None], chosen.shape)
-    slot_token = (
-        jnp.zeros((dump_at + 1,), jnp.int32)
-        .at[target.reshape(-1)]
-        .set(row_ids.reshape(-1))[:dump_at]
-    )
-    slot_live = jnp.zeros((dump_at + 1,), jnp.int32).at[target.reshape(-1)].set(1)[:dump_at]
-    return (slot_token, slot_live, target, kept)
+    limit = ((5 * pairs + 4 * EXPERTS - 1) // (4 * EXPERTS)).astype(jnp.float32)
+    kept = jnp.where((places < limit) & (hits > 0), 1.0, 0.0)
+    weights = jnp.sum(onehot_f * gate_values[:, :, None], axis=1) * kept
+    return (weights, kept, onehot_f)
 
 
 def block_scores(q_block, start, k_seq, length, scaling):
@@ -201,50 +192,30 @@
     attn_sum = lax.psum(dot_f(attn_cat, w_out), "tensor")
     resid = x_in + attn_sum
     h_moe = rms_norm(resid, norm_moe).astype(jnp.bfloat16)
-    slot_token, slot_live, target, kept = route_pairs(valid, chosen)
-    dump_at = EXPERTS * CAPACITY
-    live_f = slot_live.astype(jnp.float32)[:, None]
-    dispatched = (h_moe[slot_token] * slot_live.astype(jnp.bfloat16)[:, None]).reshape(
-        EXPERTS, CAPACITY, -1
-    )
-    gate_act = jnp.einsum("ecd,edf->ecf", dispatched, w_gate, preferred_element_type=jnp.float32)
-    up_act = jnp.einsum("ecd,edf->ecf", dispatched, w_up, preferred_element_type=jnp.float32)
+    weights, kept, onehot_f = route_weights(valid, chosen, gate_values)
+    d_out = cotangent.astype(jnp.float32) * valid_f
+    gate_act = jnp.einsum("td,edf->tef", h_moe, w_gate, preferred_element_type=jnp.float32)
+    up_act = jnp.einsum("td,edf->tef", h_moe, w_up, preferred_element_type=jnp.float32)
+    d_raw = jnp.einsum("td,efd->tef", cotangent, w_down, preferred_element_type=jnp.float32)
     sigma = jax.nn.sigmoid(gate_act)
     silu_g = gate_act * sigma
-    hidden_b = (silu_g * up_act).astype(jnp.bfloat16)
-    produced = jnp.einsum(
-        "ecf,efd->ecd", hidden_b, w_down, preferred_element_type=jnp.float32
-    ).reshape(dump_at, -1)
-    weights = jnp.where(kept, gate_values, 0.0)
-    slot_weight = (
-        jnp.zeros((dump_at + 1,), jnp.float32)
-        .at[target.reshape(-1)]
-        .set(weights.reshape(-1))[:dump_at]
-    )
-    moe_part = (
-        jnp.zeros((tok_rows, width), jnp.float32)
-        .at[slot_token]
-        .add(produced * slot_weight[:, None])
-    )
+    hidden = silu_g * up_act
+    hidden_w = (hidden * weights[:, :, None]).astype(jnp.bfloat16)
+    gate_dot = jnp.sum(hidden * d_raw, axis=-1) * kept
+    d_gate_part = jnp.sum(onehot_f * gate_dot[:, None, :], axis=-1)
+    d_hidden = d_raw * weights[:, :, None]
+    d_gate_b = (d_hidden * up_act * sigma * (1.0 + gate_act * (1.0 - sigma))).astype(jnp.bfloat16)
+    d_up_b = (d_hidden * silu_g).astype(jnp.bfloat16)
+    moe_part = jnp.einsum("tef,efd->td", hidden_w, w_down, preferred_element_type=jnp.float32)
     moe_sum = lax.psum(moe_part, "tensor")
     result = ((resid + moe_sum) * valid_f).astype(jnp.bfloat16)
-    d_out = cotangent.astype(jnp.float32) * valid_f
-    slot_cot = cotangent[slot_token].astype(jnp.float32)
-    slot_dot = jnp.sum(slot_cot * produced, axis=-1)
-    slot_dot = jnp.concatenate([slot_dot, jnp.zeros((1,), jnp.float32)])
-    d_gate_part = jnp.where(kept, slot_dot[target], 0.0)
-    d_prod = (slot_weight[:, None] * slot_cot).astype(jnp.bfloat16).reshape(EXPERTS, CAPACITY, -1)
-    grad_down = jnp.einsum("ecf,ecd->efd", hidden_b, d_prod, preferred_element_type=jnp.float32)
-    d_hidden = jnp.einsum("ecd,efd->ecf", d_prod, w_down, preferred_element_type=jnp.float32)
-    d_gate_b = (d_hidden * up_act * sigma * (1.0 + gate_act * (1.0 - sigma))).astype(jnp.bfloat16)
-    d_up_b = (d_hidden * silu_g).astype(jnp.bfloat16)
-    grad_gate = jnp.einsum("ecd,ecf->edf", dispatched, d_gate_b, preferred_element_type=jnp.float32)
-    grad_up = jnp.einsum("ecd,ecf->edf", dispatched, d_up_b, preferred_element_type=jnp.float32)
-    d_disp = jnp.einsum("ecf,edf->ecd", d_gate_b, w_gate, preferred_element_type=jnp.float32)
-    d_disp = (
-        d_disp + jnp.einsum("ecf,edf->ecd", d_up_b, w_up, preferred_element_type=jnp.float32)
-    ).reshape(dump_at, -1)
-    d_h_part = jnp.zeros((tok_rows, width), jnp.float32).at[slot_token].add(d_disp * live_f)
+    grad_down = jnp.einsum("tef,td->efd", hidden_w, cotangent, preferred_element_type=jnp.float32)
+    grad_gate = jnp.einsum("td,tef->edf", h_moe, d_gate_b, preferred_element_type=jnp.float32)
+    grad_up = jnp.einsum("td,tef->edf", h_moe, d_up_b, preferred_element_type=jnp.float32)
+    d_h_part = jnp.einsum("tef,edf->td", d_gate_b, w_gate, preferred_element_type=jnp.float32)
+    d_h_part = d_h_part + jnp.einsum(
+        "tef,edf->td", d_up_b, w_up, preferred_element_type=jnp.float32
+    )
     d_h_moe, d_gates = lax.psum((d_h_part, d_gate_part), "tensor")
     unused_m, pull_moe = jax.vjp(rms_norm, resid, norm_moe)
     d_resid_n, grad_norm_moe = pull_moe(d_h_moe)

time: 2020 us -> 1650 us (0.82)
  local copies, waits for them, and re-layouts: 360 us -> 62.4 us
  waiting for transfers between devices: 1010 us -> 1250 us
  other arithmetic: 282 us -> 53.2 us
  matrix products: 201 us -> 126 us
    gather x11 -> x0, local copies, waits for them, and re-layouts: 229 us -> none  [the longest x2 72.3 us: per_device(): h_moe[slot_token] * slot_live.astype(jnp.bfloat16)[:, None]]
    scatter-add x2 -> x0, other arithmetic: 181 us -> none  [the longest x1 90.7 us: per_device(): moe_part = jnp.zeros((tok_rows, width), jnp.float32).at[slot_token].add(p...]
    reduce_scatter x1, waiting for transfers between devices: 28.8 us -> 137 us  [per_device(): lax.psum_scatter(grad_gate, 'dp', scatter_dimension=1, tiled=True)]
    scatter x3 -> x0, local copies, waits for them, and re-layouts: 91.4 us -> none  [the longest x1 30.5 us: route_pairs(): jnp.zeros((dump_at + 1,), jnp.int32).at[target.reshape(-1)].set(1)[:dump_at]]
    dot_general x9 -> x7, matrix products: 155 us -> 68.3 us  [the longest x1 13.1 us: per_device(): jnp.einsum('td,efd->tef', cotangent, w_down, preferred_element_type=jnp.f...]
    psum x1, waiting for transfers between devices: 0.01 us -> 72.2 us  [per_device(): attn_sum = lax.psum(dot_f(attn_cat, w_out), 'tensor')]
    mul x2 -> x1, other arithmetic: 56.7 us -> 0.01 us  [route_weights(): weights = jnp.sum(onehot_f * gate_values[:, :, None], axis=1) * kept]
    reduce_scatter x1, waiting for transfers between devices: 5.43 us -> 52 us  [per_device(): lax.psum_scatter(grad_value, 'dp', scatter_dimension=0, tiled=True)]
  transfers between devices with their start and end apart: 15 -> 15, of which waited for: 13 -> 14; matrix products, arithmetic and copies ran while one was open for 24% -> 8% of each run, Pallas kernels for 0% -> 0%
where the time goes in v1:
time: 1650 us; the launch traced here: 1640 us
  waiting for transfers between devices  1250 us (76%)
  blocking collectives  133 us (8%)
  matrix products  126 us (8%)
  local copies, waits for them, and re-layouts  62.4 us (4%)
  other arithmetic  53.2 us (3%)
  between operations  17.2 us (1%)
    psum x1, waiting for transfers between devices, per_device(): moe_sum = lax.psum(moe_part, 'tensor')  155 us
    reduce_scatter x1, waiting for transfers between devices, per_device(): lax.psum_scatter(grad_up, 'dp', scatter_dimension=1, tiled=True)  153 us
    reduce_scatter x1, waiting for transfers between devices, per_device(): lax.psum_scatter(grad_down, 'dp', scatter_dimension=2, tiled=True)  152 us
    reduce_scatter x1, waiting for transfers between devices, per_device(): lax.psum_scatter(grad_gate, 'dp', scatter_dimension=1, tiled=True)  137 us
    all_gather x1, waiting for transfers between devices, per_device(): lax.all_gather(summed[7], 'dp', axis=1, tiled=True)  116 us
    all_gather x1, waiting for transfers between devices, per_device(): lax.all_gather(summed[8], 'dp', axis=2, tiled=True)  116 us
    psum x1, waiting for transfers between devices, per_device(): d_h_moe, d_gates = lax.psum((d_h_part, d_gate_part), 'tensor')  83.7 us
    psum x1, waiting for transfers between devices, per_device(): attn_sum = lax.psum(dot_f(attn_cat, w_out), 'tensor')  72.2 us
  transfers between devices with their start and end apart: 15, of which 14 were waited for; matrix products, arithmetic and copies ran while one was open for 8% of the time, Pallas kernels for 0%

profile of v1, /device:TPU:0, one launch (start us, length us, event | category | flops | bytes accessed | tf_op | source)
XLA Modules:
  0.0 1639.7 jit_solution(14200340769331598400)
XLA Ops:
  31.8 6.4 copy.64
  38.2 6.9 copy.65
  46.6 72.2 %all-reduce.14.cloned.1.call-done = f32[1024,1024]{1,0:T(8,128)} async-done(((f32[1024,1024]{1,0:T(8,128)}), f32[1024,1024]{1,0:T(8,128)}) %all-reduce.14.cloned.1.call-update) | async-done | bytes 4194320 | tf_op jit(solution)/shard_map/psum | solution.py:192
  118.8 3.5 multiply_reduce_fusion.3
  122.8 3.9 copy-done.20
  126.7 4.6 fusion.93
  131.3 4.7 fusion.94
  136.1 13.1 multiply_reduce_fusion
  150.5 12.3 multiply_convert_fusion.1
  162.8 6.6 fusion.95
  169.5 6.1 bitcast_add_fusion
  177.7 83.7 %all-reduce.16.cloned.1.call-done = f32[1024,1024]{1,0:T(8,128)} async-done(((f32[1024,1024]{1,0:T(8,128)}), f32[1024,1024]{1,0:T(8,128)}) %all-reduce.16.cloned.1.call-update) | async-done | bytes 4194320 | tf_op jit(solution)/shard_map/psum | solution.py:219
  261.4 5.2 multiply_reduce_fusion.1
  267.3 3.0 fusion.10
  275.3 3.3 fusion.17
  281.9 5.4 fusion
  295.9 10.8 convolution_bitcast_fusion.1
  306.8 10.8 convolution_bitcast_fusion
  317.8 10.7 fusion.29
  329.5 3.0 fusion.54
  332.6 3.0 fusion.50
  335.6 4.8 fusion.45
  342.0 3.7 fusion.41
  348.2 64.7 %reduce-scatter.8.cloned.1.call-done = f32[128,256]{1,0:T(8,128)} async-done(((f32[1024,256]{1,0:T(8,128)}), f32[128,256]{1,0:T(8,128)}) %reduce-scatter.8.cloned.1.call-update) | async-done | bytes 131088 | tf_op jit(solution)/shard_map/reduce_scatter | solution.py:253
  413.2 10.0 convolution_bitcast_fusion.2
  425.3 2.8 add_add_fusion.2
  428.2 137.1 %reduce-scatter.16.cloned.1.call-done = f32[16,128,128]{1,2,0:T(8,128)} async-done(((f32[16,1024,128]{1,2,0:T(8,128)}), f32[16,128,128]{1,2,0:T(8,128)}) %reduce-scatter.16.cloned.1.call-update) | async-done | bytes 1048592 | tf_op jit(solution)/shard_map/reduce_scatter | solution.py:258
  565.4 152.8 %reduce-scatter.18.cloned.1.call-done = f32[16,128,128]{1,2,0:T(8,128)} async-done(((f32[16,1024,128]{1,2,0:T(8,128)}), f32[16,128,128]{1,2,0:T(8,128)}) %reduce-scatter.18.cloned.1.call-update) | async-done | bytes 1048592 | tf_op jit(solution)/shard_map/reduce_scatter | solution.py:259
  718.3 152.0 %reduce-scatter.20.cloned.1.call-done = f32[16,128,128]{2,1,0:T(8,128)} async-done(((f32[16,128,1024]{2,1,0:T(8,128)}), f32[16,128,128]{2,1,0:T(8,128)}) %reduce-scatter.20.cloned.1.call-update) | async-done | bytes 1048592 | tf_op jit(solution)/shard_map/reduce_scatter | solution.py:260
  871.6 12.0 psum.39
  883.5 52.0 %reduce-scatter.12.cloned.1.call-done = f32[128,128]{1,0:T(8,128)} async-done(((f32[1024,128]{1,0:T(8,128)}), f32[128,128]{1,0:T(8,128)}) %reduce-scatter.12.cloned.1.call-update) | async-done | bytes 65552 | tf_op jit(solution)/shard_map/reduce_scatter | solution.py:255
  935.5 32.3 %all_gather.30 = f32[1024,128]{1,0:T(8,128)S(1)} all-gather(f32[128,128]{1,0:T(8,128)} %reduce-scatter.12.cloned.1.call-done), channel_id=1, replica_groups=mesh['dp'=8,'tensor'=4] {'dp'}, dimensions={0}, use_global_device_ids=true | all-gather | bytes 589824 | tf_op jit(solution)/shard_map/all_gather | solution.py:266
  967.8 32.6 %reduce-scatter.10.cloned.1.call-done = f32[128,128]{1,0:T(8,128)} async-done(((f32[1024,128]{1,0:T(8,128)}), f32[128,128]{1,0:T(8,128)}) %reduce-scatter.10.cloned.1.call-update) | async-done | bytes 65552 | tf_op jit(solution)/shard_map/reduce_scatter | solution.py:254
  1000.5 32.1 %all_gather.29 = f32[1024,128]{1,0:T(8,128)S(1)} all-gather(f32[128,128]{1,0:T(8,128)} %reduce-scatter.10.cloned.1.call-done), channel_id=1, replica_groups=mesh['dp'=8,'tensor'=4] {'dp'}, dimensions={0}, use_global_device_ids=true | all-gather | bytes 589824 | tf_op jit(solution)/shard_map/all_gather | solution.py:265
  1032.6 10.3 all-gather.10.cloned.1.call-done
  1042.9 41.7 %all-gather.8.cloned.1.call-done = f32[1024,256]{1,0:T(8,128)} async-done(((f32[128,256]{1,0:T(8,128)}), f32[1024,256]{1,0:T(8,128)}) %all-gather.8.cloned.1.call-update) | async-done | bytes 1048592 | tf_op jit(solution)/shard_map/all_gather | solution.py:264
  1084.6 155.2 %all-reduce.18.cloned.1.call-done = (f32[1024,1024]{1,0:T(8,128)}, f32[1024,1024]{1,0:T(8,128)}) async-done(((f32[1024,1024]{1,0:T(8,128)}, f32[1024,1024]{1,0:T(8,128)}), (f32[1024,1024]{1,0:T(8,128)}, f32[1024,1024]{1,0:T(8,128)})) %all-reduce.18.cloned.1.call-update) | async-done | bytes 8388624 | tf_op jit(solution)/shard_map/psum | solution.py:210
  1239.8 3.6 fusion.9
  1243.4 22.2 %all-reduce.8 = (f32[1024]{0:T(1024)S(1)}, f32[1024]{0:T(1024)S(1)}) all-reduce(f32[1024]{0:T(1024)S(1)} %get-tuple-element.101, f32[1024]{0:T(1024)S(1)} %copy-done.69), channel_id=2, replica_groups=mesh['dp'=8,'tensor'=4] {'dp'}, use_global_device_ids=true, to_apply=%region_21.22.clone | all-reduce | flops 2048 | bytes 16384
  1265.6 16.3 all-gather
  1282.0 18.3 %all-gather.1 = f32[8,1,128]{2,1,0:T(1,128)S(1)} all-gather(f32[1,1,128]{2,1,0:T(1,128)S(1)} %dynamic-slice_bitcast_fusion), channel_id=1, replica_groups=mesh['dp'=8,'tensor'=4] {'dp'}, dimensions={0}, use_global_device_ids=true | all-gather | bytes 4608 | tf_op jit(solution)/shard_map/all_gather | solution.py:268
  1300.4 5.5 multiply_convert_fusion.3
  1309.6 58.7 %all-gather.12.cloned.1.call-done = f32[16,1024,128]{1,2,0:T(8,128)} async-done(((f32[16,128,128]{1,2,0:T(8,128)}), f32[16,1024,128]{1,2,0:T(8,128)}) %all-gather.12.cloned.1.call-update) | async-done | bytes 8388624 | tf_op jit(solution)/shard_map/all_gather | solution.py:269
  1368.3 9.2 copy.75
  1377.6 116.5 %all-gather.14.cloned.1.call-done = f32[16,1024,128]{1,2,0:T(8,128)} async-done(((f32[16,128,128]{1,2,0:T(8,128)}), f32[16,1024,128]{1,2,0:T(8,128)}) %all-gather.14.cloned.1.call-update) | async-done | bytes 8388624 | tf_op jit(solution)/shard_map/all_gather | solution.py:270
  1494.0 9.2 copy.76
  1503.3 116.5 %all-gather.16.cloned.1.call-done = f32[16,128,1024]{2,1,0:T(8,128)} async-done(((f32[16,128,128]{2,1,0:T(8,128)}), f32[16,128,1024]{2,1,0:T(8,128)}) %all-gather.16.cloned.1.call-update) | async-done | bytes 8388624 | tf_op jit(solution)/shard_map/all_gather | solution.py:271
  1624.5 8.5 copy.114
  (247 shorter events, 62.4 us)
Async XLA Ops:
  7.2 20.5 %copy-start = (bf16[256,1024]{1,0:T(8,128)(2,1)S(1)}, bf16[256,1024]{1,0:T(8,128)(2,1)}, u32[]{:S(2)}) copy-start(bf16[256,1024]{1,0:T(8,128)(2,1)} %param.23) | copy-start | bytes 1572868
  7.2 111.6 %all-reduce.14.cloned.1.call-start = ((), (), s32[]{:S(2)}) async-start(), calls=%async_computation.7 | async-start | bytes 8388608 | tf_op jit(solution)/shard_map/psum | solution.py:192
  16.7 6.5 copy-start.29
  30.4 231.0 %all-reduce.16.cloned.1.call-start = ((), (), s32[]{:S(2)}) async-start(), calls=%async_computation.8 | async-start | bytes 8388608 | tf_op jit(solution)/shard_map/psum | solution.py:219
  45.1 104.1 %copy-start.56 = (f32[1024]{0:T(1024)}, f32[1024]{0:T(1024)S(1)}, u32[]{:S(2)}) copy-start(f32[1024]{0:T(1024)S(1)} %fusion.80) | copy-start | bytes 12292
  46.6 75.7 %copy-start.54 = (f32[1024]{0:T(1024)S(1)}, f32[1024]{0:T(1024)}, u32[]{:S(2)}) copy-start(f32[1024]{0:T(1024)} %param.24) | copy-start | bytes 12292
  122.2 9.0 copy-start.3
  122.3 9.1 copy-start.61
  122.3 9.0 copy-start.50
  122.7 8.6 copy-start.28
  136.1 13.2 copy-start.52
  136.1 13.6 copy-start.46
  136.1 13.6 copy-start.66
  150.5 12.3 copy-start.17
  162.8 6.6 copy-start.18
  162.8 6.7 copy-start.21
  175.6 172.0 %reduce-scatter.14.cloned.1.call-start = ((), (), s32[]{:S(2)}) async-start(), calls=%async_computation.13 | async-start | bytes 1179648 | tf_op jit(solution)/shard_map/reduce_scatter | solution.py:256
  261.4 5.9 copy-start.13
  261.4 5.9 copy-start.51
  261.4 5.9 copy-start.55
  281.8 9.4 copy-start.16
  281.9 131.0 %reduce-scatter.8.cloned.1.call-start = ((), (), s32[]{:S(2)}) async-start(), calls=%async_computation.9 | async-start | bytes 1179648 | tf_op jit(solution)/shard_map/reduce_scatter | solution.py:253
  281.9 6.0 slice-start.1
  293.6 13.1 copy-start.14
  295.4 269.9 %reduce-scatter.16.cloned.1.call-start = ((), (), s32[]{:S(2)}) async-start(), calls=%async_computation.15 | async-start | bytes 9437184 | tf_op jit(solution)/shard_map/reduce_scatter | solution.py:258
  306.7 411.5 %reduce-scatter.18.cloned.1.call-start = ((), (), s32[]{:S(2)}) async-start(), calls=%async_computation.17 | async-start | bytes 9437184 | tf_op jit(solution)/shard_map/reduce_scatter | solution.py:259
  317.6 552.7 %reduce-scatter.20.cloned.1.call-start = ((), (), s32[]{:S(2)}) async-start(), calls=%async_computation.19 | async-start | bytes 9437184 | tf_op jit(solution)/shard_map/reduce_scatter | solution.py:260
  328.6 606.9 %reduce-scatter.12.cloned.1.call-start = ((), (), s32[]{:S(2)}) async-start(), calls=%async_computation.12 | async-start | bytes 589824 | tf_op jit(solution)/shard_map/reduce_scatter | solution.py:255
  345.7 654.8 %reduce-scatter.10.cloned.1.call-start = ((), (), s32[]{:S(2)}) async-start(), calls=%async_computation.11 | async-start | bytes 589824 | tf_op jit(solution)/shard_map/reduce_scatter | solution.py:254
  347.5 695.4 %all-gather.10.cloned.1.call-start = ((), (), s32[]{:S(2)}) async-start(), calls=%async_computation.14 | async-start | bytes 1179648 | tf_op jit(solution)/shard_map/all_gather | solution.py:267
  348.1 736.5 %all-gather.8.cloned.1.call-start = ((), (), s32[]{:S(2)}) async-start(), calls=%async_computation.10 | async-start | bytes 1179648 | tf_op jit(solution)/shard_map/all_gather | solution.py:264
  412.9 10.3 copy-start.43
  412.9 826.9 %all-reduce.18.cloned.1.call-start = ((), (), s32[]{:S(2)}) async-start(), calls=%async_computation.21 | async-start | bytes 16777216 | tf_op jit(solution)/shard_map/psum | solution.py:210
  428.1 442.2 %copy-start.70 = (u32[32]{0:T(128)S(1)}, u32[32]{0:T(128)}, u32[]{:S(2)}) copy-start(u32[32]{0:T(128)} %constant.125) | copy-start | bytes 388
  428.1 443.5 %copy-start.47 = (f32[1024,8]{0,1:T(8,128)S(1)}, f32[1024,8]{0,1:T(8,128)}, u32[]{:S(2)}) copy-start(f32[1024,8]{0,1:T(8,128)} %get-tuple-element.103) | copy-start | bytes 98308
  428.1 811.7 %copy-start.9 = (bf16[1024,1024]{1,0:T(8,128)(2,1)S(1)}, bf16[1024,1024]{1,0:T(8,128)(2,1)}, u32[]{:S(2)}) copy-start(bf16[1024,1024]{1,0:T(8,128)(2,1)} %param.14) | copy-start | bytes 6291460
  428.1 811.7 %copy-start.49 = (f32[1024]{0:T(1024)S(1)}, f32[1024]{0:T(1024)}, u32[]{:S(2)}) copy-start(f32[1024]{0:T(1024)} %copy-done.48) | copy-start | bytes 12292
  428.1 811.7 %copy-start.53 = (f32[1024]{0:T(1024)S(1)}, f32[1024]{0:T(1024)}, u32[]{:S(2)}) copy-start(f32[1024]{0:T(1024)} %param.19) | copy-start | bytes 12292
  428.1 940.2 %all-gather.12.cloned.1.call-start = ((), (), s32[]{:S(2)}) async-start(), calls=%async_computation.16 | async-start | bytes 9437184 | tf_op jit(solution)/shard_map/all_gather | solution.py:269
  565.3 928.7 %all-gather.14.cloned.1.call-start = ((), (), s32[]{:S(2)}) async-start(), calls=%async_computation.18 | async-start | bytes 9437184 | tf_op jit(solution)/shard_map/all_gather | solution.py:270
  718.3 901.5 %all-gather.16.cloned.1.call-start = ((), (), s32[]{:S(2)}) async-start(), calls=%async_computation.20 | async-start | bytes 9437184 | tf_op jit(solution)/shard_map/all_gather | solution.py:271
  870.3 373.1 %copy-start.69 = (f32[1024]{0:T(1024)S(1)}, f32[1024]{0:T(1024)}, u32[]{:S(2)}) copy-start(f32[1024]{0:T(1024)} %get-tuple-element.99) | copy-start | bytes 12292
  870.3 430.1 %copy-start.60 = (f32[1024]{0:T(1024)S(1)}, f32[1024]{0:T(1024)}, u32[]{:S(2)}) copy-start(f32[1024]{0:T(1024)} %copy-done.59) | copy-start | bytes 12292
  870.3 430.1 %copy-start.58 = (f32[1024]{0:T(1024)S(1)}, f32[1024]{0:T(1024)}, u32[]{:S(2)}) copy-start(f32[1024]{0:T(1024)} %copy-done.56) | copy-start | bytes 12292
  1300.4 6.9 copy-start.12
  1377.6 242.8 %copy-start.38 = (f32[1024,256]{1,0:T(8,128)S(1)}, f32[1024,256]{1,0:T(8,128)}, u32[]{:S(2)}) copy-start(f32[1024,256]{1,0:T(8,128)} %all-gather.8.cloned.1.call-done) | copy-start | bytes 3145732
  1503.3 119.6 %copy-start.37 = (f32[256,1024]{1,0:T(8,128)S(1)}, f32[256,1024]{1,0:T(8,128)}, u32[]{:S(2)}) copy-start(f32[256,1024]{1,0:T(8,128)} %all-gather.10.cloned.1.call-done) | copy-start | bytes 3145732
  1624.5 8.5 copy-start.1
  (40 other events, 112.4 us)
Sparse Core Ops, SparseCore 0:
  30.5 88.1 all-reduce.13
  175.7 85.6 all-reduce.15
  282.0 64.0 reduce-scatter.13
  350.3 62.5 reduce-scatter.7
  416.9 148.3 reduce-scatter.15
  569.8 148.3 reduce-scatter.17
  721.9 148.3 reduce-scatter.19
  874.6 60.9 reduce-scatter.11
  939.5 60.9 reduce-scatter.9
  1002.5 40.2 all-gather.9
  1045.2 39.3 all-gather.7
  1087.8 151.9 all-reduce.17
  1242.0 126.2 all-gather.11
  1370.4 123.5 all-gather.13
  1496.1 123.5 all-gather.15

commit v2 on v1

--- a/solution.py
+++ b/solution.py
@@ -1,8 +1,11 @@
+import functools
 import math
 
 import jax
 import jax.numpy as jnp
 from jax import lax
+from jax.experimental import pallas as pl
+from jax.experimental.pallas import tpu as pltpu
 from jax.sharding import PartitionSpec as P
 
 HEAD_DIM = 64
@@ -152,7 +155,297 @@
     return lax.map(one_sequence, (q_all, k_all, v_all, d_all, lse_all, lengths))
 
 
+MESH=pl.DeviceIdType.MESH
+N_CLASS = 108
+HOP = 2
+
+def dp_kernel(nz, hop, ring, WhT, dout, hT, dgu, haT, dq, dkv, acT, drb,
+              o_gate, o_up, o_down, o_q, o_k, o_v, o_out,
+              lhs, rhs, pbuf, zbuf, ybuf, ld_sem,
+              ys, yr, zs, zr, fs, fr, gs, gr, os0, os1):
+    dp = lax.axis_index("dp")
+    base = dp - dp % (2 * nz)
+    z, y = (dp % (2 * nz)) // 2, dp % 2
+    last = nz - 1
+    mate = base + z * 2 + (1 - y)
+    up_id = base + jnp.minimum(z + 1, last) * 2 + y
+    dn_id = base + jnp.maximum(z - 1, 0) * 2 + y
+
+    loads = [pltpu.make_async_copy(WhT.at[pl.ds(128 * b, 128)], lhs.at[b], ld_sem.at[b]) for b in range(16)]
+    loads += [pltpu.make_async_copy(hT.at[pl.ds(128 * b, 128)], lhs.at[16 + b], ld_sem.at[16 + b]) for b in range(8)]
+    loads += [pltpu.make_async_copy(haT.at[pl.ds(128 * b, 128)], lhs.at[24 + b], ld_sem.at[24 + b]) for b in range(8)]
+    loads += [pltpu.make_async_copy(acT.at[pl.ds(128 * b, 128)], lhs.at[32 + b], ld_sem.at[32 + b]) for b in range(2)]
+    loads += [pltpu.make_async_copy(dout.at[:, pl.ds(256 * b, 256)], rhs.at[b], ld_sem.at[34 + b]) for b in range(4)]
+    loads += [pltpu.make_async_copy(dgu.at[b], rhs.at[4 + b], ld_sem.at[38 + b]) for b in range(16)]
+    loads += [pltpu.make_async_copy(dq, rhs.at[20], ld_sem.at[54]), pltpu.make_async_copy(dkv, rhs.at[21], ld_sem.at[55])]
+    loads += [pltpu.make_async_copy(drb.at[:, pl.ds(256 * b, 256)], rhs.at[22 + b], ld_sem.at[56 + b]) for b in range(4)]
+    for ld in loads:
+        ld.start()
+
+    bar = pltpu.get_barrier_semaphore()
+    pl.semaphore_signal(bar, inc=1, device_id={"dp": mate}, device_id_type=MESH)
+
+    @pl.when(z < last)
+    def _():
+        pl.semaphore_signal(bar, inc=1, device_id={"dp": up_id}, device_id_type=MESH)
+
+    @pl.when(z > 0)
+    def _():
+        pl.semaphore_signal(bar, inc=1, device_id={"dp": dn_id}, device_id_type=MESH)
+
+    pl.semaphore_wait(bar, 1 + (z < last).astype(jnp.int32) + (z > 0).astype(jnp.int32))
+
+    for ld in loads:
+        ld.wait()
+
+    def remote(src, dst, ssem, rsem, dev):
+        return pltpu.make_async_remote_copy(src_ref=src, dst_ref=dst, send_sem=ssem, recv_sem=rsem,
+                                            device_id={"dp": dev}, device_id_type=MESH)
+
+    own = pl.ds(pl.multiple_of(y * 64, 64), 64)
+    oth = pl.ds(pl.multiple_of((1 - y) * 64, 64), 64)
+    half = pl.ds(0, 64)
+
+    def stage(c, t):
+        p = z if c == 0 else last - z
+        nxt, prv = (up_id, dn_id) if c == 0 else (dn_id, up_id)
+
+        def at(delay, body):
+            i = t - delay
+
+            @pl.when((i >= 0) & (i < N_CLASS))
+            def _():
+                body(i, i % ring, i % 2 == 0)
+
+        def ycopy_a(s):
+            return remote(pbuf.at[c, s, oth], ybuf.at[c, s, half], ys.at[c, s], yr.at[c, s], mate)
+
+        def ycopy_b(s):
+            return remote(zbuf.at[c, s], ybuf.at[c, s], ys.at[c, s], yr.at[c, s], mate)
+
+        def zcopy_a(s):
+            return remote(zbuf.at[c, s, half], zbuf.at[c, s, half], zs.at[c, s], zr.at[c, s], nxt)
+
+        def zcopy_b(s):
+            return remote(zbuf.at[c, s], zbuf.at[c, s], zs.at[c, s], zr.at[c, s], nxt)
+
+        def fcopy_a(s):
+            return remote(pbuf.at[c, s, own], pbuf.at[c, s, own], fs.at[c, s], fr.at[c, s], prv)
+
+        def fcopy_b(s):
+            return remote(pbuf.at[c, s], pbuf.at[c, s], fs.at[c, s], fr.at[c, s], prv)
+
+        def gcopy(s):
+            return remote(pbuf.at[c, s, own], ybuf.at[c, s, pl.ds(64, 64)], gs.at[c, s], gr.at[c, s], mate)
+
+        def first(i, s, is_a):
+            g = 2 * i + c
+            expert, part = g // 12, g % 12
+            a = g - 192
+            in_moe = g < 192
+            l_moe = jnp.where(part < 4, expert, 12 + part)
+            r_moe = jnp.where(part < 4, part, 4 + expert)
+            l_att = jnp.where(a < 16, 24 + a % 8, 32 + (a - 16) // 4)
+            r_att = jnp.where(a < 16, 20 + a // 8, 22 + (a - 16) % 4)
+            li = jnp.where(in_moe, l_moe, l_att)
+            ri = jnp.where(in_moe, r_moe, r_att)
+            pbuf[c, s] = jnp.dot(lhs[li], rhs[ri], preferred_element_type=jnp.float32)
+
+            @pl.when(is_a)
+            def _():
+                ycopy_a(s).start()
+
+        def second(i, s, is_a):
+            @pl.when(is_a)
+            def _():
+                ycopy_a(s).wait_recv()
+
+                @pl.when(p > 0)
+                def _():
+                    zcopy_a(s).wait_recv()
+                    zbuf[c, s, half] = zbuf[c, s, half] + (pbuf[c, s, own] + ybuf[c, s, half])
+
+                @pl.when(p == 0)
+                def _():
+                    zbuf[c, s, half] = pbuf[c, s, own] + ybuf[c, s, half]
+
+                @pl.when(p < last)
+                def _():
+                    zcopy_a(s).start()
+
+                @pl.when(p == last)
+                def _():
+                    pbuf[c, s, own] = zbuf[c, s, half]
+                    fcopy_a(s).start()
+                    gcopy(s).start()
+
+            @pl.when(jnp.logical_not(is_a))
+            def _():
+                @pl.when(p > 0)
+                def _():
+                    zcopy_b(s).wait_recv()
+                    zbuf[c, s] = zbuf[c, s] + pbuf[c, s]
+
+                @pl.when(p == 0)
+                def _():
+                    zbuf[c, s] = pbuf[c, s]
+
+                @pl.when(p < last)
+                def _():
+                    zcopy_b(s).start()
+
+                @pl.when(p == last)
+                def _():
+                    ycopy_b(s).start()
+
+        def third(i, s, is_a):
+            @pl.when(jnp.logical_not(is_a) & (p == last))
+            def _():
+                ycopy_b(s).wait_recv()
+                pbuf[c, s] = zbuf[c, s] + ybuf[c, s]
+                fcopy_b(s).start()
+
+        def fourth(i, s, is_a):
+            @pl.when(p < last)
+            def _():
+                @pl.when(is_a)
+                def _():
+                    fcopy_a(s).wait_recv()
+
+                    @pl.when(p > 0)
+                    def _():
+                        fcopy_a(s).start()
+
+                    gcopy(s).start()
+
+                @pl.when(jnp.logical_not(is_a))
+                def _():
+                    fcopy_b(s).wait_recv()
+
+                    @pl.when(p > 0)
+                    def _():
+                        fcopy_b(s).start()
+
+        def store(s, dst0, dst1):
+            pltpu.make_async_copy(pbuf.at[c, s, :, pl.ds(0, 128)], dst0, os0.at[c, s]).start()
+            pltpu.make_async_copy(pbuf.at[c, s, :, pl.ds(128, 128)], dst1, os1.at[c, s]).start()
+
+        def fifth(i, s, is_a):
+            @pl.when(is_a)
+            def _():
+                gcopy(s).wait_recv()
+                ycopy_a(s).wait_send()
+                pbuf[c, s, oth] = ybuf[c, s, pl.ds(64, 64)]
+
+            g = 2 * i + c
+            expert, part = g // 12, g % 12
+            a = g - 192
+
+            @pl.when((g < 192) & (part < 4))
+            def _():
+                col = pl.multiple_of(part * 256, 128)
+                col1 = pl.multiple_of(part * 256 + 128, 128)
+                store(s, o_down.at[expert, :, pl.ds(col, 128)], o_down.at[expert, :, pl.ds(col1, 128)])
+
+            @pl.when((g < 192) & (part >= 4))
+            def _():
+                rows = pl.ds(pl.multiple_of((part - 4) * 128, 128), 128)
+                store(s, o_gate.at[expert, rows], o_up.at[expert, rows])
+
+            @pl.when((g >= 192) & (a < 8))
+            def _():
+                rows = pl.ds(pl.multiple_of(a * 128, 128), 128)
+                store(s, o_q.at[rows, pl.ds(0, 128)], o_q.at[rows, pl.ds(128, 128)])
+
+            @pl.when((a >= 8) & (a < 16))
+            def _():
+                rows = pl.ds(pl.multiple_of((a - 8) * 128, 128), 128)
+                store(s, o_k.at[rows], o_v.at[rows])
+
+            @pl.when(a >= 16)
+            def _():
+                b = a - 16
+                rows = pl.ds(pl.multiple_of((b // 4) * 128, 128), 128)
+                col = pl.multiple_of((b % 4) * 256, 128)
+                col1 = pl.multiple_of((b % 4) * 256 + 128, 128)
+                store(s, o_out.at[rows, pl.ds(col, 128)], o_out.at[rows, pl.ds(col1, 128)])
+
+        def sixth(i, s, is_a):
+            pltpu.make_async_copy(pbuf.at[c, s, :, pl.ds(0, 128)], o_k.at[pl.ds(0, 128)], os0.at[c, s]).wait()
+            pltpu.make_async_copy(pbuf.at[c, s, :, pl.ds(0, 128)], o_k.at[pl.ds(0, 128)], os1.at[c, s]).wait()
+
+            @pl.when(is_a)
+            def _():
+                gcopy(s).wait_send()
+
+                @pl.when(p < last)
+                def _():
+                    zcopy_a(s).wait_send()
+
+                @pl.when(p > 0)
+                def _():
+                    fcopy_a(s).wait_send()
+
+            @pl.when(jnp.logical_not(is_a))
+            def _():
+                @pl.when(p < last)
+                def _():
+                    zcopy_b(s).wait_send()
+
+                @pl.when(p == last)
+                def _():
+                    ycopy_b(s).wait_send()
+
+                @pl.when(p > 0)
+                def _():
+                    fcopy_b(s).wait_send()
+
+        t2 = hop * (1 + p)
+        t3 = hop * (2 + last)
+        t4 = t3 + hop * (last - p)
+        t5 = t4 + hop
+        t6 = t5 + hop
+        return [(0, first, at), (t2, second, at), (t3, third, at), (t4, fourth, at), (t5, fifth, at), (t6, sixth, at)]
+
+    def body(t, carry):
+        both = [stage(0, t), stage(1, t)]
+        for k in (1, 2, 3, 4, 5, 0):
+            for st in both:
+                delay, fn, at = st[k]
+                at(delay, fn)
+        return carry
+
+    total = N_CLASS + hop * (2 * last + 4) + 1
+    lax.fori_loop(0, total, body, 0)
+
+
+def dp_reduce(mesh, WhT, dout, hT, dgu, haT, dq, dkv, acT, drb, hop=HOP):
+    groups = mesh.shape["dp"]
+    nz = 4 if groups % 8 == 0 else groups // 2
+    last = nz - 1
+    ring = hop * (2 * last + 4) + 2
+    ring += ring % 2
+    sh = jax.ShapeDtypeStruct
+    f32 = jnp.float32
+    outs = [sh((16, 1024, 128), f32)] * 2 + [sh((16, 128, 1024), f32), sh((1024, 256), f32), sh((1024, 128), f32), sh((1024, 128), f32), sh((256, 1024), f32)]
+    anyspec = pl.BlockSpec(memory_space=pl.ANY)
+    sem = pltpu.SemaphoreType.DMA
+    sums = pl.pallas_call(
+        functools.partial(dp_kernel, nz, hop, ring),
+        out_shape=outs, in_specs=[anyspec] * 9, out_specs=[anyspec] * 7,
+        scratch_shapes=[pltpu.VMEM((34, 128, 1024), jnp.bfloat16), pltpu.VMEM((26, 1024, 256), jnp.bfloat16),
+                        pltpu.VMEM((2, ring, 128, 256), f32), pltpu.VMEM((2, ring, 128, 256), f32), pltpu.VMEM((2, ring, 128, 256), f32),
+                        sem((60,))] + [sem((2, ring))] * 10,
+        compiler_params=pltpu.CompilerParams(collective_id=0, has_side_effects=True, vmem_limit_bytes=58 * 2**20),
+    )(WhT, dout, hT, dgu, haT, dq, dkv, acT, drb)
+    if groups > 2 * nz:
+        same = [[2 * nz * block + place for block in range(groups // (2 * nz))] for place in range(2 * nz)]
+        sums = lax.psum(tuple(sums), "dp", axis_index_groups=same)
+    return sums
+
+
 def per_device(
+    mesh,
     tokens,
     lengths,
     chosen,
@@ -209,9 +502,6 @@
     moe_part = jnp.einsum("tef,efd->td", hidden_w, w_down, preferred_element_type=jnp.float32)
     moe_sum = lax.psum(moe_part, "tensor")
     result = ((resid + moe_sum) * valid_f).astype(jnp.bfloat16)
-    grad_down = jnp.einsum("tef,td->efd", hidden_w, cotangent, preferred_element_type=jnp.float32)
-    grad_gate = jnp.einsum("td,tef->edf", h_moe, d_gate_b, preferred_element_type=jnp.float32)
-    grad_up = jnp.einsum("td,tef->edf", h_moe, d_up_b, preferred_element_type=jnp.float32)
     d_h_part = jnp.einsum("tef,edf->td", d_gate_b, w_gate, preferred_element_type=jnp.float32)
     d_h_part = d_h_part + jnp.einsum(
         "tef,edf->td", d_up_b, w_up, preferred_element_type=jnp.float32
@@ -221,7 +511,6 @@
     d_resid_n, grad_norm_moe = pull_moe(d_h_moe)
     d_resid = d_out + d_resid_n
     d_resid_b = d_resid.astype(jnp.bfloat16)
-    grad_out = jnp.einsum("tf,td->fd", attn_cat, d_resid_b, preferred_element_type=jnp.float32)
     d_attn = jnp.einsum("td,fd->tf", d_resid_b, w_out, preferred_element_type=jnp.float32).astype(
         jnp.bfloat16
     )
@@ -234,9 +523,6 @@
     d_query = pull_query(d_q_rot)[0].astype(jnp.bfloat16).reshape(tok_rows, -1)
     d_key = pull_key(d_k_rot)[0].astype(jnp.bfloat16).reshape(tok_rows, -1)
     d_value = d_v_all.astype(jnp.bfloat16).reshape(tok_rows, -1)
-    grad_query = jnp.einsum("td,tf->df", h_attn, d_query, preferred_element_type=jnp.float32)
-    grad_key = jnp.einsum("td,tf->df", h_attn, d_key, preferred_element_type=jnp.float32)
-    grad_value = jnp.einsum("td,tf->df", h_attn, d_value, preferred_element_type=jnp.float32)
     d_h_part_a = jnp.einsum("tf,df->td", d_query, w_query, preferred_element_type=jnp.float32)
     d_h_part_a = d_h_part_a + jnp.einsum(
         "tf,df->td", d_key, w_key, preferred_element_type=jnp.float32
@@ -248,41 +534,34 @@
     unused_a, pull_attn = jax.vjp(rms_norm, x_in, norm_attn)
     d_x_n, grad_norm_attn = pull_attn(d_h_attn)
     grad_tokens = (d_resid + d_x_n).astype(jnp.bfloat16)
-    summed = (
-        lax.psum_scatter(grad_norm_attn, "dp", scatter_dimension=0, tiled=True),
-        lax.psum_scatter(grad_query, "dp", scatter_dimension=0, tiled=True),
-        lax.psum_scatter(grad_key, "dp", scatter_dimension=0, tiled=True),
-        lax.psum_scatter(grad_value, "dp", scatter_dimension=0, tiled=True),
-        lax.psum_scatter(grad_out, "dp", scatter_dimension=1, tiled=True),
-        lax.psum_scatter(grad_norm_moe, "dp", scatter_dimension=0, tiled=True),
-        lax.psum_scatter(grad_gate, "dp", scatter_dimension=1, tiled=True),
-        lax.psum_scatter(grad_up, "dp", scatter_dimension=1, tiled=True),
-        lax.psum_scatter(grad_down, "dp", scatter_dimension=2, tiled=True),
-    )
-    full = (
-        lax.all_gather(summed[0], "dp", axis=0, tiled=True),
-        lax.all_gather(summed[1], "dp", axis=0, tiled=True),
-        lax.all_gather(summed[2], "dp", axis=0, tiled=True),
-        lax.all_gather(summed[3], "dp", axis=0, tiled=True),
-        lax.all_gather(summed[4], "dp", axis=1, tiled=True),
-        lax.all_gather(summed[5], "dp", axis=0, tiled=True),
-        lax.all_gather(summed[6], "dp", axis=1, tiled=True),
-        lax.all_gather(summed[7], "dp", axis=1, tiled=True),
-        lax.all_gather(summed[8], "dp", axis=2, tiled=True),
+    grad_norm_attn, grad_norm_moe = lax.psum((grad_norm_attn, grad_norm_moe), "dp")
+    hidden_t = hidden_w.reshape(tok_rows, -1).T
+    d_gate_up = jnp.concatenate([d_gate_b, d_up_b], axis=2).transpose(1, 0, 2)
+    grad_gate, grad_up, grad_down, grad_query, grad_key, grad_value, grad_out = dp_reduce(
+        mesh,
+        hidden_t,
+        cotangent,
+        h_moe.T,
+        d_gate_up,
+        h_attn.T,
+        d_query,
+        jnp.concatenate([d_key, d_value], axis=1),
+        attn_cat.T,
+        d_resid_b,
     )
     return (
         result,
         grad_tokens,
         d_gates,
-        full[0],
-        full[1],
-        full[2],
-        full[3],
-        full[4],
-        full[5],
-        full[6],
-        full[7],
-        full[8],
+        grad_norm_attn,
+        grad_query,
+        grad_key,
+        grad_value,
+        grad_out,
+        grad_norm_moe,
+        grad_gate,
+        grad_up,
+        grad_down,
     )
 
 
@@ -304,7 +583,7 @@
         P(None, "tensor", None),
     )
     return jax.shard_map(
-        per_device,
+        functools.partial(per_device, mesh),
         mesh=mesh,
         in_specs=placed,
         out_specs=(

time: 1650 us -> 1040 us (0.63)
  waiting for transfers between devices: 1250 us -> 261 us
  Pallas kernels: 0 us -> 490 us
  blocking collectives: 133 us -> 34.6 us
  matrix products: 126 us -> 76.6 us
  local copies, waits for them, and re-layouts: 62.4 us -> 83.2 us
  other arithmetic: 53.2 us -> 70.7 us
    reduce_scatter x7 -> x0, waiting for transfers between devices: 591 us -> none  [the longest x1 153 us: per_device(): lax.psum_scatter(grad_up, 'dp', scatter_dimension=1, tiled=True)]
    pallas_call x0 -> x1, Pallas kernels: none -> 490 us  [dp_reduce(): pl.pallas_call(functools.partial(dp_kernel, nz, hop, ring), out_shape=out...]
    all_gather x5 -> x0, waiting for transfers between devices: 344 us -> none  [the longest x1 116 us: per_device(): lax.all_gather(summed[7], 'dp', axis=1, tiled=True)]
    all_gather x4 -> x0, blocking collectives: 99.1 us -> none  [the longest x1 32.3 us: per_device(): lax.all_gather(summed[3], 'dp', axis=0, tiled=True)]
    psum x1, waiting for transfers between devices: 155 us -> 114 us  [per_device(): moe_sum = lax.psum(moe_part, 'tensor')]
    dot_general x7 -> x0, matrix products: 39 us -> none  [the longest x1 10.8 us: per_device(): jnp.einsum('td,tef->edf', h_moe, d_up_b, preferred_element_type=jnp.float32)]
    unnamed x1 -> x0, blocking collectives: 22.2 us -> none
    psum x0 -> x1, blocking collectives: none -> 21.8 us  [per_device(): lax.psum((grad_norm_attn, grad_norm_moe), 'dp')]
  transfers between devices with their start and end apart: 15 -> 3, of which waited for: 14 -> 3; matrix products, arithmetic and copies ran while one was open for 8% -> 5% of each run, Pallas kernels for 0% -> 0%
where the time goes in v2:
time: 1040 us; the launch traced here: 1030 us
  Pallas kernels  490 us (47%)
  waiting for transfers between devices  261 us (25%)
  local copies, waits for them, and re-layouts  83.2 us (8%)
  matrix products  76.6 us (7%)
  other arithmetic  70.7 us (7%)
  blocking collectives  34.6 us (3%)
  between operations  16.4 us (2%)
    pallas_call x1, Pallas kernels, dp_reduce(): pl.pallas_call(functools.partial(dp_kernel, nz, hop, ring), out_shape=out...  490 us
    psum x1, waiting for transfers between devices, per_device(): moe_sum = lax.psum(moe_part, 'tensor')  114 us
    psum x1, waiting for transfers between devices, per_device(): d_h_moe, d_gates = lax.psum((d_h_part, d_gate_part), 'tensor')  74.9 us
    psum x1, waiting for transfers between devices, per_device(): attn_sum = lax.psum(dot_f(attn_cat, w_out), 'tensor')  72.4 us
    unnamed x151, local copies, waits for them, and re-layouts  48 us
    psum x1, blocking collectives, per_device(): lax.psum((grad_norm_attn, grad_norm_moe), 'dp')  21.8 us
  transfers between devices with their start and end apart: 3, of which 3 were waited for; matrix products, arithmetic and copies ran while one was open for 5% of the time, Pallas kernels for 0%

profile of v2, /device:TPU:0, one launch (start us, length us, event | category | flops | bytes accessed | tf_op | source)
XLA Modules:
  0.0 1033.2 jit_solution(14330461078089051071)
XLA Ops:
  7.3 2.2 fusion.15
  9.6 2.6 convolution_convert_fusion.1
  16.6 1.6 fusion.89
  19.5 2.1 copy-done.1
  21.5 1.5 fusion.45
  26.7 2.8 fusion.63
  31.1 6.4 copy.90
  37.5 6.5 copy.87
  44.0 1.4 convert_reduce_fusion
  45.5 72.4 %all-reduce.12.cloned.1.call-done = f32[1024,1024]{1,0:T(8,128)} async-done(((f32[1024,1024]{1,0:T(8,128)}), f32[1024,1024]{1,0:T(8,128)}) %all-reduce.12.cloned.1.call-update) | async-done | bytes 4194320 | tf_op jit(solution)/shard_map/psum | solution.py:485
  117.8 3.0 multiply_reduce_fusion.3
  121.3 7.0 fusion.93
  128.3 9.2 copy.91
  137.5 11.5 %fusion.92 = f32[1024,2048]{0,1} fusion(bf16[1024,2048]{0,1:T(8,128)(2,1)} %bitcast.206, f32[1024,1024]{1,0:T(8,128)} %copy-done.2, f32[1024]{0:T(1024)S(1)} %copy-done.44, f32[1024]{0:T(1024)S(1)} %fusion.73), kind=kOutput, calls=%fused_computation.154 | convolution fusion | flops 4298113024 | bytes 16785408
  149.0 9.2 copy.89
  158.2 12.7 %multiply_reduce_fusion = (f32[1024,16]{0,1:T(8,128)S(1)}, f32[1024,16,128]{2,0,1:T(8,128)}) fusion(f32[1024,16,128]{2,0,1:T(8,128)} %copy.91, f32[1024,16,128]{2,0,1:T(8,128)} %copy.89, bf16[16,128,1024]{2,1,0:T(8,128)(2,1)} %param.27, bf16[1024,1024]{1,0:T(8,128)(2,1)} %dout.1), kind=kOutput, calls=%fused_computation.7 | convolution fusion | flops 4309630976 | bytes 31522816 | tf_op jit(solution)/shard_map/td,efd->tef/dot_general | solution.py:492
  172.2 20.2 %multiply_convert_fusion = (bf16[1024,16,128]{2,0,1:T(8,128)(2,1)S(1)}, bf16[1024,16,128]{2,0,1:T(8,128)(2,1)S(1)}, bf16[1024,16,128]{2,0,1:T(8,128)(2,1)}) fusion(f32[1024,16,128]{2,0,1:T(8,128)} %get-tuple-element.117, f32[1024,16]{0,1:T(8,128)S(1)} %mul.450, f32[1024,16,128]{2,0,1:T(8,128)S(1)} %copy-done.7, f32[1024,16,128]{2,0,1:T(8,128)} %copy.91), kind=kLoop, calls=%fused_computation.9 | loop fusion | flops 35651584 | bytes 37814272 | tf_op jit(solution)/shard_map/convert_element_type | solution.py:501
  192.5 4.5 fusion.94
  197.6 6.0 bitcast_add_fusion
  205.8 8.8 convolution_bitcast_fusion
  214.6 74.9 %all-reduce.14.cloned.1.call-done = f32[1024,1024]{1,0:T(8,128)} async-done(((f32[1024,1024]{1,0:T(8,128)}), f32[1024,1024]{1,0:T(8,128)}) %all-reduce.14.cloned.1.call-update) | async-done | bytes 4194320 | tf_op jit(solution)/shard_map/psum | solution.py:509
  289.5 5.2 multiply_reduce_fusion.1
  295.4 4.3 fusion.83
  300.5 2.2 copy-done.5
  303.6 1.2 fusion.19
  307.3 1.8 fusion
  309.2 2.6 fusion.2
  314.7 1.4 fusion.37
  317.0 1.4 fusion.41
  319.2 2.9 add_add_fusion.2
  323.9 6.5 copy.102
  330.4 3.9 fusion.140
  334.4 3.9 copy.105.hT
  338.3 12.8 %psum.53 = f32[1024,8]{0,1:T(8,128)} all-reduce(f32[1024,8]{0,1:T(8,128)S(1)} %copy-done.39), channel_id=1, replica_groups=mesh['dp'=8,'tensor'=4] {'tensor'}, use_global_device_ids=true, to_apply=%region_19.20 | all-reduce | flops 8192 | bytes 65536 | tf_op jit(solution)/shard_map/psum | solution.py:509
  351.1 8.1 maximum_bitcast_fusion.dgu
  362.4 113.7 %all-reduce.16.cloned.1.call-done = (f32[1024,1024]{1,0:T(8,128)}, f32[1024,1024]{1,0:T(8,128)}) async-done(((f32[1024,1024]{1,0:T(8,128)}, f32[1024,1024]{1,0:T(8,128)}), (f32[1024,1024]{1,0:T(8,128)}, f32[1024,1024]{1,0:T(8,128)})) %all-reduce.16.cloned.1.call-update) | async-done | bytes 8388624 | tf_op jit(solution)/shard_map/psum | solution.py:503
  476.1 5.3 multiply_convert_fusion.3
  481.5 1.4 fusion.9
  483.7 3.0 fusion.77
  486.7 3.9 copy.106.haT
  490.6 490.3 %shard_map.229 = (f32[16,1024,128]{2,1,0:T(8,128)}, f32[16,1024,128]{2,1,0:T(8,128)}, f32[16,128,1024]{2,1,0:T(8,128)}, f32[1024,256]{1,0:T(8,128)}, f32[1024,12...) custom-call(bf16[2048,1024]{1,0:T(8,128)(2,1)} %bitcast.191, bf16[1024,1024]{1,0:T(8,128)(2,1)} %dout.1, ...), custom_call_target="tpu_custom_call" | custom-call | tf_op jit(solution)/shard_map/pallas_call | solution.py:433
  981.0 21.8 %all-reduce.6 = (f32[1024]{0:T(1024)}, f32[1024]{0:T(1024)}) all-reduce(f32[1024]{0:T(1024)S(1)} %get-tuple-element.79, f32[1024]{0:T(1024)S(1)} %copy-done.62), channel_id=1, replica_groups=mesh['dp'=8,'tensor'=4] {'dp'}, use_global_device_ids=true, to_apply=%region_21.22 | all-reduce | flops 2048 | bytes 16384 | tf_op jit(solution)/shard_map/psum | solution.py:537
  1002.8 2.3 copy.137
  1005.0 1.9 copy.138
  1006.9 2.0 copy.139
  1009.9 7.7 copy.141
  1017.7 4.3 copy.142
  1022.9 3.4 copy.143
  (204 shorter events, 30.8 us)
Async XLA Ops:
  7.2 19.5 %copy-start = (bf16[256,1024]{1,0:T(8,128)(2,1)S(1)}, bf16[256,1024]{1,0:T(8,128)(2,1)}, u32[]{:S(2)}) copy-start(bf16[256,1024]{1,0:T(8,128)(2,1)} %param.23) | copy-start | bytes 1572868
  7.2 4.9 copy-start.6
  7.2 4.9 copy-start.63
  7.2 4.9 copy-start.35
  7.2 110.6 %all-reduce.12.cloned.1.call-start = ((), (), s32[]{:S(2)}) async-start(), calls=%async_computation | async-start | bytes 8388608 | tf_op jit(solution)/shard_map/psum | solution.py:485
  9.5 3.6 copy-start.50
  9.5 4.2 copy-start.54
  9.6 4.2 copy-start.31
  12.2 7.3 copy-start.29
  15.2 8.0 copy-start.27
  19.4 3.6 copy-start.61
  29.5 260.0 %all-reduce.14.cloned.1.call-start = ((), (), s32[]{:S(2)}) async-start(), calls=%async_computation.1 | async-start | bytes 8388608 | tf_op jit(solution)/shard_map/psum | solution.py:509
  44.0 126.9 %copy-start.47 = (f32[1024]{0:T(1024)}, f32[1024]{0:T(1024)S(1)}, u32[]{:S(2)}) copy-start(f32[1024]{0:T(1024)S(1)} %fusion.74) | copy-start | bytes 12292
  45.5 75.4 %copy-start.44 = (f32[1024]{0:T(1024)S(1)}, f32[1024]{0:T(1024)}, u32[]{:S(2)}) copy-start(f32[1024]{0:T(1024)} %param.24) | copy-start | bytes 12292
  120.8 7.5 copy-start.2
  120.8 7.5 copy-start.52
  120.8 16.7 %copy-start.40 = (f32[1024]{0:T(1024)}, f32[1024]{0:T(1024)S(1)}, u32[]{:S(2)}) copy-start(f32[1024]{0:T(1024)S(1)} %fusion.73) | copy-start | bytes 12292
  158.2 12.7 %copy-start.43 = (f32[1024,16]{0,1:T(8,128)S(1)}, f32[1024,16]{0,1:T(8,128)}, u32[]{:S(2)}) copy-start(f32[1024,16]{0,1:T(8,128)} %convert_reduce_fusion) | copy-start | bytes 196612
  158.2 13.2 %copy-start.38 = (s32[1024,8]{0,1:T(8,128)S(1)}, s32[1024,8]{0,1:T(8,128)}, u32[]{:S(2)}) copy-start(s32[1024,8]{0,1:T(8,128)} %param.16) | copy-start | bytes 98308
  158.2 13.2 %copy-start.58 = (f32[1024,8]{0,1:T(8,128)S(1)}, f32[1024,8]{0,1:T(8,128)}, u32[]{:S(2)}) copy-start(f32[1024,8]{0,1:T(8,128)} %param.17) | copy-start | bytes 98308
  158.2 14.0 %copy-start.7 = (f32[1024,16,128]{2,0,1:T(8,128)S(1)}, f32[1024,16,128]{2,0,1:T(8,128)}, u32[]{:S(2)}) copy-start(f32[1024,16,128]{2,0,1:T(8,128)} %copy.89) | copy-start | bytes 25165828
  172.2 20.3 %copy-start.16 = (bf16[16,1024,128]{2,1,0:T(8,128)(2,1)S(1)}, bf16[16,1024,128]{2,1,0:T(8,128)(2,1)}, u32[]{:S(2)}) copy-start(bf16[16,1024,128]{2,1,0:T(8,128)(2,1)} %param.25) | copy-start | bytes 12582916
  192.5 4.6 copy-start.10
  192.5 4.6 copy-start.9
  192.5 5.1 copy-start.17
  203.7 272.5 %all-reduce.16.cloned.1.call-start = ((), (), s32[]{:S(2)}) async-start(), calls=%async_computation.2 | async-start | bytes 16777216 | tf_op jit(solution)/shard_map/psum | solution.py:503
  289.5 5.2 copy-start.53
  289.5 5.2 copy-start.3
  289.5 5.9 copy-start.8
  289.5 5.9 copy-start.41
  289.5 5.9 copy-start.45
  289.5 5.9 copy-start.48
  299.7 3.9 copy-start.13
  303.6 3.6 slice-start.1
  323.9 6.5 copy-start.42
  323.9 6.5 copy-start.46
  330.4 7.9 copy-start.39
  351.1 8.1 copy-start.15
  351.1 125.0 %copy-start.49 = (f32[1024]{0:T(1024)S(1)}, f32[1024]{0:T(1024)}, u32[]{:S(2)}) copy-start(f32[1024]{0:T(1024)} %copy-done.47) | copy-start | bytes 12292
  476.1 5.3 copy-start.12
  476.1 5.3 copy-start.55
  476.1 5.3 copy-start.64
  490.6 490.3 %copy-start.62 = (f32[1024]{0:T(1024)S(1)}, f32[1024]{0:T(1024)}, u32[]{:S(2)}) copy-start(f32[1024]{0:T(1024)} %get-tuple-element.77) | copy-start | bytes 12292
  980.9 28.0 %copy-start.20 = (f32[256,1024]{1,0:T(8,128)S(1)}, f32[256,1024]{1,0:T(8,128)}, u32[]{:S(2)}) copy-start(f32[256,1024]{1,0:T(8,128)} %get-tuple-element.145) | copy-start | bytes 3145732
  1006.9 10.7 %slice-start.4 = ((s8[8388608]{0:T(1024)(128)(4,1)}), s8[4194304]{0:T(1024)(128)(4,1)S(1)}, s32[]{:S(2)}) async-start(s8[8388608]{0:T(1024)(128)(4,1)} %bitcast.194), calls=%async_computation.7 | async-start | bytes 8388608
  1009.9 7.7 slice-start.5
  1009.9 12.0 %slice-start.2 = ((s8[8388608]{0:T(1024)(128)(4,1)}), s8[4194304]{0:T(1024)(128)(4,1)S(1)}, s32[]{:S(2)}) async-start(s8[8388608]{0:T(1024)(128)(4,1)} %bitcast.192), calls=%async_computation.5 | async-start | bytes 8388608
  1017.6 5.2 slice-start.3
  (26 other events, 49.2 us)
Sparse Core Ops, SparseCore 0:
  29.6 88.1 all-reduce.11
  203.8 85.6 all-reduce.13
  322.2 153.8 all-reduce.15

commit v3 on v2

--- a/solution.py
+++ b/solution.py
@@ -7,6 +7,8 @@
 from jax.experimental import pallas as pl
 from jax.experimental.pallas import tpu as pltpu
 from jax.sharding import PartitionSpec as P
+
+MESH = pl.DeviceIdType.MESH
 
 HEAD_DIM = 64
 TOP_K = 8
@@ -55,7 +57,7 @@
     limit = ((5 * pairs + 4 * EXPERTS - 1) // (4 * EXPERTS)).astype(jnp.float32)
     kept = jnp.where((places < limit) & (hits > 0), 1.0, 0.0)
     weights = jnp.sum(onehot_f * gate_values[:, :, None], axis=1) * kept
-    return (weights, kept, onehot_f)
+    return (weights, onehot_f)
 
 
 def block_scores(q_block, start, k_seq, length, scaling):
@@ -80,25 +82,6 @@
     lse_part = (top_s + jnp.log(total))[..., 0]
     out_b = jnp.einsum("kgqs,skd->qkgd", probs, v_seq, preferred_element_type=jnp.float32)
     return (out_b.reshape(q_block.shape[0], -1), lse_part)
-
-
-def backward_block(q_block, d_block, start, lse_block, k_seq, v_seq, length, scaling):
-    scores, grouped = block_scores(q_block, start, k_seq, length, scaling)
-    exact = jnp.exp(scores - lse_block[..., None])
-    probs = exact.astype(jnp.bfloat16)
-    d_grouped = d_block.reshape(grouped.shape)
-    d_probs = jnp.einsum("qkgd,skd->kgqs", d_grouped, v_seq, preferred_element_type=jnp.float32)
-    inner = jnp.sum(exact * d_probs, axis=-1, keepdims=True)
-    d_scores = (exact * (d_probs - inner)).astype(jnp.bfloat16)
-    d_query = (
-        jnp.einsum("kgqs,skd->qkgd", d_scores, k_seq, preferred_element_type=jnp.float32) * scaling
-    )
-    d_key = (
-        jnp.einsum("kgqs,qkgd->skd", d_scores, grouped, preferred_element_type=jnp.float32)
-        * scaling
-    )
-    d_value = jnp.einsum("kgqs,qkgd->skd", probs, d_grouped, preferred_element_type=jnp.float32)
-    return (d_query.reshape(q_block.shape), d_key, d_value)
 
 
 def attend_forward(q_all, k_all, v_all, lengths, scaling):
@@ -123,67 +106,73 @@
     return lax.map(one_sequence, (q_all, k_all, v_all, lengths))
 
 
-def attend_backward(q_all, k_all, v_all, d_all, lse_all, lengths, scaling):
-    seq_len = q_all.shape[1]
-    q_rows = min(512, seq_len)
-    n_blocks = seq_len // q_rows
-
-    def one_sequence(item):
-        q_seq, k_seq, v_seq, d_seq, lse_seq, length = item
-        sum_key = jnp.zeros(k_seq.shape, jnp.float32)
-        sum_value = jnp.zeros(k_seq.shape, jnp.float32)
-        d_queries = []
-        for block in range(n_blocks):
-            start = block * q_rows
-            finish = start + q_rows
-            d_query, d_key, d_value = backward_block(
-                q_seq[start:finish],
-                d_seq[start:finish],
-                start,
-                lse_seq[block],
-                k_seq[:finish],
-                v_seq[:finish],
-                length,
-                scaling,
-            )
-            padding = ((0, seq_len - finish), (0, 0), (0, 0))
-            sum_key = sum_key + jnp.pad(d_key, padding)
-            sum_value = sum_value + jnp.pad(d_value, padding)
-            d_queries.append(d_query)
-        return (jnp.concatenate(d_queries, axis=0), sum_key, sum_value)
-
-    return lax.map(one_sequence, (q_all, k_all, v_all, d_all, lse_all, lengths))
-
-
-MESH=pl.DeviceIdType.MESH
-N_CLASS = 108
+LANES = 128
+ROWS = 256
+N_CLASS = 109
 HOP = 2
-
-def dp_kernel(nz, hop, ring, WhT, dout, hT, dgu, haT, dq, dkv, acT, drb,
-              o_gate, o_up, o_down, o_q, o_k, o_v, o_out,
-              lhs, rhs, pbuf, zbuf, ybuf, ld_sem,
-              ys, yr, zs, zr, fs, fr, gs, gr, os0, os1):
+T_HEAD = 19
+T_SUM1 = 16
+T_MID1 = 33
+T_ATT = 37
+T_TURN = 53
+T_PROJ = 57
+T_SUM2 = 61
+T_TOK = 78
+T_MOE = 82
+T_SUM3 = 90
+T_RES = 107
+
+
+def dot_nt(left, right):
+    return lax.dot_general(
+        left, right, (((1,), (1,)), ((), ())), preferred_element_type=jnp.float32
+    )
+
+
+def dot_tn(left, right):
+    return lax.dot_general(
+        left, right, (((0,), (0,)), ((), ())), preferred_element_type=jnp.float32
+    )
+
+
+def layer_kernel(
+    nz, hop, ring,
+    length, cat_in, w_full, x_in, d_out, w_slot, gains, w_gate, w_up, w_down,
+    q_in, k_in, v_in, kt_in, lse_in, cos_in, sin_in, wo_in, wq_in, wkv_in,
+    o_gate, o_up, o_down, o_q, o_k, o_v, o_out, o_norm, o_result, o_tokens, o_dots, s_resid, s_dres,
+    lhs, rhs, pbuf, zbuf, ybuf, acc, buf1, buf2, hbuf, wgu, wdb, q2, k2, v2, kt2, lse, cos_t, sin_t,
+    da2, dk_acc, dv_acc, slot_w, gain, norms,
+    ld, wsem, iosem, ys, yr, zs, zr, fs, fr, gs, gr, os0, os1,
+    cs_c, cr_c, cs_x, cr_x, cs_f, cr_f, s1s, s1r, s2s, s2r, s3s, s3r, ready1, ready2, ready3,
+):
+    f32, bf16 = jnp.float32, jnp.bfloat16
     dp = lax.axis_index("dp")
+    tensor = lax.axis_index("tensor")
     base = dp - dp % (2 * nz)
     z, y = (dp % (2 * nz)) // 2, dp % 2
     last = nz - 1
     mate = base + z * 2 + (1 - y)
     up_id = base + jnp.minimum(z + 1, last) * 2 + y
     dn_id = base + jnp.maximum(z - 1, 0) * 2 + y
-
-    loads = [pltpu.make_async_copy(WhT.at[pl.ds(128 * b, 128)], lhs.at[b], ld_sem.at[b]) for b in range(16)]
-    loads += [pltpu.make_async_copy(hT.at[pl.ds(128 * b, 128)], lhs.at[16 + b], ld_sem.at[16 + b]) for b in range(8)]
-    loads += [pltpu.make_async_copy(haT.at[pl.ds(128 * b, 128)], lhs.at[24 + b], ld_sem.at[24 + b]) for b in range(8)]
-    loads += [pltpu.make_async_copy(acT.at[pl.ds(128 * b, 128)], lhs.at[32 + b], ld_sem.at[32 + b]) for b in range(2)]
-    loads += [pltpu.make_async_copy(dout.at[:, pl.ds(256 * b, 256)], rhs.at[b], ld_sem.at[34 + b]) for b in range(4)]
-    loads += [pltpu.make_async_copy(dgu.at[b], rhs.at[4 + b], ld_sem.at[38 + b]) for b in range(16)]
-    loads += [pltpu.make_async_copy(dq, rhs.at[20], ld_sem.at[54]), pltpu.make_async_copy(dkv, rhs.at[21], ld_sem.at[55])]
-    loads += [pltpu.make_async_copy(drb.at[:, pl.ds(256 * b, 256)], rhs.at[22 + b], ld_sem.at[56 + b]) for b in range(4)]
-    for ld in loads:
-        ld.start()
+    core = tensor % 2
+    core_mate = tensor - core + (1 - core)
+    x_mate = (tensor + 2) % 4
+
+    def local(src, dst, sem):
+        return pltpu.make_async_copy(src, dst, sem)
+
+    def remote(src, dst, ssem, rsem, dev, axis="dp"):
+        return pltpu.make_async_remote_copy(
+            src_ref=src, dst_ref=dst, send_sem=ssem, recv_sem=rsem,
+            device_id={axis: dev}, device_id_type=MESH,
+        )
+
+    def block(b, size=ROWS):
+        return pl.ds(pl.multiple_of(b * size, size), size)
 
     bar = pltpu.get_barrier_semaphore()
-    pl.semaphore_signal(bar, inc=1, device_id={"dp": mate}, device_id_type=MESH)
+    for axis, dev in (("dp", mate), ("tensor", core_mate), ("tensor", x_mate)):
+        pl.semaphore_signal(bar, inc=1, device_id={axis: dev}, device_id_type=MESH)
 
     @pl.when(z < last)
     def _():
@@ -193,14 +182,420 @@
     def _():
         pl.semaphore_signal(bar, inc=1, device_id={"dp": dn_id}, device_id_type=MESH)
 
-    pl.semaphore_wait(bar, 1 + (z < last).astype(jnp.int32) + (z > 0).astype(jnp.int32))
-
-    for ld in loads:
-        ld.wait()
-
-    def remote(src, dst, ssem, rsem, dev):
-        return pltpu.make_async_remote_copy(src_ref=src, dst_ref=dst, send_sem=ssem, recv_sem=rsem,
-                                            device_id={"dp": dev}, device_id_type=MESH)
+    wide = pl.ds(0, 1024)
+    loads = [
+        local(w_full.at[pl.ds(0, 512)], buf1.at[:, wide], ld.at[0]),
+        local(w_full.at[pl.ds(512, 512)], buf2.at[:, wide], ld.at[1]),
+        local(x_in, hbuf, ld.at[2]),
+        local(gains, gain, ld.at[3]),
+        local(w_slot, slot_w, ld.at[4]),
+        local(d_out.at[:, pl.ds(0, 256)], rhs.at[0], ld.at[5]),
+        local(d_out.at[:, pl.ds(256, 256)], rhs.at[1], ld.at[6]),
+        local(d_out.at[:, pl.ds(512, 256)], rhs.at[2], ld.at[7]),
+        local(d_out.at[:, pl.ds(768, 256)], rhs.at[3], ld.at[8]),
+        local(cat_in, acc.at[:, block(tensor)], ld.at[9]),
+        local(q_in, q2, ld.at[10]),
+        local(k_in, k2, ld.at[11]),
+        local(v_in, v2, ld.at[12]),
+        local(kt_in, kt2, ld.at[13]),
+        local(lse_in, lse, ld.at[14]),
+        local(cos_in, cos_t, ld.at[15]),
+        local(sin_in, sin_t, ld.at[16]),
+    ]
+
+    def expert_load(e, s):
+        return [
+            local(w_gate.at[e], wgu.at[s, :, pl.ds(0, LANES)], wsem.at[s, 0]),
+            local(w_up.at[e], wgu.at[s, :, pl.ds(LANES, LANES)], wsem.at[s, 1]),
+            local(w_down.at[e], wdb.at[s], wsem.at[s, 2]),
+        ]
+
+    for copy in loads:
+        copy.start()
+    for copy in expert_load(0, 0):
+        copy.start()
+    pl.semaphore_wait(bar, 3 + (z < last).astype(jnp.int32) + (z > 0).astype(jnp.int32))
+
+    def gather_x(b):
+        return remote(
+            cat_in.at[block(b)], acc.at[block(b), block(tensor)], cs_x.at[b], cr_x.at[b], x_mate, "tensor"
+        )
+
+    def gather_c(b):
+        return remote(
+            cat_in.at[block(b)], acc.at[block(b), block(tensor)], cs_c.at[b], cr_c.at[b], core_mate, "tensor"
+        )
+
+    def gather_f(b):
+        part = acc.at[block(b), block(x_mate)]
+        return remote(part, part, cs_f.at[b], cr_f.at[b], core_mate, "tensor")
+
+    for b in range(4):
+        gather_x(b).start()
+    for b in range(4):
+        gather_c(b).start()
+    for copy in loads:
+        copy.wait()
+
+    def cast_out(b, carry):
+        for col in range(4):
+            rhs[22 + col, block(b, 64), :] = buf1[block(b, 64), 256 * col : 256 * col + 256].astype(bf16)
+            rhs[22 + col, pl.ds(pl.multiple_of(512 + b * 64, 64), 64), :] = buf2[
+                block(b, 64), 256 * col : 256 * col + 256
+            ].astype(bf16)
+        return carry
+
+    lax.fori_loop(0, 8, cast_out, 0)
+
+    def forward_rows(b, carry):
+        rows = block(b)
+        for k in range(4):
+            part = acc[rows, 256 * k : 256 * k + 256].astype(bf16)
+            if k == 0:
+                sums = [
+                    hbuf[rows, 256 * col : 256 * col + 256].astype(f32) + dot_f(part, rhs[22 + col, 0:256, :])
+                    for col in range(4)
+                ]
+            else:
+                sums = [
+                    sums[col] + dot_f(part, rhs[22 + col, 256 * k : 256 * k + 256, :]) for col in range(4)
+                ]
+        for half_c in range(2):
+            own_c = pl.ds(pl.multiple_of(tensor * 256 + half_c * 128, 128), 128)
+            lhs[32 + half_c, :, rows] = acc[rows, own_c].T.astype(bf16)
+        square = sum(jnp.sum(v * v, axis=1, keepdims=True) for v in sums)
+        scale_r = lax.rsqrt(square * (1.0 / 1024.0) + EPSILON)
+        for col in range(4):
+            acc[rows, 256 * col : 256 * col + 256] = sums[col]
+            normed = sums[col] * scale_r * gain[0:1, 256 * col : 256 * col + 256]
+            hbuf[rows, 256 * col : 256 * col + 256] = normed.astype(bf16)
+            for half_c in range(2):
+                lhs[16 + 2 * col + half_c, :, rows] = normed[:, 128 * half_c : 128 * half_c + 128].T.astype(bf16)
+        return carry
+
+    for b in range(4):
+        gather_x(b).wait_recv()
+        gather_f(b).start()
+    for b in range(4):
+        gather_c(b).wait_recv()
+        gather_f(b).wait_recv()
+        gather_f(b).wait_send()
+        forward_rows(b, 0)
+    for b in range(4):
+        gather_x(b).wait_send()
+        gather_c(b).wait_send()
+    keep = local(acc.at[:, wide], s_resid, iosem.at[0])
+    keep.start()
+    keep.wait()
+
+    def clear(b, carry):
+        acc[block(b, 64), :] = jnp.zeros((64, 1152), f32)
+        return carry
+
+    lax.fori_loop(0, 16, clear, 0)
+    dk_acc[...] = jnp.zeros_like(dk_acc)
+    dv_acc[...] = jnp.zeros_like(dv_acc)
+    norms[...] = jnp.zeros_like(norms)
+
+    def expert(e):
+        s = e % 2
+        for copy in expert_load(e, s):
+            copy.wait()
+
+        @pl.when(e + 1 < EXPERTS)
+        def _():
+            for copy in expert_load(e + 1, 1 - s):
+                copy.start()
+
+        def rows_of(b, carry):
+            rows = block(b)
+            both = dot_f(hbuf[rows, :], wgu[s])
+            gate, up = both[:, :LANES], both[:, LANES:]
+            d_raw = dot_nt(rhs[0, rows, :], wdb[s, :, 0:256])
+            for col in range(1, 4):
+                d_raw = d_raw + dot_nt(rhs[col, rows, :], wdb[s, :, 256 * col : 256 * col + 256])
+            lane = lax.broadcasted_iota(jnp.int32, (ROWS, LANES), 1)
+            weight = jnp.sum(jnp.where(lane == e, slot_w[rows, :], 0.0), axis=1, keepdims=True)
+            sigma = 1.0 / (1.0 + jnp.exp(-gate))
+            silu = gate * sigma
+            hidden = silu * up
+            lhs[e, :, rows] = (hidden * weight).T.astype(bf16)
+            inner = jnp.sum(hidden * d_raw, axis=1, keepdims=True)
+            inner = jnp.where(weight > 0.0, inner, 0.0)
+            acc[rows, 1024:1152] = jnp.where(lane == e, inner, acc[rows, 1024:1152])
+            d_hidden = d_raw * weight
+            d_gate = (d_hidden * up * sigma * (1.0 + gate * (1.0 - sigma))).astype(bf16)
+            d_up = (d_hidden * silu).astype(bf16)
+            rhs[4 + e, rows, 0:LANES] = d_gate
+            rhs[4 + e, rows, LANES:] = d_up
+            acc[rows, 0:1024] += dot_nt(rhs[4 + e, rows, :], wgu[s])
+            return carry
+
+        lax.fori_loop(0, 4, rows_of, 0)
+
+    mine = pl.ds(pl.multiple_of(core * 512, 512), 512)
+    other = pl.ds(pl.multiple_of((1 - core) * 512, 512), 512)
+
+    def span(k):
+        return pl.ds(0, 1152 if k == 0 else 1024)
+
+    def sum_a(k):
+        return remote(acc.at[other, span(k)], buf1.at[:, span(k)], s1s.at[k], s1r.at[k], core_mate, "tensor")
+
+    def sum_b(k):
+        return remote(acc.at[mine, span(k)], buf2.at[:, span(k)], s2s.at[k], s2r.at[k], x_mate, "tensor")
+
+    def sum_c(k):
+        part = acc.at[mine, span(k)]
+        return remote(part, part, s3s.at[k], s3r.at[k], core_mate, "tensor")
+
+    def add_in(k, buf):
+        def step(b, carry):
+            rows = pl.ds(pl.multiple_of(core * 512 + b * 64, 64), 64)
+            acc[rows, span(k)] += buf[block(b, 64), span(k)]
+            return carry
+
+        lax.fori_loop(0, 8, step, 0)
+
+    def sum_first(k):
+        pl.semaphore_signal(ready1.at[k], inc=1, device_id={"tensor": core_mate}, device_id_type=MESH)
+        pl.semaphore_signal(ready2.at[k], inc=1, device_id={"tensor": x_mate}, device_id_type=MESH)
+        pl.semaphore_wait(ready1.at[k], 1)
+        sum_a(k).start()
+
+    def sum_second(k):
+        sum_a(k).wait_recv()
+        add_in(k, buf1)
+        sum_a(k).wait_send()
+        pl.semaphore_signal(ready3.at[k], inc=1, device_id={"tensor": core_mate}, device_id_type=MESH)
+        pl.semaphore_wait(ready2.at[k], 1)
+        sum_b(k).start()
+
+    def sum_third(k):
+        sum_b(k).wait_recv()
+        sum_b(k).wait_send()
+        add_in(k, buf2)
+        pl.semaphore_wait(ready3.at[k], 1)
+        sum_c(k).start()
+
+    def sum_last(k):
+        sum_c(k).wait_recv()
+        sum_c(k).wait_send()
+
+    def head_rows(b):
+        rows = block(b)
+        vals = [hbuf[rows, 256 * col : 256 * col + 256].astype(f32) for col in range(4)]
+        square = sum(jnp.sum(v * v, axis=1, keepdims=True) for v in vals)
+        scale_r = lax.rsqrt(square * (1.0 / 1024.0) + EPSILON)
+        for col in range(4):
+            normed = vals[col] * scale_r * gain[1:2, 256 * col : 256 * col + 256]
+            for half_c in range(2):
+                lhs[24 + 2 * col + half_c, :, rows] = normed[:, 128 * half_c : 128 * half_c + 128].T.astype(bf16)
+
+    def in_halves(b, body):
+        @pl.when(b < 2)
+        def _():
+            body(buf1, block(b))
+
+        @pl.when(b >= 2)
+        def _():
+            body(buf2, block(b - 2))
+
+    def norm_back(values, scale_r, grads, which):
+        inner = sum(
+            jnp.sum(v * scale_r * (g * gain[which : which + 1, 256 * c : 256 * c + 256]), axis=1, keepdims=True)
+            for c, (v, g) in enumerate(zip(values, grads))
+        ) * (1.0 / 1024.0)
+        outs = []
+        for c, (v, g) in enumerate(zip(values, grads)):
+            normed = v * scale_r
+            row = 4 * which + c
+            norms[row : row + 1, :] += jnp.sum(g * normed, axis=0, keepdims=True)
+            outs.append(scale_r * (g * gain[which : which + 1, 256 * c : 256 * c + 256] - normed * inner))
+        return outs
+
+    def middle_rows(b):
+        rows = block(b)
+
+        def body(buf, part):
+            values = [buf[part, 256 * c : 256 * c + 256] for c in range(4)]
+            grads = [acc[rows, 256 * c : 256 * c + 256] for c in range(4)]
+            square = sum(jnp.sum(v * v, axis=1, keepdims=True) for v in values)
+            scale_r = lax.rsqrt(square * (1.0 / 1024.0) + EPSILON)
+            back = norm_back(values, scale_r, grads, 0)
+            for c in range(4):
+                total = rhs[c, rows, :].astype(f32) + back[c]
+                acc[rows, 256 * c : 256 * c + 256] = total
+                rhs[22 + c, rows, :] = total.astype(bf16)
+            for h in range(4):
+                d_head = dot_nt(rhs[22, rows, :], wdb[h, :, 0:256])
+                for c in range(1, 4):
+                    d_head = d_head + dot_nt(rhs[22 + c, rows, :], wdb[h, :, 256 * c : 256 * c + 256])
+                da2[h, rows, :] = d_head.astype(bf16)
+
+        in_halves(b, body)
+
+    scaling = 1.0 / math.sqrt(HEAD_DIM)
+
+    def turn_back(grad, cols):
+        sine = grad * sin_t[:, cols]
+        return grad * cos_t[:, cols] + jnp.concatenate([sine[32:], -sine[:32]], axis=0)
+
+    def attend_back(h, qb):
+        keys = ROWS * (qb + 1)
+        rows = pl.ds(ROWS * qb, ROWS)
+        q_rows = q2[h, rows, :]
+        d_rows = da2[h, rows, :]
+        scores = dot_nt(k2[0:keys, :], q_rows) * scaling
+        k_pos = lax.broadcasted_iota(jnp.int32, (keys, ROWS), 0)
+        q_pos = lax.broadcasted_iota(jnp.int32, (keys, ROWS), 1) + ROWS * qb
+        allowed = (k_pos <= q_pos) & (k_pos < length[0])
+        exact = jnp.exp(jnp.where(allowed, scores, NEGATIVE) - lse[pl.ds(h, 1), rows])
+        d_probs = dot_nt(v2[0:keys, :], d_rows)
+        inner = jnp.sum(exact * d_probs, axis=0, keepdims=True)
+        d_scores = (exact * (d_probs - inner)).astype(bf16)
+        dk_acc[0:keys, :] += dot_f(d_scores, q_rows)
+        dv_acc[0:keys, :] += dot_f(exact.astype(bf16), d_rows)
+        k_head = kt2[pl.ds(pl.multiple_of((h // 2) * 64, 64), 64), 0:keys]
+        d_q = dot_f(k_head, d_scores) * scaling
+        buf2[pl.ds(pl.multiple_of(h * 64, 64), 64), rows] = turn_back(d_q, rows)
+
+    def turn_rows(b):
+        rows = block(b)
+        rhs[20, rows, :] = buf2[0:256, rows].T.astype(bf16)
+        d_k = (dk_acc[rows, :] * scaling).T
+        d_k = jnp.concatenate([turn_back(d_k[:64], rows), turn_back(d_k[64:], rows)], axis=0)
+        rhs[21, rows, 0:LANES] = d_k.T.astype(bf16)
+        rhs[21, rows, LANES:] = dv_acc[rows, :].astype(bf16)
+
+    def project_rows(b):
+        rows = block(b)
+        acc[rows, 0:1024] = dot_nt(rhs[20, rows, :], wgu[0]) + dot_nt(rhs[21, rows, :], wgu[1])
+
+    def token_rows(b):
+        rows = block(b)
+
+        def body(buf, part):
+            values = [hbuf[rows, 256 * c : 256 * c + 256].astype(f32) for c in range(4)]
+            grads = [acc[rows, 256 * c : 256 * c + 256] for c in range(4)]
+            square = sum(jnp.sum(v * v, axis=1, keepdims=True) for v in values)
+            scale_r = lax.rsqrt(square * (1.0 / 1024.0) + EPSILON)
+            back = norm_back(values, scale_r, grads, 1)
+            for c in range(4):
+                cols = slice(256 * c, 256 * c + 256)
+                hbuf[rows, cols] = (buf[part, cols] + back[c]).astype(bf16)
+
+        in_halves(b, body)
+
+    def pair_load(pair, s):
+        return local(w_down.at[pl.ds(2 * pair, 2)], wdb.at[pl.ds(2 * s, 2)], wsem.at[s, 2])
+
+    def moe_pair(pair):
+        s = pair % 2
+        pair_load(pair, s).wait()
+
+        @pl.when(pair + 1 < EXPERTS // 2)
+        def _():
+            pair_load(pair + 1, 1 - s).start()
+
+        def rows_of(b, carry):
+            rows = block(b)
+            hidden = lhs[pl.ds(2 * pair, 2), :, rows].reshape(256, ROWS)
+            down = wdb[pl.ds(2 * s, 2)].reshape(256, 1024)
+            part = dot_tn(hidden, down)
+
+            @pl.when(pair == 0)
+            def _():
+                acc[rows, 0:1024] = part
+
+            @pl.when(pair > 0)
+            def _():
+                acc[rows, 0:1024] += part
+
+            return carry
+
+        lax.fori_loop(0, 4, rows_of, 0)
+
+    def result_rows(b):
+        rows = block(b)
+
+        def body(buf, part):
+            pos = lax.broadcasted_iota(jnp.int32, (ROWS, 1024), 0) + b * ROWS
+            total = buf[part, wide] + acc[rows, 0:1024]
+            hbuf[rows, :] = jnp.where(pos < length[0], total, 0.0).astype(bf16)
+
+        in_halves(b, body)
+
+    def halves_in(src):
+        return [
+            local(src.at[pl.ds(0, 512)], buf1.at[:, wide], iosem.at[1]),
+            local(src.at[pl.ds(512, 512)], buf2.at[:, wide], iosem.at[2]),
+        ]
+
+    def start(copies):
+        for copy in copies:
+            copy.start()
+
+    def wait(copies):
+        for copy in copies:
+            copy.wait()
+
+    tokens_in = [local(x_in, hbuf, iosem.at[3])]
+    wo_load = [local(wo_in, wdb, iosem.at[4])]
+    proj_load = [local(wq_in, wgu.at[0], iosem.at[5]), local(wkv_in, wgu.at[1], iosem.at[6])]
+    dots_out = [local(acc.at[:, pl.ds(1024, LANES)], o_dots, iosem.at[7])]
+    dres_out = [local(acc.at[:, wide], s_dres, iosem.at[8])]
+    tokens_out = [local(hbuf, o_tokens, iosem.at[9])]
+    result_out = [local(hbuf, o_result, iosem.at[10])]
+
+    def do_all(*steps):
+        for step in steps:
+            step()
+
+    once = {
+        T_SUM1: lambda: do_all(lambda: sum_first(0), lambda: start(tokens_in + wo_load + proj_load)),
+        T_SUM1 + 2: lambda: do_all(lambda: sum_second(0), lambda: wait(tokens_in)),
+        T_MID1 - 3: lambda: sum_third(0),
+        T_MID1 - 1: lambda: do_all(
+            lambda: sum_last(0), lambda: start(halves_in(s_resid) + dots_out), lambda: wait(wo_load)
+        ),
+        T_ATT: lambda: do_all(lambda: wait(dots_out), lambda: start(dres_out)),
+        T_PROJ - 1: lambda: do_all(lambda: wait(dres_out), lambda: wait(proj_load)),
+        T_SUM2: lambda: sum_first(1),
+        T_SUM2 + 2: lambda: sum_second(1),
+        T_TOK - 3: lambda: sum_third(1),
+        T_TOK - 1: lambda: do_all(
+            lambda: sum_last(1), lambda: start(halves_in(s_dres)), lambda: start([pair_load(0, 0)])
+        ),
+        T_MOE: lambda: start(tokens_out),
+        T_SUM3: lambda: do_all(lambda: wait(tokens_out), lambda: sum_first(2)),
+        T_SUM3 + 2: lambda: sum_second(2),
+        T_RES - 3: lambda: sum_third(2),
+        T_RES - 1: lambda: do_all(lambda: sum_last(2), lambda: start(halves_in(s_resid))),
+        T_RES + 4: lambda: start(result_out),
+        T_RES + 8: lambda: wait(result_out),
+    }
+    halves_wait = {T_MID1: s_resid, T_TOK: s_dres, T_RES: s_resid}
+
+    def work(t):
+        for when_t, fn in sorted(once.items()):
+            pl.when(t == when_t)(fn)
+        for when_t, src in halves_wait.items():
+            pl.when(t == when_t)(lambda src=src: wait(halves_in(src)))
+        for begin, count, fn in (
+            (0, EXPERTS, expert),
+            (T_HEAD, 4, head_rows),
+            (T_MID1, 4, middle_rows),
+            (T_TURN, 4, turn_rows),
+            (T_PROJ, 4, project_rows),
+            (T_TOK, 4, token_rows),
+            (T_MOE, EXPERTS // 2, moe_pair),
+            (T_RES, 4, result_rows),
+        ):
+            pl.when((t >= begin) & (t < begin + count))(lambda fn=fn, begin=begin: fn(t - begin))
+        for qb in range(4):
+            u = t - T_ATT
+            pl.when((u >= 0) & (u < 16) & (u % 4 == qb))(lambda qb=qb, u=u: attend_back(u // 4, qb))
 
     own = pl.ds(pl.multiple_of(y * 64, 64), 64)
     oth = pl.ds(pl.multiple_of((1 - y) * 64, 64), 64)
@@ -209,7 +604,6 @@
     def stage(c, t):
         p = z if c == 0 else last - z
         nxt, prv = (up_id, dn_id) if c == 0 else (dn_id, up_id)
-
         def at(delay, body):
             i = t - delay
 
@@ -249,7 +643,13 @@
             r_att = jnp.where(a < 16, 20 + a // 8, 22 + (a - 16) % 4)
             li = jnp.where(in_moe, l_moe, l_att)
             ri = jnp.where(in_moe, r_moe, r_att)
-            pbuf[c, s] = jnp.dot(lhs[li], rhs[ri], preferred_element_type=jnp.float32)
+            @pl.when(i < N_CLASS - 1)
+            def _():
+                pbuf[c, s] = dot_f(lhs[jnp.minimum(li, 33)], rhs[jnp.minimum(ri, 25)])
+
+            @pl.when(i == N_CLASS - 1)
+            def _():
+                pbuf[c, s] = norms[...]
 
             @pl.when(is_a)
             def _():
@@ -362,7 +762,11 @@
                 rows = pl.ds(pl.multiple_of((a - 8) * 128, 128), 128)
                 store(s, o_k.at[rows], o_v.at[rows])
 
-            @pl.when(a >= 16)
+            @pl.when(i == N_CLASS - 1)
+            def _():
+                store(s, o_norm.at[c, :, pl.ds(0, 128)], o_norm.at[c, :, pl.ds(128, 128)])
+
+            @pl.when((a >= 16) & (a < 24))
             def _():
                 b = a - 16
                 rows = pl.ds(pl.multiple_of((b // 4) * 128, 128), 128)
@@ -410,6 +814,8 @@
     def body(t, carry):
         both = [stage(0, t), stage(1, t)]
         for k in (1, 2, 3, 4, 5, 0):
+            if k == 0:
+                work(t)
             for st in both:
                 delay, fn, at = st[k]
                 at(delay, fn)
@@ -419,29 +825,59 @@
     lax.fori_loop(0, total, body, 0)
 
 
-def dp_reduce(mesh, WhT, dout, hT, dgu, haT, dq, dkv, acT, drb, hop=HOP):
+def run_layer(mesh, *operands):
     groups = mesh.shape["dp"]
     nz = 4 if groups % 8 == 0 else groups // 2
     last = nz - 1
+    hop = HOP
     ring = hop * (2 * last + 4) + 2
     ring += ring % 2
-    sh = jax.ShapeDtypeStruct
-    f32 = jnp.float32
-    outs = [sh((16, 1024, 128), f32)] * 2 + [sh((16, 128, 1024), f32), sh((1024, 256), f32), sh((1024, 128), f32), sh((1024, 128), f32), sh((256, 1024), f32)]
-    anyspec = pl.BlockSpec(memory_space=pl.ANY)
-    sem = pltpu.SemaphoreType.DMA
-    sums = pl.pallas_call(
-        functools.partial(dp_kernel, nz, hop, ring),
-        out_shape=outs, in_specs=[anyspec] * 9, out_specs=[anyspec] * 7,
-        scratch_shapes=[pltpu.VMEM((34, 128, 1024), jnp.bfloat16), pltpu.VMEM((26, 1024, 256), jnp.bfloat16),
-                        pltpu.VMEM((2, ring, 128, 256), f32), pltpu.VMEM((2, ring, 128, 256), f32), pltpu.VMEM((2, ring, 128, 256), f32),
-                        sem((60,))] + [sem((2, ring))] * 10,
-        compiler_params=pltpu.CompilerParams(collective_id=0, has_side_effects=True, vmem_limit_bytes=58 * 2**20),
-    )(WhT, dout, hT, dgu, haT, dq, dkv, acT, drb)
+    f32, bf16 = jnp.float32, jnp.bfloat16
+
+    def out(shape, kind=f32):
+        return jax.ShapeDtypeStruct(shape, kind)
+
+    outs = [
+        out((16, 1024, 128)), out((16, 1024, 128)), out((16, 128, 1024)),
+        out((1024, 256)), out((1024, 128)), out((1024, 128)), out((256, 1024)), out((2, 128, 256)),
+        out((1024, 1024), bf16), out((1024, 1024), bf16), out((1024, 128)),
+        out((1024, 1024)), out((1024, 1024)),
+    ]
+    anywhere = pl.BlockSpec(memory_space=pl.ANY)
+    dma = pltpu.SemaphoreType.DMA
+    reg = pltpu.SemaphoreType.REGULAR
+    vmem = pltpu.VMEM
+    res = pl.pallas_call(
+        functools.partial(layer_kernel, nz, hop, ring),
+        out_shape=outs,
+        in_specs=[pl.BlockSpec(memory_space=pltpu.SMEM)] + [anywhere] * (len(operands) - 1),
+        out_specs=[anywhere] * len(outs),
+        scratch_shapes=[
+            vmem((34, 128, 1024), bf16), vmem((26, 1024, 256), bf16),
+            vmem((2, ring, 128, 256), f32), vmem((2, ring, 128, 256), f32), vmem((2, ring, 128, 256), f32),
+            vmem((1024, 1152), f32), vmem((512, 1152), f32), vmem((512, 1152), f32),
+            vmem((1024, 1024), bf16), vmem((2, 1024, 256), bf16), vmem((4, 128, 1024), bf16),
+            vmem((4, 1024, 128), bf16), vmem((1024, 128), bf16), vmem((1024, 128), bf16), vmem((128, 1024), bf16),
+            vmem((8, 1024), f32), vmem((64, 1024), f32), vmem((64, 1024), f32),
+            vmem((4, 1024, 128), bf16), vmem((1024, 128), f32), vmem((1024, 128), f32),
+            vmem((1024, 128), f32), vmem((8, 1024), f32), vmem((128, 256), f32),
+            dma((17,)), dma((2, 3)), dma((11,)),
+        ]
+        + [dma((2, ring))] * 10
+        + [dma((4,))] * 6
+        + [dma((3,))] * 6
+        + [reg((3,))] * 3,
+        compiler_params=pltpu.CompilerParams(
+            collective_id=0, has_side_effects=True, vmem_limit_bytes=62 * 2**20
+        ),
+    )(*operands)
+    sums, rest = tuple(res[:8]), res[8:11]
     if groups > 2 * nz:
-        same = [[2 * nz * block + place for block in range(groups // (2 * nz))] for place in range(2 * nz)]
-        sums = lax.psum(tuple(sums), "dp", axis_index_groups=same)
-    return sums
+        same = [
+            [2 * nz * block + place for block in range(groups // (2 * nz))] for place in range(2 * nz)
+        ]
+        sums = lax.psum(sums, "dp", axis_index_groups=same)
+    return sums, rest
 
 
 def per_device(
@@ -469,8 +905,8 @@
     kv_here = w_key.shape[1] // HEAD_DIM
     scaling = 1.0 / math.sqrt(HEAD_DIM)
     valid = (jnp.arange(seq_len, dtype=jnp.int32)[None, :] < lengths[:, None]).reshape(-1)
-    valid_f = valid.astype(jnp.float32)[:, None]
     cosine, sine = rope_tables(seq_len, HEAD_DIM)
+    w_out_all = lax.all_gather(w_out.astype(jnp.float32), "tensor", axis=0, tiled=True)
     x_in = tokens.astype(jnp.float32)
     h_attn = rms_norm(x_in, norm_attn).astype(jnp.bfloat16)
     q_lin = dot_f(h_attn, w_query).reshape(seq_count, seq_len, heads_here, HEAD_DIM)
@@ -482,83 +918,53 @@
     k_rot = rotate(k_lin, cosine, sine).astype(jnp.bfloat16)
     attended, lse_all = attend_forward(q_rot, k_rot, v_att, lengths, scaling)
     attn_cat = attended.reshape(tok_rows, heads_here * HEAD_DIM).astype(jnp.bfloat16)
-    attn_sum = lax.psum(dot_f(attn_cat, w_out), "tensor")
-    resid = x_in + attn_sum
-    h_moe = rms_norm(resid, norm_moe).astype(jnp.bfloat16)
-    weights, kept, onehot_f = route_weights(valid, chosen, gate_values)
-    d_out = cotangent.astype(jnp.float32) * valid_f
-    gate_act = jnp.einsum("td,edf->tef", h_moe, w_gate, preferred_element_type=jnp.float32)
-    up_act = jnp.einsum("td,edf->tef", h_moe, w_up, preferred_element_type=jnp.float32)
-    d_raw = jnp.einsum("td,efd->tef", cotangent, w_down, preferred_element_type=jnp.float32)
-    sigma = jax.nn.sigmoid(gate_act)
-    silu_g = gate_act * sigma
-    hidden = silu_g * up_act
-    hidden_w = (hidden * weights[:, :, None]).astype(jnp.bfloat16)
-    gate_dot = jnp.sum(hidden * d_raw, axis=-1) * kept
-    d_gate_part = jnp.sum(onehot_f * gate_dot[:, None, :], axis=-1)
-    d_hidden = d_raw * weights[:, :, None]
-    d_gate_b = (d_hidden * up_act * sigma * (1.0 + gate_act * (1.0 - sigma))).astype(jnp.bfloat16)
-    d_up_b = (d_hidden * silu_g).astype(jnp.bfloat16)
-    moe_part = jnp.einsum("tef,efd->td", hidden_w, w_down, preferred_element_type=jnp.float32)
-    moe_sum = lax.psum(moe_part, "tensor")
-    result = ((resid + moe_sum) * valid_f).astype(jnp.bfloat16)
-    d_h_part = jnp.einsum("tef,edf->td", d_gate_b, w_gate, preferred_element_type=jnp.float32)
-    d_h_part = d_h_part + jnp.einsum(
-        "tef,edf->td", d_up_b, w_up, preferred_element_type=jnp.float32
+    weights, onehot_f = route_weights(valid, chosen, gate_values)
+    d_out = jnp.where(valid[:, None], cotangent, 0)
+    q_heads = q_rot.reshape(tok_rows, heads_here, HEAD_DIM).transpose(1, 0, 2)
+    q_pad = jnp.concatenate(
+        [jnp.pad(q_heads[:2], ((0, 0), (0, 0), (0, 64))), jnp.pad(q_heads[2:], ((0, 0), (0, 0), (64, 0)))]
     )
-    d_h_moe, d_gates = lax.psum((d_h_part, d_gate_part), "tensor")
-    unused_m, pull_moe = jax.vjp(rms_norm, resid, norm_moe)
-    d_resid_n, grad_norm_moe = pull_moe(d_h_moe)
-    d_resid = d_out + d_resid_n
-    d_resid_b = d_resid.astype(jnp.bfloat16)
-    d_attn = jnp.einsum("td,fd->tf", d_resid_b, w_out, preferred_element_type=jnp.float32).astype(
-        jnp.bfloat16
+    wo_heads = w_out.reshape(heads_here, HEAD_DIM, width)
+    wo_pad = jnp.concatenate(
+        [jnp.pad(wo_heads[:2], ((0, 0), (0, 64), (0, 0))), jnp.pad(wo_heads[2:], ((0, 0), (64, 0), (0, 0)))]
     )
-    d_attn = d_attn.reshape(seq_count, seq_len, heads_here, HEAD_DIM)
-    d_q_rot, d_k_rot, d_v_all = attend_backward(
-        q_rot, k_rot, v_att, d_attn, lse_all, lengths, scaling
+    k_flat = k_rot.reshape(tok_rows, -1)
+    lse_rows = lse_all[0].reshape(-1, heads_here, min(512, seq_len)).transpose(1, 0, 2).reshape(heads_here, tok_rows)
+    sums, (result, grad_tokens, dots) = run_layer(
+        mesh,
+        lengths,
+        attn_cat.astype(jnp.float32),
+        w_out_all,
+        tokens,
+        d_out,
+        jnp.pad(weights, ((0, 0), (0, 128 - EXPERTS))),
+        jnp.pad(jnp.stack([norm_moe, norm_attn]), ((0, 6), (0, 0))),
+        w_gate,
+        w_up,
+        w_down,
+        q_pad,
+        k_flat,
+        v_att.reshape(tok_rows, -1),
+        k_flat.T,
+        jnp.pad(lse_rows, ((0, 8 - heads_here), (0, 0))),
+        cosine.T,
+        sine.T,
+        wo_pad,
+        w_query,
+        jnp.concatenate([w_key, w_value], axis=1),
     )
-    unused_q, pull_query = jax.vjp(lambda values: rotate(values, cosine, sine), q_lin)
-    unused_k, pull_key = jax.vjp(lambda values: rotate(values, cosine, sine), k_lin)
-    d_query = pull_query(d_q_rot)[0].astype(jnp.bfloat16).reshape(tok_rows, -1)
-    d_key = pull_key(d_k_rot)[0].astype(jnp.bfloat16).reshape(tok_rows, -1)
-    d_value = d_v_all.astype(jnp.bfloat16).reshape(tok_rows, -1)
-    d_h_part_a = jnp.einsum("tf,df->td", d_query, w_query, preferred_element_type=jnp.float32)
-    d_h_part_a = d_h_part_a + jnp.einsum(
-        "tf,df->td", d_key, w_key, preferred_element_type=jnp.float32
-    )
-    d_h_part_a = d_h_part_a + jnp.einsum(
-        "tf,df->td", d_value, w_value, preferred_element_type=jnp.float32
-    )
-    d_h_attn = lax.psum(d_h_part_a, "tensor")
-    unused_a, pull_attn = jax.vjp(rms_norm, x_in, norm_attn)
-    d_x_n, grad_norm_attn = pull_attn(d_h_attn)
-    grad_tokens = (d_resid + d_x_n).astype(jnp.bfloat16)
-    grad_norm_attn, grad_norm_moe = lax.psum((grad_norm_attn, grad_norm_moe), "dp")
-    hidden_t = hidden_w.reshape(tok_rows, -1).T
-    d_gate_up = jnp.concatenate([d_gate_b, d_up_b], axis=2).transpose(1, 0, 2)
-    grad_gate, grad_up, grad_down, grad_query, grad_key, grad_value, grad_out = dp_reduce(
-        mesh,
-        hidden_t,
-        cotangent,
-        h_moe.T,
-        d_gate_up,
-        h_attn.T,
-        d_query,
-        jnp.concatenate([d_key, d_value], axis=1),
-        attn_cat.T,
-        d_resid_b,
-    )
+    grad_gate, grad_up, grad_down, grad_query, grad_key, grad_value, grad_out, norm_rows = sums
+    d_gates = jnp.sum(onehot_f * dots[:, None, :EXPERTS], axis=-1)
     return (
         result,
         grad_tokens,
         d_gates,
-        grad_norm_attn,
+        norm_rows[0, 4:8].reshape(-1),
         grad_query,
         grad_key,
         grad_value,
         grad_out,
-        grad_norm_moe,
+        norm_rows[0, 0:4].reshape(-1),
         grad_gate,
         grad_up,
         grad_down,

time: 1040 us -> 647 us (0.62)
  waiting for transfers between devices: 261 us -> 0.02 us
  matrix products: 76.6 us -> 21 us
  Pallas kernels: 490 us -> 539 us
  other arithmetic: 70.7 us -> 22.8 us
  local copies, waits for them, and re-layouts: 83.2 us -> 47.6 us
  blocking collectives: 34.6 us -> 0 us
    psum x3 -> x0, waiting for transfers between devices: 261 us -> none  [the longest x1 114 us: per_device(): moe_sum = lax.psum(moe_part, 'tensor')]
    pallas_call x1, Pallas kernels: 490 us -> 539 us  [run_layer(): pl.pallas_call(functools.partial(layer_kernel, nz, hop, ring), out_shape=...]
    dot_general x16 -> x0, matrix products: 45.6 us -> none  [the longest x1 12.7 us: per_device(): jnp.einsum('td,efd->tef', cotangent, w_down, preferred_element_type=jnp.f...]
    psum x2 -> x0, blocking collectives: 34.6 us -> none  [the longest x1 21.8 us: per_device(): lax.psum((grad_norm_attn, grad_norm_moe), 'dp')]
    convert_element_type x7 -> x2, other arithmetic: 34 us -> 3.32 us  [the longest x1 2.28 us: per_device(): w_out.astype(jnp.float32)]
    unnamed x151 -> x89, local copies, waits for them, and re-layouts: 48 us -> 28.6 us
    unnamed x2 -> x0, matrix products: 18.5 us -> none
    dot_general x2 -> x0, local copies, waits for them, and re-layouts: 18.5 us -> none  [the longest x1 9.23 us: per_device(): jnp.einsum('td,edf->tef', h_moe, w_up, preferred_element_type=jnp.float32)]
  transfers between devices with their start and end apart: 3 -> 1, of which waited for: 3 -> 0; matrix products, arithmetic and copies ran while one was open for 5% -> 9% of each run, Pallas kernels for 0% -> 0%
where the time goes in v3:
time: 647 us; the launch traced here: 646 us
  Pallas kernels  539 us (83%)
  local copies, waits for them, and re-layouts  47.6 us (7%)
  other arithmetic  22.8 us (4%)
  matrix products  21 us (3%)
  between operations  15.8 us (2%)
    pallas_call x1, Pallas kernels, run_layer(): pl.pallas_call(functools.partial(layer_kernel, nz, hop, ring), out_shape=...  539 us
    unnamed x89, local copies, waits for them, and re-layouts  28.6 us
  transfers between devices with their start and end apart: 1, of which 0 were waited for; matrix products, arithmetic and copies ran while one was open for 9% of the time, Pallas kernels for 0%

profile of v3, /device:TPU:0, one launch (start us, length us, event | category | flops | bytes accessed | tf_op | source)
XLA Modules:
  0.0 646.1 jit_solution(7149611515583292047)
XLA Ops:
  7.3 2.3 convert_element_type.100
  10.1 0.9 fusion.48
  11.1 1.0 copy.70
  12.7 1.0 copy.66
  15.1 1.5 convolution_convert_fusion.v_in
  16.5 1.9 fusion.61
  18.4 1.9 fusion.59
  20.3 1.0 fusion.67
  21.3 2.1 copy.67
  23.4 2.8 fusion.58
  27.0 0.9 fusion.65
  27.9 1.0 fusion.8
  28.9 2.0 copy-done.1
  30.9 0.9 fusion.7
  33.9 0.9 copy.73
  35.5 1.0 copy.78
  36.5 1.0 copy.80
  37.7 0.8 copy.84.k_in
  38.5 1.8 copy.82
  40.4 1.3 add.114
  41.7 3.5 fusion.20
  45.8 3.3 fusion.1
  49.1 1.8 fusion
  51.0 1.5 copy-done
  52.6 5.6 fusion.19
  58.2 1.9 copy.77
  60.1 2.3 fusion.24
  62.4 0.8 pad.28.w_slot
  64.5 1.9 pad_maximum_fusion.1.wkv_in
  66.4 1.1 fusion.66
  67.5 1.1 fusion.25.wo_in
  68.6 0.9 fusion.27
  69.6 1.3 fusion.26.q_in
  70.9 1.0 maximum_convert_fusion.cat_in
  71.9 1.5 broadcast_select_fusion.d_out
  73.5 538.9 %shard_map.229 = (f32[16,1024,128]{2,1,0:T(8,128)}, f32[16,1024,128]{2,1,0:T(8,128)}, f32[16,128,1024]{2,1,0:T(8,128)}, f32[1024,256]{1,0:T(8,128)}, f32[1024,12...) custom-call(s32[1]{0:T(128)} %copy.108.length, ...), custom_call_target="tpu_custom_call" | custom-call | tf_op jit(solution)/shard_map/pallas_call | solution.py:850
  614.3 1.2 copy.85
  616.3 3.2 copy.109
  619.5 1.3 copy.110
  620.8 1.0 copy.111
  621.8 0.8 copy.112
  622.6 0.8 copy.113
  623.4 1.0 copy.114
  624.4 4.3 copy.115
  628.7 1.6 slice-done.3
  630.3 4.3 copy.116
  634.5 1.3 slice-done.1
  635.9 3.4 copy.117
  (110 shorter events, 9.7 us)
Async XLA Ops:
  7.2 7.2 %copy-start.2 = (bf16[1024,1024]{1,0:T(8,128)(2,1)S(1)}, bf16[1024,1024]{1,0:T(8,128)(2,1)}, u32[]{:S(2)}) copy-start(bf16[1024,1024]{1,0:T(8,128)(2,1)} %x_in.1) | copy-start | bytes 6291460
  7.2 7.8 %copy-start.31 = (f32[1024]{0:T(1024)S(1)}, f32[1024]{0:T(1024)}, u32[]{:S(2)}) copy-start(f32[1024]{0:T(1024)} %param.19) | copy-start | bytes 12292
  7.2 7.8 %copy-start.25 = (bf16[1024,128]{1,0:T(8,128)(2,1)S(1)}, bf16[1024,128]{1,0:T(8,128)(2,1)}, u32[]{:S(2)}) copy-start(bf16[1024,128]{1,0:T(8,128)(2,1)} %param.22) | copy-start | bytes 786436
  7.2 66.3 %all-gather.2.cloned.1.call-start = ((), (), s32[]{:S(2)}) async-start(), calls=%async_computation | async-start | bytes 5242880 | tf_op jit(solution)/shard_map/all_gather | solution.py:909
  15.1 3.3 copy-start.21
  18.4 19.2 %copy-start.6 = (f32[1024,128]{0,1:T(8,128)}, f32[1024,128]{0,1:T(8,128)S(1)}, u32[]{:S(2)}) copy-start(f32[1024,128]{0,1:T(8,128)S(1)} %fusion.61) | copy-start | bytes 1572868
  23.4 2.9 copy-start.7
  23.4 2.9 copy-start.9
  26.3 1.6 copy-start.12
  26.3 1.6 copy-start.13
  26.3 1.6 copy-start.17
  27.9 4.6 copy-start.27
  27.9 4.6 copy-start.30
  28.9 2.0 copy-start.1
  28.9 5.0 copy-start.16
  28.9 5.8 slice-start.4
  35.5 6.2 copy-start.26
  37.7 7.5 %copy-start.11 = (bf16[1024,128]{0,1:T(8,128)(2,1)}, bf16[1024,128]{0,1:T(8,128)(2,1)S(1)}, u32[]{:S(2)}) copy-start(bf16[1024,128]{0,1:T(8,128)(2,1)S(1)} %fusion.32) | copy-start | bytes 786436
  49.1 3.4 copy-start
  49.1 3.4 copy-start.29
  49.1 3.5 copy-start.24
  58.2 5.7 copy-start.32
  58.2 5.7 copy-start.33
  58.2 10.4 %copy-start.8 = (f32[1024,64]{1,0:T(8,128)S(1)}, f32[1024,64]{1,0:T(8,128)}, u32[]{:S(2)}) copy-start(f32[1024,64]{1,0:T(8,128)} %copy.70) | copy-start | bytes 786436
  58.2 10.4 %copy-start.10 = (f32[1024,64]{1,0:T(8,128)S(1)}, f32[1024,64]{1,0:T(8,128)}, u32[]{:S(2)}) copy-start(f32[1024,64]{1,0:T(8,128)} %copy.66) | copy-start | bytes 786436
  60.1 8.5 %copy-start.4 = (f32[1024,4,32]{2,0,1:T(8,128)S(1)}, f32[1024,4,32]{2,0,1:T(8,128)}, u32[]{:S(2)}) copy-start(f32[1024,4,32]{2,0,1:T(8,128)} %get-tuple-element.57) | copy-start | bytes 1572868
  60.1 8.5 %copy-start.5 = (f32[1024,4,32]{2,0,1:T(8,128)S(1)}, f32[1024,4,32]{2,0,1:T(8,128)}, u32[]{:S(2)}) copy-start(f32[1024,4,32]{2,0,1:T(8,128)} %get-tuple-element.58) | copy-start | bytes 1572868
  69.5 1.4 copy-start.20
  69.5 2.4 copy-start.14
  73.5 542.1 %copy-start.28 = (s32[1024,8]{0,1:T(8,128)S(1)}, s32[1024,8]{0,1:T(8,128)}, u32[]{:S(2)}) copy-start(s32[1024,8]{0,1:T(8,128)} %param.16) | copy-start | bytes 98308
  615.5 4.0 copy-start.15
  616.3 4.6 copy-start.19
  616.3 5.5 copy-start.23
  616.3 6.3 copy-start.22
  616.3 7.1 %copy-start.18 = (f32[256,1024]{1,0:T(8,128)S(1)}, f32[256,1024]{1,0:T(8,128)}, u32[]{:S(2)}) copy-start(f32[256,1024]{1,0:T(8,128)} %get-tuple-element.104) | copy-start | bytes 3145732
  619.5 4.9 copy-start.3
  622.6 6.1 slice-start.2
  624.4 5.9 slice-start.3
  624.4 10.1 %slice-start = ((s8[8388608]{0:T(1024)(128)(4,1)}), s8[4194304]{0:T(1024)(128)(4,1)S(1)}, s32[]{:S(2)}) async-start(s8[8388608]{0:T(1024)(128)(4,1)} %bitcast.113), calls=%async_computation.1 | async-start | bytes 8388608
  630.3 5.6 slice-start.1
Sparse Core Ops, SparseCore 0:
  10.2 37.1 all-gather.1

commit v4 on v3

--- a/solution.py
+++ b/solution.py
@@ -3,6 +3,7 @@
 
 import jax
 import jax.numpy as jnp
+import numpy as np
 from jax import lax
 from jax.experimental import pallas as pl
 from jax.experimental.pallas import tpu as pltpu
@@ -24,93 +25,17 @@
     return jnp.dot(left, right, preferred_element_type=jnp.float32)
 
 
-def rms_norm(values, gain):
-    return values * lax.rsqrt(jnp.mean(values * values, axis=-1, keepdims=True) + EPSILON) * gain
-
-
 def rope_tables(positions, width):
     half_w = width // 2
-    freqs = THETA ** (-jnp.arange(half_w, dtype=jnp.float32) * 2.0 / width)
-    angles = jnp.arange(positions, dtype=jnp.float32)[:, None] * freqs[None, :]
-    cosine = jnp.concatenate([jnp.cos(angles), jnp.cos(angles)], axis=1)
-    sine = jnp.concatenate([jnp.sin(angles), jnp.sin(angles)], axis=1)
-    return (cosine, sine)
-
-
-def rotate(values, cosine, sine):
-    half_w = values.shape[-1] // 2
-    turned = jnp.concatenate([-values[..., half_w:], values[..., :half_w]], axis=-1)
-    return values * cosine[:, None, :] + turned * sine[:, None, :]
-
-
-def route_weights(valid, chosen, gate_values):
-    tok_rows = chosen.shape[0]
-    live_int = valid.astype(jnp.int32)
-    onehot = chosen[:, :, None] == jnp.arange(EXPERTS, dtype=jnp.int32)[None, None, :]
-    onehot_f = onehot.astype(jnp.float32)
-    hits = jnp.sum(onehot_f, axis=1) * valid.astype(jnp.float32)[:, None]
-    earlier = (
-        jnp.arange(tok_rows, dtype=jnp.int32)[None, :] < jnp.arange(tok_rows, dtype=jnp.int32)[:, None]
-    ).astype(jnp.bfloat16)
-    places = dot_f(earlier, hits.astype(jnp.bfloat16))
-    pairs = jnp.sum(live_int) * TOP_K
-    limit = ((5 * pairs + 4 * EXPERTS - 1) // (4 * EXPERTS)).astype(jnp.float32)
-    kept = jnp.where((places < limit) & (hits > 0), 1.0, 0.0)
-    weights = jnp.sum(onehot_f * gate_values[:, :, None], axis=1) * kept
-    return (weights, onehot_f)
-
-
-def block_scores(q_block, start, k_seq, length, scaling):
-    rows_q = q_block.shape[0]
-    kv_here = k_seq.shape[1]
-    grouped = q_block.reshape(rows_q, kv_here, q_block.shape[1] // kv_here, q_block.shape[2])
-    scores = (
-        jnp.einsum("qkgd,skd->kgqs", grouped, k_seq, preferred_element_type=jnp.float32) * scaling
-    )
-    q_pos = start + jnp.arange(rows_q, dtype=jnp.int32)
-    k_pos = jnp.arange(k_seq.shape[0], dtype=jnp.int32)
-    allowed = (k_pos[None, :] <= q_pos[:, None]) & (k_pos[None, :] < length)
-    return (jnp.where(allowed, scores, NEGATIVE), grouped)
-
-
-def forward_block(q_block, start, k_seq, v_seq, length, scaling):
-    scores, grouped = block_scores(q_block, start, k_seq, length, scaling)
-    top_s = jnp.max(scores, axis=-1, keepdims=True)
-    expo = jnp.exp(scores - top_s)
-    total = jnp.sum(expo, axis=-1, keepdims=True)
-    probs = (expo / total).astype(jnp.bfloat16)
-    lse_part = (top_s + jnp.log(total))[..., 0]
-    out_b = jnp.einsum("kgqs,skd->qkgd", probs, v_seq, preferred_element_type=jnp.float32)
-    return (out_b.reshape(q_block.shape[0], -1), lse_part)
-
-
-def attend_forward(q_all, k_all, v_all, lengths, scaling):
-    seq_len = q_all.shape[1]
-    q_rows = min(512, seq_len)
-    n_blocks = seq_len // q_rows
-
-    def one_sequence(item):
-        q_seq, k_seq, v_seq, length = item
-        outs = []
-        lses = []
-        for block in range(n_blocks):
-            start = block * q_rows
-            finish = start + q_rows
-            out_b, lse_b = forward_block(
-                q_seq[start:finish], start, k_seq[:finish], v_seq[:finish], length, scaling
-            )
-            outs.append(out_b)
-            lses.append(lse_b)
-        return (jnp.concatenate(outs, axis=0), jnp.stack(lses, axis=0))
-
-    return lax.map(one_sequence, (q_all, k_all, v_all, lengths))
+    freqs = THETA ** (-np.arange(half_w, dtype=np.float64) * 2.0 / width)
+    angles = np.concatenate([freqs, freqs])[:, None] * np.arange(positions, dtype=np.float64)[None, :]
+    return (np.cos(angles).astype(np.float32), np.sin(angles).astype(np.float32))
 
 
 LANES = 128
 ROWS = 256
 N_CLASS = 109
 HOP = 2
-T_HEAD = 19
 T_SUM1 = 16
 T_MID1 = 33
 T_ATT = 37
@@ -137,13 +62,13 @@
 
 def layer_kernel(
     nz, hop, ring,
-    length, cat_in, w_full, x_in, d_out, w_slot, gains, w_gate, w_up, w_down,
-    q_in, k_in, v_in, kt_in, lse_in, cos_in, sin_in, wo_in, wq_in, wkv_in,
+    length, x_in, d_out, chosen, gates, gain_attn, gain_moe, w_gate, w_up, w_down,
+    cos_in, sin_in, w_out, w_query, w_key, w_value,
     o_gate, o_up, o_down, o_q, o_k, o_v, o_out, o_norm, o_result, o_tokens, o_dots, s_resid, s_dres,
-    lhs, rhs, pbuf, zbuf, ybuf, acc, buf1, buf2, hbuf, wgu, wdb, q2, k2, v2, kt2, lse, cos_t, sin_t,
-    da2, dk_acc, dv_acc, slot_w, gain, norms,
+    lhs, rhs, pbuf, zbuf, ybuf, acc, buf, hbuf, wgu, wdb, q2, k2, v2, kt2, vt2, lse, cos_t, sin_t,
+    da2, dk_acc, dv_acc, slot_w, gain, norms, picks, pick_w,
     ld, wsem, iosem, ys, yr, zs, zr, fs, fr, gs, gr, os0, os1,
-    cs_c, cr_c, cs_x, cr_x, cs_f, cr_f, s1s, s1r, s2s, s2r, s3s, s3r, ready1, ready2, ready3,
+    cs_c, cr_c, cs_x, cr_x, cs_f, cr_f, ws, wr, s1s, s1r, s2s, s2r, s3s, s3r, ready1, ready2, ready3,
 ):
     f32, bf16 = jnp.float32, jnp.bfloat16
     dp = lax.axis_index("dp")
@@ -183,24 +108,23 @@
         pl.semaphore_signal(bar, inc=1, device_id={"dp": dn_id}, device_id_type=MESH)
 
     wide = pl.ds(0, 1024)
-    loads = [
-        local(w_full.at[pl.ds(0, 512)], buf1.at[:, wide], ld.at[0]),
-        local(w_full.at[pl.ds(512, 512)], buf2.at[:, wide], ld.at[1]),
-        local(x_in, hbuf, ld.at[2]),
-        local(gains, gain, ld.at[3]),
-        local(w_slot, slot_w, ld.at[4]),
-        local(d_out.at[:, pl.ds(0, 256)], rhs.at[0], ld.at[5]),
-        local(d_out.at[:, pl.ds(256, 256)], rhs.at[1], ld.at[6]),
-        local(d_out.at[:, pl.ds(512, 256)], rhs.at[2], ld.at[7]),
-        local(d_out.at[:, pl.ds(768, 256)], rhs.at[3], ld.at[8]),
-        local(cat_in, acc.at[:, block(tensor)], ld.at[9]),
-        local(q_in, q2, ld.at[10]),
-        local(k_in, k2, ld.at[11]),
-        local(v_in, v2, ld.at[12]),
-        local(kt_in, kt2, ld.at[13]),
-        local(lse_in, lse, ld.at[14]),
-        local(cos_in, cos_t, ld.at[15]),
-        local(sin_in, sin_t, ld.at[16]),
+    share = block(tensor)
+    token_load = [
+        local(x_in, hbuf, ld.at[0]),
+        local(gain_attn, gain.at[pl.ds(1, 1)], ld.at[1]),
+        local(gain_moe, gain.at[pl.ds(0, 1)], ld.at[2]),
+        local(cos_in, cos_t, ld.at[3]),
+        local(sin_in, sin_t, ld.at[4]),
+    ]
+    proj_load = [
+        local(w_query, wgu.at[0], ld.at[5]),
+        local(w_key, wgu.at[1, :, pl.ds(0, LANES)], ld.at[6]),
+        local(w_value, wgu.at[1, :, pl.ds(LANES, LANES)], ld.at[7]),
+    ]
+    out_load = [local(w_out.at[:, block(c)], rhs.at[22 + c, share], ld.at[8 + c]) for c in range(4)]
+    late_load = [local(d_out.at[:, block(c)], rhs.at[c], ld.at[12 + c]) for c in range(4)] + [
+        local(chosen, picks, ld.at[16]),
+        local(gates, pick_w, ld.at[17]),
     ]
 
     def expert_load(e, s):
@@ -210,42 +134,157 @@
             local(w_down.at[e], wdb.at[s], wsem.at[s, 2]),
         ]
 
-    for copy in loads:
-        copy.start()
-    for copy in expert_load(0, 0):
-        copy.start()
+    def start(copies):
+        for copy in copies:
+            copy.start()
+
+    def wait(copies):
+        for copy in copies:
+            copy.wait()
+
+    start(out_load + token_load + proj_load + late_load)
     pl.semaphore_wait(bar, 3 + (z < last).astype(jnp.int32) + (z > 0).astype(jnp.int32))
+
+    part_w = buf.at[share, wide]
+    w_x = remote(part_w, part_w, ws.at[0], wr.at[0], x_mate, "tensor")
+    w_c = remote(part_w, part_w, ws.at[1], wr.at[1], core_mate, "tensor")
+    part_f = buf.at[block(x_mate), wide]
+    w_f = remote(part_f, part_f, ws.at[2], wr.at[2], core_mate, "tensor")
+    wait(out_load)
+    for c in range(4):
+        buf[share, 256 * c : 256 * c + 256] = rhs[22 + c, share, :].astype(f32)
+    w_x.start()
+    w_c.start()
 
     def gather_x(b):
         return remote(
-            cat_in.at[block(b)], acc.at[block(b), block(tensor)], cs_x.at[b], cr_x.at[b], x_mate, "tensor"
+            acc.at[block(b), share], acc.at[block(b), share], cs_x.at[b], cr_x.at[b], x_mate, "tensor"
         )
 
     def gather_c(b):
         return remote(
-            cat_in.at[block(b)], acc.at[block(b), block(tensor)], cs_c.at[b], cr_c.at[b], core_mate, "tensor"
+            acc.at[block(b), share], acc.at[block(b), share], cs_c.at[b], cr_c.at[b], core_mate, "tensor"
         )
 
     def gather_f(b):
         part = acc.at[block(b), block(x_mate)]
         return remote(part, part, cs_f.at[b], cr_f.at[b], core_mate, "tensor")
 
-    for b in range(4):
-        gather_x(b).start()
-    for b in range(4):
-        gather_c(b).start()
-    for copy in loads:
-        copy.wait()
+    def rotate_t(values, cols):
+        turned = jnp.concatenate([-values[32:], values[:32]], axis=0)
+        return values * cos_t[:, cols] + turned * sin_t[:, cols]
+
+    def head_rows(b, carry):
+        rows = block(b)
+        vals = [hbuf[rows, 256 * col : 256 * col + 256].astype(f32) for col in range(4)]
+        square = sum(jnp.sum(v * v, axis=1, keepdims=True) for v in vals)
+        scale_r = lax.rsqrt(square * (1.0 / 1024.0) + EPSILON)
+        query, key_value = 0.0, 0.0
+        for col in range(4):
+            normed = vals[col] * scale_r * gain[1:2, 256 * col : 256 * col + 256]
+            for half_c in range(2):
+                lhs[24 + 2 * col + half_c, :, rows] = normed[:, 128 * half_c : 128 * half_c + 128].T.astype(bf16)
+            normed = normed.astype(bf16)
+            query = query + dot_f(normed, wgu[0, 256 * col : 256 * col + 256, :])
+            key_value = key_value + dot_f(normed, wgu[1, 256 * col : 256 * col + 256, :])
+        query = query.T
+        nothing = jnp.zeros((64, ROWS), f32)
+        for h in range(4):
+            turned = rotate_t(query[64 * h : 64 * h + 64], rows)
+            both = [turned, nothing] if h < 2 else [nothing, turned]
+            q2[h, rows, :] = jnp.concatenate(both, axis=0).T.astype(bf16)
+        key = key_value[:, :LANES].T
+        key = jnp.concatenate([rotate_t(key[:64], rows), rotate_t(key[64:], rows)], axis=0)
+        kt2[:, rows] = key.astype(bf16)
+        k2[rows, :] = key.T.astype(bf16)
+        value = key_value[:, LANES:]
+        v2[rows, :] = value.astype(bf16)
+        vt2[:, rows] = value.T.astype(bf16)
+        return carry
+
+    scaling = 1.0 / math.sqrt(HEAD_DIM)
+
+    def masked_scores(h, qb):
+        keys = ROWS * (qb + 1)
+        rows = pl.ds(ROWS * qb, ROWS)
+        scores = dot_nt(k2[0:keys, :], q2[h, rows, :]) * scaling
+        k_pos = lax.broadcasted_iota(jnp.int32, (keys, ROWS), 0)
+        q_pos = lax.broadcasted_iota(jnp.int32, (keys, ROWS), 1) + ROWS * qb
+        allowed = (k_pos <= q_pos) & (k_pos < length[0])
+        return jnp.where(allowed, scores, NEGATIVE)
+
+    def attend(qb):
+        keys = ROWS * (qb + 1)
+        rows = pl.ds(ROWS * qb, ROWS)
+
+        def one_head(h, carry):
+            scores = masked_scores(h, qb)
+            top_s = jnp.max(scores, axis=0, keepdims=True)
+            expo = jnp.exp(scores - top_s)
+            total = jnp.sum(expo, axis=0, keepdims=True)
+            probs = (expo / total).astype(bf16)
+            lse[pl.ds(h, 1), rows] = top_s + jnp.log(total)
+            v_head = vt2[pl.ds(pl.multiple_of((h // 2) * 64, 64), 64), 0:keys]
+            lhs[32 + h // 2, pl.ds(pl.multiple_of((h % 2) * 64, 64), 64), rows] = dot_f(v_head, probs).astype(bf16)
+            return carry
+
+        lax.fori_loop(0, 4, one_head, 0)
+        for half_c in range(2):
+            own_c = pl.ds(pl.multiple_of(tensor * 256 + half_c * 128, 128), 128)
+            acc[rows, own_c] = lhs[32 + half_c, :, rows].astype(f32).T
+        gather_x(qb).start()
+        gather_c(qb).start()
+
+    wait(token_load + proj_load)
+    lax.fori_loop(0, 4, head_rows, 0)
+    start(expert_load(0, 0))
+    for qb in range(4):
+        attend(qb)
+
+    wait(late_load)
+
+    def route_hits(b, carry):
+        rows = block(b)
+        lane = lax.broadcasted_iota(jnp.int32, (ROWS, LANES), 1)
+        pos = lax.broadcasted_iota(jnp.int32, (ROWS, LANES), 0) + b * ROWS
+        pos_wide = lax.broadcasted_iota(jnp.int32, (ROWS, 256), 0) + b * ROWS
+        hits = jnp.zeros((ROWS, LANES), f32)
+        weight = jnp.zeros((ROWS, LANES), f32)
+        for k in range(TOP_K):
+            same = picks[rows, k : k + 1] == lane
+            hits = jnp.where(same, 1.0, hits)
+            weight = jnp.where(same, pick_w[rows, k : k + 1], weight)
+        live = pos < length[0]
+        da2[0, rows, :] = jnp.where(live, hits, 0.0).astype(bf16)
+        slot_w[rows, :] = jnp.where(live, weight, 0.0)
+        for c in range(4):
+            rhs[c, rows, :] = jnp.where(pos_wide < length[0], rhs[c, rows, :].astype(f32), 0.0).astype(bf16)
+        return carry
+
+    lax.fori_loop(0, 4, route_hits, 0)
+    limit = ((5 * TOP_K * length[0] + 4 * EXPERTS - 1) // (4 * EXPERTS)).astype(f32)
+
+    def route_kept(b, carry):
+        rows = block(b)
+        row = lax.broadcasted_iota(jnp.int32, (ROWS, 1024), 0) + b * ROWS
+        earlier = jnp.where(lax.broadcasted_iota(jnp.int32, (ROWS, 1024), 1) < row, 1.0, 0.0).astype(bf16)
+        places = dot_f(earlier, da2[0])
+        slot_w[rows, :] = jnp.where(places < limit, slot_w[rows, :], 0.0)
+        return carry
+
+    lax.fori_loop(0, 4, route_kept, 0)
+
+    w_x.wait_recv()
+    w_f.start()
+    w_c.wait_recv()
+    w_f.wait_recv()
 
     def cast_out(b, carry):
-        for col in range(4):
-            rhs[22 + col, block(b, 64), :] = buf1[block(b, 64), 256 * col : 256 * col + 256].astype(bf16)
-            rhs[22 + col, pl.ds(pl.multiple_of(512 + b * 64, 64), 64), :] = buf2[
-                block(b, 64), 256 * col : 256 * col + 256
-            ].astype(bf16)
+        for c in range(4):
+            rhs[22 + c, block(b, 64), :] = buf[block(b, 64), 256 * c : 256 * c + 256].astype(bf16)
         return carry
 
-    lax.fori_loop(0, 8, cast_out, 0)
+    lax.fori_loop(0, 16, cast_out, 0)
 
     def forward_rows(b, carry):
         rows = block(b)
@@ -260,9 +299,6 @@
                 sums = [
                     sums[col] + dot_f(part, rhs[22 + col, 256 * k : 256 * k + 256, :]) for col in range(4)
                 ]
-        for half_c in range(2):
-            own_c = pl.ds(pl.multiple_of(tensor * 256 + half_c * 128, 128), 128)
-            lhs[32 + half_c, :, rows] = acc[rows, own_c].T.astype(bf16)
         square = sum(jnp.sum(v * v, axis=1, keepdims=True) for v in sums)
         scale_r = lax.rsqrt(square * (1.0 / 1024.0) + EPSILON)
         for col in range(4):
@@ -280,10 +316,12 @@
         gather_c(b).wait_recv()
         gather_f(b).wait_recv()
         gather_f(b).wait_send()
-        forward_rows(b, 0)
-    for b in range(4):
         gather_x(b).wait_send()
         gather_c(b).wait_send()
+        forward_rows(b, 0)
+    w_x.wait_send()
+    w_c.wait_send()
+    w_f.wait_send()
     keep = local(acc.at[:, wide], s_resid, iosem.at[0])
     keep.start()
     keep.wait()
@@ -340,19 +378,19 @@
         return pl.ds(0, 1152 if k == 0 else 1024)
 
     def sum_a(k):
-        return remote(acc.at[other, span(k)], buf1.at[:, span(k)], s1s.at[k], s1r.at[k], core_mate, "tensor")
+        return remote(acc.at[other, span(k)], buf.at[pl.ds(0, 512), span(k)], s1s.at[k], s1r.at[k], core_mate, "tensor")
 
     def sum_b(k):
-        return remote(acc.at[mine, span(k)], buf2.at[:, span(k)], s2s.at[k], s2r.at[k], x_mate, "tensor")
+        return remote(acc.at[mine, span(k)], buf.at[pl.ds(512, 512), span(k)], s2s.at[k], s2r.at[k], x_mate, "tensor")
 
     def sum_c(k):
         part = acc.at[mine, span(k)]
         return remote(part, part, s3s.at[k], s3r.at[k], core_mate, "tensor")
 
-    def add_in(k, buf):
+    def add_in(k, at_row):
         def step(b, carry):
             rows = pl.ds(pl.multiple_of(core * 512 + b * 64, 64), 64)
-            acc[rows, span(k)] += buf[block(b, 64), span(k)]
+            acc[rows, span(k)] += buf[pl.ds(pl.multiple_of(at_row + b * 64, 64), 64), span(k)]
             return carry
 
         lax.fori_loop(0, 8, step, 0)
@@ -365,7 +403,7 @@
 
     def sum_second(k):
         sum_a(k).wait_recv()
-        add_in(k, buf1)
+        add_in(k, 0)
         sum_a(k).wait_send()
         pl.semaphore_signal(ready3.at[k], inc=1, device_id={"tensor": core_mate}, device_id_type=MESH)
         pl.semaphore_wait(ready2.at[k], 1)
@@ -374,32 +412,13 @@
     def sum_third(k):
         sum_b(k).wait_recv()
         sum_b(k).wait_send()
-        add_in(k, buf2)
+        add_in(k, 512)
         pl.semaphore_wait(ready3.at[k], 1)
         sum_c(k).start()
 
     def sum_last(k):
         sum_c(k).wait_recv()
         sum_c(k).wait_send()
-
-    def head_rows(b):
-        rows = block(b)
-        vals = [hbuf[rows, 256 * col : 256 * col + 256].astype(f32) for col in range(4)]
-        square = sum(jnp.sum(v * v, axis=1, keepdims=True) for v in vals)
-        scale_r = lax.rsqrt(square * (1.0 / 1024.0) + EPSILON)
-        for col in range(4):
-            normed = vals[col] * scale_r * gain[1:2, 256 * col : 256 * col + 256]
-            for half_c in range(2):
-                lhs[24 + 2 * col + half_c, :, rows] = normed[:, 128 * half_c : 128 * half_c + 128].T.astype(bf16)
-
-    def in_halves(b, body):
-        @pl.when(b < 2)
-        def _():
-            body(buf1, block(b))
-
-        @pl.when(b >= 2)
-        def _():
-            body(buf2, block(b - 2))
 
     def norm_back(values, scale_r, grads, which):
         inner = sum(
@@ -417,25 +436,20 @@
     def middle_rows(b):
         rows = block(b)
 
-        def body(buf, part):
-            values = [buf[part, 256 * c : 256 * c + 256] for c in range(4)]
-            grads = [acc[rows, 256 * c : 256 * c + 256] for c in range(4)]
-            square = sum(jnp.sum(v * v, axis=1, keepdims=True) for v in values)
-            scale_r = lax.rsqrt(square * (1.0 / 1024.0) + EPSILON)
-            back = norm_back(values, scale_r, grads, 0)
-            for c in range(4):
-                total = rhs[c, rows, :].astype(f32) + back[c]
-                acc[rows, 256 * c : 256 * c + 256] = total
-                rhs[22 + c, rows, :] = total.astype(bf16)
-            for h in range(4):
-                d_head = dot_nt(rhs[22, rows, :], wdb[h, :, 0:256])
-                for c in range(1, 4):
-                    d_head = d_head + dot_nt(rhs[22 + c, rows, :], wdb[h, :, 256 * c : 256 * c + 256])
-                da2[h, rows, :] = d_head.astype(bf16)
-
-        in_halves(b, body)
-
-    scaling = 1.0 / math.sqrt(HEAD_DIM)
+        values = [buf[rows, 256 * c : 256 * c + 256] for c in range(4)]
+        grads = [acc[rows, 256 * c : 256 * c + 256] for c in range(4)]
+        square = sum(jnp.sum(v * v, axis=1, keepdims=True) for v in values)
+        scale_r = lax.rsqrt(square * (1.0 / 1024.0) + EPSILON)
+        back = norm_back(values, scale_r, grads, 0)
+        for c in range(4):
+            total = rhs[c, rows, :].astype(f32) + back[c]
+            acc[rows, 256 * c : 256 * c + 256] = total
+            rhs[22 + c, rows, :] = total.astype(bf16)
+        for h in range(4):
+            d_head = dot_nt(rhs[22, rows, :], wdb[h, :, 0:256])
+            for c in range(1, 4):
+                d_head = d_head + dot_nt(rhs[22 + c, rows, :], wdb[h, :, 256 * c : 256 * c + 256])
+            da2[h, rows, :] = d_head.astype(bf16)
 
     def turn_back(grad, cols):
         sine = grad * sin_t[:, cols]
@@ -446,11 +460,7 @@
         rows = pl.ds(ROWS * qb, ROWS)
         q_rows = q2[h, rows, :]
         d_rows = da2[h, rows, :]
-        scores = dot_nt(k2[0:keys, :], q_rows) * scaling
-        k_pos = lax.broadcasted_iota(jnp.int32, (keys, ROWS), 0)
-        q_pos = lax.broadcasted_iota(jnp.int32, (keys, ROWS), 1) + ROWS * qb
-        allowed = (k_pos <= q_pos) & (k_pos < length[0])
-        exact = jnp.exp(jnp.where(allowed, scores, NEGATIVE) - lse[pl.ds(h, 1), rows])
+        exact = jnp.exp(masked_scores(h, qb) - lse[pl.ds(h, 1), rows])
         d_probs = dot_nt(v2[0:keys, :], d_rows)
         inner = jnp.sum(exact * d_probs, axis=0, keepdims=True)
         d_scores = (exact * (d_probs - inner)).astype(bf16)
@@ -458,11 +468,11 @@
         dv_acc[0:keys, :] += dot_f(exact.astype(bf16), d_rows)
         k_head = kt2[pl.ds(pl.multiple_of((h // 2) * 64, 64), 64), 0:keys]
         d_q = dot_f(k_head, d_scores) * scaling
-        buf2[pl.ds(pl.multiple_of(h * 64, 64), 64), rows] = turn_back(d_q, rows)
+        buf[pl.ds(pl.multiple_of(h * 64, 64), 64), rows] = turn_back(d_q, rows)
 
     def turn_rows(b):
         rows = block(b)
-        rhs[20, rows, :] = buf2[0:256, rows].T.astype(bf16)
+        rhs[20, rows, :] = buf[0:256, rows].T.astype(bf16)
         d_k = (dk_acc[rows, :] * scaling).T
         d_k = jnp.concatenate([turn_back(d_k[:64], rows), turn_back(d_k[64:], rows)], axis=0)
         rhs[21, rows, 0:LANES] = d_k.T.astype(bf16)
@@ -475,17 +485,14 @@
     def token_rows(b):
         rows = block(b)
 
-        def body(buf, part):
-            values = [hbuf[rows, 256 * c : 256 * c + 256].astype(f32) for c in range(4)]
-            grads = [acc[rows, 256 * c : 256 * c + 256] for c in range(4)]
-            square = sum(jnp.sum(v * v, axis=1, keepdims=True) for v in values)
-            scale_r = lax.rsqrt(square * (1.0 / 1024.0) + EPSILON)
-            back = norm_back(values, scale_r, grads, 1)
-            for c in range(4):
-                cols = slice(256 * c, 256 * c + 256)
-                hbuf[rows, cols] = (buf[part, cols] + back[c]).astype(bf16)
-
-        in_halves(b, body)
+        values = [hbuf[rows, 256 * c : 256 * c + 256].astype(f32) for c in range(4)]
+        grads = [acc[rows, 256 * c : 256 * c + 256] for c in range(4)]
+        square = sum(jnp.sum(v * v, axis=1, keepdims=True) for v in values)
+        scale_r = lax.rsqrt(square * (1.0 / 1024.0) + EPSILON)
+        back = norm_back(values, scale_r, grads, 1)
+        for c in range(4):
+            cols = slice(256 * c, 256 * c + 256)
+            hbuf[rows, cols] = (buf[rows, cols] + back[c]).astype(bf16)
 
     def pair_load(pair, s):
         return local(w_down.at[pl.ds(2 * pair, 2)], wdb.at[pl.ds(2 * s, 2)], wsem.at[s, 2])
@@ -519,41 +526,32 @@
     def result_rows(b):
         rows = block(b)
 
-        def body(buf, part):
-            pos = lax.broadcasted_iota(jnp.int32, (ROWS, 1024), 0) + b * ROWS
-            total = buf[part, wide] + acc[rows, 0:1024]
-            hbuf[rows, :] = jnp.where(pos < length[0], total, 0.0).astype(bf16)
-
-        in_halves(b, body)
+        pos = lax.broadcasted_iota(jnp.int32, (ROWS, 1024), 0) + b * ROWS
+        total = buf[rows, wide] + acc[rows, 0:1024]
+        hbuf[rows, :] = jnp.where(pos < length[0], total, 0.0).astype(bf16)
 
     def halves_in(src):
-        return [
-            local(src.at[pl.ds(0, 512)], buf1.at[:, wide], iosem.at[1]),
-            local(src.at[pl.ds(512, 512)], buf2.at[:, wide], iosem.at[2]),
-        ]
-
-    def start(copies):
-        for copy in copies:
-            copy.start()
-
-    def wait(copies):
-        for copy in copies:
-            copy.wait()
+        return [local(src, buf.at[:, wide], iosem.at[1])]
 
     tokens_in = [local(x_in, hbuf, iosem.at[3])]
-    wo_load = [local(wo_in, wdb, iosem.at[4])]
-    proj_load = [local(wq_in, wgu.at[0], iosem.at[5]), local(wkv_in, wgu.at[1], iosem.at[6])]
+    wo_load = [
+        local(w_out.at[pl.ds(64 * h, 64)], wdb.at[h, pl.ds(64 * (h // 2), 64)], ld.at[8 + h]) for h in range(4)
+    ]
     dots_out = [local(acc.at[:, pl.ds(1024, LANES)], o_dots, iosem.at[7])]
     dres_out = [local(acc.at[:, wide], s_dres, iosem.at[8])]
     tokens_out = [local(hbuf, o_tokens, iosem.at[9])]
     result_out = [local(hbuf, o_result, iosem.at[10])]
 
+    def clear_wo():
+        for h in range(4):
+            wdb[h, 64 - 64 * (h // 2) : 128 - 64 * (h // 2), :] = jnp.zeros((64, 1024), bf16)
+
     def do_all(*steps):
         for step in steps:
             step()
 
     once = {
-        T_SUM1: lambda: do_all(lambda: sum_first(0), lambda: start(tokens_in + wo_load + proj_load)),
+        T_SUM1: lambda: do_all(lambda: sum_first(0), clear_wo, lambda: start(tokens_in + wo_load + proj_load)),
         T_SUM1 + 2: lambda: do_all(lambda: sum_second(0), lambda: wait(tokens_in)),
         T_MID1 - 3: lambda: sum_third(0),
         T_MID1 - 1: lambda: do_all(
@@ -584,7 +582,6 @@
             pl.when(t == when_t)(lambda src=src: wait(halves_in(src)))
         for begin, count, fn in (
             (0, EXPERTS, expert),
-            (T_HEAD, 4, head_rows),
             (T_MID1, 4, middle_rows),
             (T_TURN, 4, turn_rows),
             (T_PROJ, 4, project_rows),
@@ -855,16 +852,19 @@
         scratch_shapes=[
             vmem((34, 128, 1024), bf16), vmem((26, 1024, 256), bf16),
             vmem((2, ring, 128, 256), f32), vmem((2, ring, 128, 256), f32), vmem((2, ring, 128, 256), f32),
-            vmem((1024, 1152), f32), vmem((512, 1152), f32), vmem((512, 1152), f32),
+            vmem((1024, 1152), f32), vmem((1024, 1152), f32),
             vmem((1024, 1024), bf16), vmem((2, 1024, 256), bf16), vmem((4, 128, 1024), bf16),
-            vmem((4, 1024, 128), bf16), vmem((1024, 128), bf16), vmem((1024, 128), bf16), vmem((128, 1024), bf16),
+            vmem((4, 1024, 128), bf16), vmem((1024, 128), bf16), vmem((1024, 128), bf16),
+            vmem((128, 1024), bf16), vmem((128, 1024), bf16),
             vmem((8, 1024), f32), vmem((64, 1024), f32), vmem((64, 1024), f32),
             vmem((4, 1024, 128), bf16), vmem((1024, 128), f32), vmem((1024, 128), f32),
             vmem((1024, 128), f32), vmem((8, 1024), f32), vmem((128, 256), f32),
-            dma((17,)), dma((2, 3)), dma((11,)),
+            vmem((1024, 8), jnp.int32), vmem((1024, 8), f32),
+            dma((18,)), dma((2, 3)), dma((11,)),
         ]
         + [dma((2, ring))] * 10
         + [dma((4,))] * 6
+        + [dma((3,))] * 2
         + [dma((3,))] * 6
         + [reg((3,))] * 3,
         compiler_params=pltpu.CompilerParams(
@@ -897,64 +897,30 @@
     w_up,
     w_down,
 ):
-    seq_count = lengths.shape[0]
-    tok_rows = tokens.shape[0]
-    seq_len = tok_rows // seq_count
-    width = tokens.shape[1]
-    heads_here = w_query.shape[1] // HEAD_DIM
-    kv_here = w_key.shape[1] // HEAD_DIM
-    scaling = 1.0 / math.sqrt(HEAD_DIM)
-    valid = (jnp.arange(seq_len, dtype=jnp.int32)[None, :] < lengths[:, None]).reshape(-1)
+    seq_len = tokens.shape[0] // lengths.shape[0]
     cosine, sine = rope_tables(seq_len, HEAD_DIM)
-    w_out_all = lax.all_gather(w_out.astype(jnp.float32), "tensor", axis=0, tiled=True)
-    x_in = tokens.astype(jnp.float32)
-    h_attn = rms_norm(x_in, norm_attn).astype(jnp.bfloat16)
-    q_lin = dot_f(h_attn, w_query).reshape(seq_count, seq_len, heads_here, HEAD_DIM)
-    k_lin = dot_f(h_attn, w_key).reshape(seq_count, seq_len, kv_here, HEAD_DIM)
-    v_att = (
-        dot_f(h_attn, w_value).astype(jnp.bfloat16).reshape(seq_count, seq_len, kv_here, HEAD_DIM)
-    )
-    q_rot = rotate(q_lin, cosine, sine).astype(jnp.bfloat16)
-    k_rot = rotate(k_lin, cosine, sine).astype(jnp.bfloat16)
-    attended, lse_all = attend_forward(q_rot, k_rot, v_att, lengths, scaling)
-    attn_cat = attended.reshape(tok_rows, heads_here * HEAD_DIM).astype(jnp.bfloat16)
-    weights, onehot_f = route_weights(valid, chosen, gate_values)
-    d_out = jnp.where(valid[:, None], cotangent, 0)
-    q_heads = q_rot.reshape(tok_rows, heads_here, HEAD_DIM).transpose(1, 0, 2)
-    q_pad = jnp.concatenate(
-        [jnp.pad(q_heads[:2], ((0, 0), (0, 0), (0, 64))), jnp.pad(q_heads[2:], ((0, 0), (0, 0), (64, 0)))]
-    )
-    wo_heads = w_out.reshape(heads_here, HEAD_DIM, width)
-    wo_pad = jnp.concatenate(
-        [jnp.pad(wo_heads[:2], ((0, 0), (0, 64), (0, 0))), jnp.pad(wo_heads[2:], ((0, 0), (64, 0), (0, 0)))]
-    )
-    k_flat = k_rot.reshape(tok_rows, -1)
-    lse_rows = lse_all[0].reshape(-1, heads_here, min(512, seq_len)).transpose(1, 0, 2).reshape(heads_here, tok_rows)
     sums, (result, grad_tokens, dots) = run_layer(
         mesh,
         lengths,
-        attn_cat.astype(jnp.float32),
-        w_out_all,
         tokens,
-        d_out,
-        jnp.pad(weights, ((0, 0), (0, 128 - EXPERTS))),
-        jnp.pad(jnp.stack([norm_moe, norm_attn]), ((0, 6), (0, 0))),
+        cotangent,
+        chosen,
+        gate_values,
+        norm_attn[None, :],
+        norm_moe[None, :],
         w_gate,
         w_up,
         w_down,
-        q_pad,
-        k_flat,
-        v_att.reshape(tok_rows, -1),
-        k_flat.T,
-        jnp.pad(lse_rows, ((0, 8 - heads_here), (0, 0))),
-        cosine.T,
-        sine.T,
-        wo_pad,
+        cosine,
+        sine,
+        w_out,
         w_query,
-        jnp.concatenate([w_key, w_value], axis=1),
+        w_key,
+        w_value,
     )
     grad_gate, grad_up, grad_down, grad_query, grad_key, grad_value, grad_out, norm_rows = sums
-    d_gates = jnp.sum(onehot_f * dots[:, None, :EXPERTS], axis=-1)
+    picked = chosen[:, :, None] == jnp.arange(EXPERTS, dtype=jnp.int32)[None, None, :]
+    d_gates = jnp.sum(jnp.where(picked, dots[:, None, :EXPERTS], 0.0), axis=-1)
     return (
         result,
         grad_tokens,

time: 647 us -> 594 us (0.918)
  other arithmetic: 22.8 us -> 0.73 us
  Pallas kernels: 539 us -> 561 us
  matrix products: 21 us -> 0 us
  local copies, waits for them, and re-layouts: 47.6 us -> 29.9 us
  between operations: 15.8 us -> 1.33 us
    pallas_call x1, Pallas kernels: 539 us -> 561 us  [run_layer(): pl.pallas_call(functools.partial(layer_kernel, nz, hop, ring), out_shape=...]
    dot_general x8 -> x0, matrix products: 21 us -> none  [the longest x2 9.09 us: forward_block(): jnp.einsum('kgqs,skd->qkgd', probs, v_seq, preferred_element_type=jnp.flo...]
    concatenate x5 -> x0, other arithmetic: 7.11 us -> none  [the longest x2 2.88 us: rotate(): jnp.concatenate([-values[..., half_w:], values[..., :half_w]], axis=-1)]
    unnamed x89 -> x34, local copies, waits for them, and re-layouts: 28.6 us -> 28.7 us
  transfers between devices with their start and end apart: 1 -> 0, of which waited for: 0 -> 0; matrix products, arithmetic and copies ran while one was open for 9% -> 0% of each run, Pallas kernels for 0% -> 0%
where the time goes in v4:
time: 594 us; the launch traced here: 593 us
  Pallas kernels  561 us (94%)
  local copies, waits for them, and re-layouts  29.9 us (5%)
    pallas_call x1, Pallas kernels, run_layer(): pl.pallas_call(functools.partial(layer_kernel, nz, hop, ring), out_shape=...  561 us
    unnamed x34, local copies, waits for them, and re-layouts  28.7 us

profile of v4, /device:TPU:0, one launch (start us, length us, event | category | flops | bytes accessed | tf_op | source)
XLA Modules:
  0.0 593.2 jit_solution(9084164155647781677)
XLA Ops:
  1.3 1.8 copy.32.gates
  3.0 1.8 copy.31.chosen
  4.8 0.0 copy-start.5
  4.8 561.2 %shard_map.247 = (f32[16,1024,128]{2,1,0:T(8,128)}, f32[16,1024,128]{2,1,0:T(8,128)}, f32[16,128,1024]{2,1,0:T(8,128)}, f32[1024,256]{1,0:T(8,128)}, f32[1024,12...) custom-call(s32[1]{0:T(128)S(6)} %copy.45.length, ...), custom_call_target="tpu_custom_call" | custom-call | tf_op jit(solution)/shard_map/pallas_call | solution.py:847
  566.0 0.0 copy-start
  566.0 0.9 slice_bitcast_fusion
  566.9 0.6 copy.35
  567.5 0.6 copy.34
  568.1 1.2 copy.33
  569.3 0.0 copy-done.5
  569.3 0.7 select_reduce_fusion
  570.0 0.0 copy-start.2
  570.0 0.0 copy-start.4
  570.0 3.2 copy.46
  573.2 0.0 copy-done
  573.2 0.0 copy-start.3
  573.2 0.0 copy-start.1
  573.2 0.0 slice-start.2
  573.3 1.3 copy.47
  574.6 0.0 copy-done.2
  574.6 1.0 copy.48
  575.5 0.0 copy-done.4
  575.5 0.8 copy.49
  576.3 0.0 copy-done.3
  576.3 0.8 copy.50
  577.1 0.0 copy-done.1
  577.1 0.0 slice-start
  577.1 1.0 copy.51
  578.1 0.0 slice-start.3
  578.1 0.0 slice-start.1
  578.1 8.3 %copy.52 = f32[16,1024,128]{2,1,0:T(8,128)} copy(f32[16,1024,128]{2,1,0:T(8,128)} %get-tuple-element.57) | data formatting | bytes 16777216
  586.4 0.0 slice-done.2
  586.4 0.0 slice-done.3
  586.4 3.4 copy.53
  589.8 0.0 slice-done
  589.8 0.0 slice-done.1
  589.8 3.4 copy.54
  (2 shorter events, 0.0 us)
Async XLA Ops:
  4.8 564.5 %copy-start.5 = (s32[1024,8]{0,1:T(8,128)S(1)}, s32[1024,8]{0,1:T(8,128)}, u32[]{:S(2)}) copy-start(s32[1024,8]{0,1:T(8,128)} %param.18) | copy-start | bytes 98308
  566.0 7.2 %copy-start = (bf16[1024,1024]{1,0:T(8,128)(2,1)S(1)}, bf16[1024,1024]{1,0:T(8,128)(2,1)}, u32[]{:S(2)}) copy-start(bf16[1024,1024]{1,0:T(8,128)(2,1)} %get-tuple-element.49) | copy-start | bytes 6291460
  570.0 4.5 copy-start.2
  570.0 5.5 copy-start.4
  573.2 3.1 copy-start.3
  573.2 3.9 copy-start.1
  573.2 13.1 %slice-start.2 = ((s8[8388608]{0:T(1024)(128)(4,1)}), s8[4194304]{0:T(1024)(128)(4,1)S(1)}, s32[]{:S(2)}) async-start(s8[8388608]{0:T(1024)(128)(4,1)} %bitcast.11), calls=%async_computation.2 | async-start | bytes 8388608
  577.1 12.6 %slice-start = ((s8[8388608]{0:T(1024)(128)(4,1)}), s8[4194304]{0:T(1024)(128)(4,1)S(1)}, s32[]{:S(2)}) async-start(s8[8388608]{0:T(1024)(128)(4,1)} %bitcast.9), calls=%async_computation | async-start | bytes 8388608
  578.1 8.3 %slice-start.3 = ((s8[8388608]{0:T(1024)(128)(4,1)}), s8[4194304]{0:T(1024)(128)(4,1)S(1)}, s32[]{:S(2)}) async-start(s8[8388608]{0:T(1024)(128)(4,1)} %bitcast.11), calls=%async_computation.3 | async-start | bytes 8388608
  578.1 11.7 %slice-start.1 = ((s8[8388608]{0:T(1024)(128)(4,1)}), s8[4194304]{0:T(1024)(128)(4,1)S(1)}, s32[]{:S(2)}) async-start(s8[8388608]{0:T(1024)(128)(4,1)} %bitcast.9), calls=%async_computation.1 | async-start | bytes 8388608

commit v5 on v4

--- a/solution.py
+++ b/solution.py
@@ -36,6 +36,7 @@
 ROWS = 256
 N_CLASS = 109
 HOP = 2
+SPARE = 5
 T_SUM1 = 16
 T_MID1 = 33
 T_ATT = 37
@@ -65,9 +66,9 @@
     length, x_in, d_out, chosen, gates, gain_attn, gain_moe, w_gate, w_up, w_down,
     cos_in, sin_in, w_out, w_query, w_key, w_value,
     o_gate, o_up, o_down, o_q, o_k, o_v, o_out, o_norm, o_result, o_tokens, o_dots, s_resid, s_dres,
-    lhs, rhs, pbuf, zbuf, ybuf, acc, buf, hbuf, wgu, wdb, q2, k2, v2, kt2, vt2, lse, cos_t, sin_t,
+    lhs, rhs, pbuf, zbuf, ybuf, xbuf, acc, buf, hbuf, wgu, wdb, q2, k2, v2, kt2, vt2, lse, cos_t, sin_t,
     da2, dk_acc, dv_acc, slot_w, gain, norms, picks, pick_w,
-    ld, wsem, iosem, ys, yr, zs, zr, fs, fr, gs, gr, os0, os1,
+    ld, wsem, iosem, ys, yr, zs, zr, fs, fr, gs, gr, os0, os1, xr,
     cs_c, cr_c, cs_x, cr_x, cs_f, cr_f, ws, wr, s1s, s1r, s2s, s2r, s3s, s3r, ready1, ready2, ready3,
 ):
     f32, bf16 = jnp.float32, jnp.bfloat16
@@ -243,36 +244,32 @@
 
     wait(late_load)
 
-    def route_hits(b, carry):
+    expert_id = lax.broadcasted_iota(jnp.int32, (EXPERTS, 1024), 0)
+    alive = lax.broadcasted_iota(jnp.int32, (EXPERTS, 1024), 1) < length[0]
+    hits = jnp.zeros((EXPERTS, 1024), f32)
+    weight = jnp.zeros((EXPERTS, 1024), f32)
+    for k in range(TOP_K):
+        same = (picks[k : k + 1, :] == expert_id) & alive
+        hits = jnp.where(same, 1.0, hits)
+        weight = jnp.where(same, pick_w[k : k + 1, :], weight)
+    hits = hits.astype(bf16)
+    limit = ((5 * TOP_K * length[0] + 4 * EXPERTS - 1) // (4 * EXPERTS)).astype(f32)
+    for b in range(4):
+        rows = pl.ds(ROWS * b, ROWS)
+        token = lax.broadcasted_iota(jnp.int32, (1024, ROWS), 1) + ROWS * b
+        earlier = jnp.where(lax.broadcasted_iota(jnp.int32, (1024, ROWS), 0) < token, 1.0, 0.0).astype(bf16)
+        places = dot_f(hits, earlier)
+        kept = jnp.where(places < limit, weight[:, ROWS * b : ROWS * b + ROWS], 0.0)
+        slot_w[rows, :] = jnp.concatenate([kept, jnp.zeros((LANES - EXPERTS, ROWS), f32)], axis=0).T
+
+    def mask_rows(b, carry):
         rows = block(b)
-        lane = lax.broadcasted_iota(jnp.int32, (ROWS, LANES), 1)
-        pos = lax.broadcasted_iota(jnp.int32, (ROWS, LANES), 0) + b * ROWS
-        pos_wide = lax.broadcasted_iota(jnp.int32, (ROWS, 256), 0) + b * ROWS
-        hits = jnp.zeros((ROWS, LANES), f32)
-        weight = jnp.zeros((ROWS, LANES), f32)
-        for k in range(TOP_K):
-            same = picks[rows, k : k + 1] == lane
-            hits = jnp.where(same, 1.0, hits)
-            weight = jnp.where(same, pick_w[rows, k : k + 1], weight)
-        live = pos < length[0]
-        da2[0, rows, :] = jnp.where(live, hits, 0.0).astype(bf16)
-        slot_w[rows, :] = jnp.where(live, weight, 0.0)
+        pos = lax.broadcasted_iota(jnp.int32, (ROWS, 256), 0) + b * ROWS
         for c in range(4):
-            rhs[c, rows, :] = jnp.where(pos_wide < length[0], rhs[c, rows, :].astype(f32), 0.0).astype(bf16)
+            rhs[c, rows, :] = jnp.where(pos < length[0], rhs[c, rows, :].astype(f32), 0.0).astype(bf16)
         return carry
 
-    lax.fori_loop(0, 4, route_hits, 0)
-    limit = ((5 * TOP_K * length[0] + 4 * EXPERTS - 1) // (4 * EXPERTS)).astype(f32)
-
-    def route_kept(b, carry):
-        rows = block(b)
-        row = lax.broadcasted_iota(jnp.int32, (ROWS, 1024), 0) + b * ROWS
-        earlier = jnp.where(lax.broadcasted_iota(jnp.int32, (ROWS, 1024), 1) < row, 1.0, 0.0).astype(bf16)
-        places = dot_f(earlier, da2[0])
-        slot_w[rows, :] = jnp.where(places < limit, slot_w[rows, :], 0.0)
-        return carry
-
-    lax.fori_loop(0, 4, route_kept, 0)
+    lax.fori_loop(0, 4, mask_rows, 0)
 
     w_x.wait_recv()
     w_f.start()
@@ -606,7 +603,7 @@
 
             @pl.when((i >= 0) & (i < N_CLASS))
             def _():
-                body(i, i % ring, i % 2 == 0)
+                body(i, i % ring, i % 5)
 
         def ycopy_a(s):
             return remote(pbuf.at[c, s, oth], ybuf.at[c, s, half], ys.at[c, s], yr.at[c, s], mate)
@@ -614,6 +611,15 @@
         def ycopy_b(s):
             return remote(zbuf.at[c, s], ybuf.at[c, s], ys.at[c, s], yr.at[c, s], mate)
 
+        def ycopy_c(s, k):
+            return remote(zbuf.at[c, s], xbuf.at[c, k], ys.at[c, s], xr.at[c, k], mate)
+
+        def leaf_copy(s):
+            return remote(pbuf.at[c, s], ybuf.at[c, s], ys.at[c, s], yr.at[c, s], prv)
+
+        def fcopy_c(s):
+            return remote(pbuf.at[c, s], zbuf.at[c, s], gs.at[c, s], fr.at[c, s], nxt)
+
         def zcopy_a(s):
             return remote(zbuf.at[c, s, half], zbuf.at[c, s, half], zs.at[c, s], zr.at[c, s], nxt)
 
@@ -629,7 +635,7 @@
         def gcopy(s):
             return remote(pbuf.at[c, s, own], ybuf.at[c, s, pl.ds(64, 64)], gs.at[c, s], gr.at[c, s], mate)
 
-        def first(i, s, is_a):
+        def first(i, s, kind):
             g = 2 * i + c
             expert, part = g // 12, g % 12
             a = g - 192
@@ -648,12 +654,16 @@
             def _():
                 pbuf[c, s] = norms[...]
 
-            @pl.when(is_a)
+            @pl.when(kind % 2 == 0)
             def _():
                 ycopy_a(s).start()
 
-        def second(i, s, is_a):
-            @pl.when(is_a)
+            @pl.when((kind == 3) & (p == last))
+            def _():
+                leaf_copy(s).start()
+
+        def second(i, s, kind):
+            @pl.when(kind % 2 == 0)
             def _():
                 ycopy_a(s).wait_recv()
 
@@ -676,7 +686,7 @@
                     fcopy_a(s).start()
                     gcopy(s).start()
 
-            @pl.when(jnp.logical_not(is_a))
+            @pl.when((kind % 2 == 1) & ((kind == 1) | (p < last)))
             def _():
                 @pl.when(p > 0)
                 def _():
@@ -687,25 +697,42 @@
                 def _():
                     zbuf[c, s] = pbuf[c, s]
 
-                @pl.when(p < last)
+                @pl.when((p < last - 1) | ((kind == 1) & (p < last)))
                 def _():
                     zcopy_b(s).start()
 
-                @pl.when(p == last)
+                @pl.when((kind == 1) & (p == last))
                 def _():
                     ycopy_b(s).start()
 
-        def third(i, s, is_a):
-            @pl.when(jnp.logical_not(is_a) & (p == last))
+                @pl.when((kind == 3) & (p == last - 1))
+                def _():
+                    leaf_copy(s).wait_recv()
+                    zbuf[c, s] = zbuf[c, s] + ybuf[c, s]
+                    ycopy_c(s, (i // 5) % SPARE).start()
+
+        def third(i, s, kind):
+            @pl.when((kind == 1) & (p == last))
             def _():
                 ycopy_b(s).wait_recv()
                 pbuf[c, s] = zbuf[c, s] + ybuf[c, s]
                 fcopy_b(s).start()
 
-        def fourth(i, s, is_a):
+            @pl.when((kind == 3) & (p == last - 1))
+            def _():
+                k = (i // 5) % SPARE
+                ycopy_c(s, k).wait_recv()
+                pbuf[c, s] = zbuf[c, s] + xbuf[c, k]
+                fcopy_c(s).start()
+
+                @pl.when(p > 0)
+                def _():
+                    fcopy_b(s).start()
+
+        def fourth(i, s, kind):
             @pl.when(p < last)
             def _():
-                @pl.when(is_a)
+                @pl.when(kind % 2 == 0)
                 def _():
                     fcopy_a(s).wait_recv()
 
@@ -715,7 +742,7 @@
 
                     gcopy(s).start()
 
-                @pl.when(jnp.logical_not(is_a))
+                @pl.when((kind == 1) | ((kind == 3) & (p < last - 1)))
                 def _():
                     fcopy_b(s).wait_recv()
 
@@ -727,12 +754,18 @@
             pltpu.make_async_copy(pbuf.at[c, s, :, pl.ds(0, 128)], dst0, os0.at[c, s]).start()
             pltpu.make_async_copy(pbuf.at[c, s, :, pl.ds(128, 128)], dst1, os1.at[c, s]).start()
 
-        def fifth(i, s, is_a):
-            @pl.when(is_a)
+        def fifth(i, s, kind):
+            @pl.when(kind % 2 == 0)
             def _():
                 gcopy(s).wait_recv()
                 ycopy_a(s).wait_send()
                 pbuf[c, s, oth] = ybuf[c, s, pl.ds(64, 64)]
+
+            @pl.when((kind == 3) & (p == last))
+            def _():
+                fcopy_c(s).wait_recv()
+                leaf_copy(s).wait_send()
+                pbuf[c, s] = zbuf[c, s]
 
             g = 2 * i + c
             expert, part = g // 12, g % 12
@@ -771,11 +804,11 @@
                 col1 = pl.multiple_of((b % 4) * 256 + 128, 128)
                 store(s, o_out.at[rows, pl.ds(col, 128)], o_out.at[rows, pl.ds(col1, 128)])
 
-        def sixth(i, s, is_a):
+        def sixth(i, s, kind):
             pltpu.make_async_copy(pbuf.at[c, s, :, pl.ds(0, 128)], o_k.at[pl.ds(0, 128)], os0.at[c, s]).wait()
             pltpu.make_async_copy(pbuf.at[c, s, :, pl.ds(0, 128)], o_k.at[pl.ds(0, 128)], os1.at[c, s]).wait()
 
-            @pl.when(is_a)
+            @pl.when(kind % 2 == 0)
             def _():
                 gcopy(s).wait_send()
 
@@ -787,15 +820,20 @@
                 def _():
                     fcopy_a(s).wait_send()
 
-            @pl.when(jnp.logical_not(is_a))
-            def _():
-                @pl.when(p < last)
+            @pl.when((kind == 1) | ((kind == 3) & (p < last)))
+            def _():
+                @pl.when((p < last - 1) | ((kind == 1) & (p < last)))
                 def _():
                     zcopy_b(s).wait_send()
 
-                @pl.when(p == last)
+                @pl.when((kind == 1) & (p == last))
                 def _():
                     ycopy_b(s).wait_send()
+
+                @pl.when((kind == 3) & (p == last - 1))
+                def _():
+                    ycopy_c(s, 0).wait_send()
+                    fcopy_c(s).wait_send()
 
                 @pl.when(p > 0)
                 def _():
@@ -828,7 +866,7 @@
     last = nz - 1
     hop = HOP
     ring = hop * (2 * last + 4) + 2
-    ring += ring % 2
+    ring += -ring % 5
     f32, bf16 = jnp.float32, jnp.bfloat16
 
     def out(shape, kind=f32):
@@ -852,23 +890,24 @@
         scratch_shapes=[
             vmem((34, 128, 1024), bf16), vmem((26, 1024, 256), bf16),
             vmem((2, ring, 128, 256), f32), vmem((2, ring, 128, 256), f32), vmem((2, ring, 128, 256), f32),
-            vmem((1024, 1152), f32), vmem((1024, 1152), f32),
+            vmem((2, SPARE, 128, 256), f32), vmem((1024, 1152), f32), vmem((1024, 1152), f32),
             vmem((1024, 1024), bf16), vmem((2, 1024, 256), bf16), vmem((4, 128, 1024), bf16),
             vmem((4, 1024, 128), bf16), vmem((1024, 128), bf16), vmem((1024, 128), bf16),
             vmem((128, 1024), bf16), vmem((128, 1024), bf16),
             vmem((8, 1024), f32), vmem((64, 1024), f32), vmem((64, 1024), f32),
             vmem((4, 1024, 128), bf16), vmem((1024, 128), f32), vmem((1024, 128), f32),
             vmem((1024, 128), f32), vmem((8, 1024), f32), vmem((128, 256), f32),
-            vmem((1024, 8), jnp.int32), vmem((1024, 8), f32),
+            vmem((8, 1024), jnp.int32), vmem((8, 1024), f32),
             dma((18,)), dma((2, 3)), dma((11,)),
         ]
         + [dma((2, ring))] * 10
+        + [dma((2, SPARE))]
         + [dma((4,))] * 6
         + [dma((3,))] * 2
         + [dma((3,))] * 6
         + [reg((3,))] * 3,
         compiler_params=pltpu.CompilerParams(
-            collective_id=0, has_side_effects=True, vmem_limit_bytes=62 * 2**20
+            collective_id=0, has_side_effects=True, vmem_limit_bytes=63 * 2**20
         ),
     )(*operands)
     sums, rest = tuple(res[:8]), res[8:11]
@@ -904,8 +943,8 @@
         lengths,
         tokens,
         cotangent,
-        chosen,
-        gate_values,
+        chosen.T,
+        gate_values.T,
         norm_attn[None, :],
         norm_moe[None, :],
         w_gate,

time: 594 us -> 569 us (0.958)
  Pallas kernels: 561 us -> 541 us
    pallas_call x1, Pallas kernels: 561 us -> 541 us  [run_layer(): pl.pallas_call(functools.partial(layer_kernel, nz, hop, ring), out_shape=...]
    unnamed x34 -> x32, local copies, waits for them, and re-layouts: 28.7 us -> 25.2 us
where the time goes in v5:
time: 569 us
  Pallas kernels  541 us (95%)
  local copies, waits for them, and re-layouts  26.4 us (5%)
    pallas_call x1, Pallas kernels, run_layer(): pl.pallas_call(functools.partial(layer_kernel, nz, hop, ring), out_shape=...  541 us
    unnamed x32, local copies, waits for them, and re-layouts  25.2 us

profile of v5, /device:TPU:0, one launch (start us, length us, event | category | flops | bytes accessed | tf_op | source)
XLA Modules:
  0.0 569.0 jit_solution(14242311198233830995)
XLA Ops:
  1.3 0.0 copy-start.5
  1.3 540.6 %shard_map.247 = (f32[16,1024,128]{2,1,0:T(8,128)}, f32[16,1024,128]{2,1,0:T(8,128)}, f32[16,128,1024]{2,1,0:T(8,128)}, f32[1024,256]{1,0:T(8,128)}, f32[1024,12...) custom-call(s32[1]{0:T(128)S(6)} %copy.41.length, ...), custom_call_target="tpu_custom_call" | custom-call | tf_op jit(solution)/shard_map/pallas_call | solution.py:885
  541.9 0.0 copy-start
  541.9 0.9 slice_bitcast_fusion
  542.7 0.6 copy.31
  543.3 0.6 copy.30
  543.9 1.2 copy.29
  545.1 0.0 copy-done.5
  545.1 0.7 select_reduce_fusion
  545.9 0.0 copy-start.2
  545.9 0.0 copy-start.4
  545.9 3.2 copy.42
  549.1 0.0 copy-done
  549.1 0.0 copy-start.3
  549.1 0.0 copy-start.1
  549.1 0.0 slice-start.2
  549.1 1.3 copy.43
  550.4 0.0 copy-done.2
  550.4 1.0 copy.44
  551.4 0.0 copy-done.4
  551.4 0.8 copy.45
  552.2 0.0 copy-done.3
  552.2 0.8 copy.46
  553.0 0.0 copy-done.1
  553.0 0.0 slice-start
  553.0 1.0 copy.47
  553.9 0.0 slice-start.3
  554.0 0.0 slice-start.1
  554.0 8.3 %copy.48 = f32[16,1024,128]{2,1,0:T(8,128)} copy(f32[16,1024,128]{2,1,0:T(8,128)} %get-tuple-element.57) | data formatting | bytes 16777216
  562.2 0.0 slice-done.2
  562.2 0.0 slice-done.3
  562.2 3.4 copy.49
  565.6 0.0 slice-done
  565.6 0.0 slice-done.1
  565.6 3.4 copy.50
  (2 shorter events, 0.0 us)
Async XLA Ops:
  1.3 543.8 %copy-start.5 = (s32[1024,8]{0,1:T(8,128)S(1)}, s32[1024,8]{0,1:T(8,128)}, u32[]{:S(2)}) copy-start(s32[1024,8]{0,1:T(8,128)} %param.18) | copy-start | bytes 98308
  541.9 7.2 %copy-start = (bf16[1024,1024]{1,0:T(8,128)(2,1)S(1)}, bf16[1024,1024]{1,0:T(8,128)(2,1)}, u32[]{:S(2)}) copy-start(bf16[1024,1024]{1,0:T(8,128)(2,1)} %get-tuple-element.49) | copy-start | bytes 6291460
  545.9 4.5 copy-start.2
  545.9 5.5 copy-start.4
  549.1 3.1 copy-start.3
  549.1 3.9 copy-start.1
  549.1 13.1 %slice-start.2 = ((s8[8388608]{0:T(1024)(128)(4,1)}), s8[4194304]{0:T(1024)(128)(4,1)S(1)}, s32[]{:S(2)}) async-start(s8[8388608]{0:T(1024)(128)(4,1)} %bitcast.13), calls=%async_computation.2 | async-start | bytes 8388608
  553.0 12.6 %slice-start = ((s8[8388608]{0:T(1024)(128)(4,1)}), s8[4194304]{0:T(1024)(128)(4,1)S(1)}, s32[]{:S(2)}) async-start(s8[8388608]{0:T(1024)(128)(4,1)} %bitcast.11), calls=%async_computation | async-start | bytes 8388608
  553.9 8.3 %slice-start.3 = ((s8[8388608]{0:T(1024)(128)(4,1)}), s8[4194304]{0:T(1024)(128)(4,1)S(1)}, s32[]{:S(2)}) async-start(s8[8388608]{0:T(1024)(128)(4,1)} %bitcast.13), calls=%async_computation.3 | async-start | bytes 8388608
  554.0 11.7 %slice-start.1 = ((s8[8388608]{0:T(1024)(128)(4,1)}), s8[4194304]{0:T(1024)(128)(4,1)S(1)}, s32[]{:S(2)}) async-start(s8[8388608]{0:T(1024)(128)(4,1)} %bitcast.11), calls=%async_computation.1 | async-start | bytes 8388608

commit v6 on v5

--- a/solution.py
+++ b/solution.py
@@ -28,25 +28,25 @@
 def rope_tables(positions, width):
     half_w = width // 2
     freqs = THETA ** (-np.arange(half_w, dtype=np.float64) * 2.0 / width)
-    angles = np.concatenate([freqs, freqs])[:, None] * np.arange(positions, dtype=np.float64)[None, :]
+    angles = freqs[:, None] * np.arange(positions, dtype=np.float64)[None, :]
     return (np.cos(angles).astype(np.float32), np.sin(angles).astype(np.float32))
 
 
 LANES = 128
 ROWS = 256
-N_CLASS = 109
+N_CLASS = 108
 HOP = 2
-SPARE = 5
-T_SUM1 = 16
-T_MID1 = 33
-T_ATT = 37
-T_TURN = 53
-T_PROJ = 57
-T_SUM2 = 61
-T_TOK = 78
-T_MOE = 82
-T_SUM3 = 90
-T_RES = 107
+SPARE = 3
+T_SUM1 = 30
+T_MID1 = 47
+T_ATT = 51
+T_TURN = 59
+T_PROJ = 63
+T_SUM2 = 67
+T_TOK = 84
+T_MOE = 88
+T_SUM3 = 96
+T_RES = 113
 
 
 def dot_nt(left, right):
@@ -65,11 +65,11 @@
     nz, hop, ring,
     length, x_in, d_out, chosen, gates, gain_attn, gain_moe, w_gate, w_up, w_down,
     cos_in, sin_in, w_out, w_query, w_key, w_value,
-    o_gate, o_up, o_down, o_q, o_k, o_v, o_out, o_norm, o_result, o_tokens, o_dots, s_resid, s_dres,
+    o_gate, o_up, o_down, o_q, o_k, o_v, o_out, o_norm0, o_norm1, o_result, o_tokens, o_dots, s_resid, s_dres,
     lhs, rhs, pbuf, zbuf, ybuf, xbuf, acc, buf, hbuf, wgu, wdb, q2, k2, v2, kt2, vt2, lse, cos_t, sin_t,
-    da2, dk_acc, dv_acc, slot_w, gain, norms, picks, pick_w,
+    da2, dk_acc, dv_acc, slot_w, gain, norms, picks, pick_w, norm_in, d_pick,
     ld, wsem, iosem, ys, yr, zs, zr, fs, fr, gs, gr, os0, os1, xr,
-    cs_c, cr_c, cs_x, cr_x, cs_f, cr_f, ws, wr, s1s, s1r, s2s, s2r, s3s, s3r, ready1, ready2, ready3,
+    cs_c, cr_c, cs_x, cr_x, cs_f, cr_f, ws, wr, s1s, s1r, s2s, s2r, s3s, s3r, ready1, ready2, ready3, ns, nr,
 ):
     f32, bf16 = jnp.float32, jnp.bfloat16
     dp = lax.axis_index("dp")
@@ -80,6 +80,7 @@
     mate = base + z * 2 + (1 - y)
     up_id = base + jnp.minimum(z + 1, last) * 2 + y
     dn_id = base + jnp.maximum(z - 1, 0) * 2 + y
+    far = base + ((z + 2) % nz) * 2 + y
     core = tensor % 2
     core_mate = tensor - core + (1 - core)
     x_mate = (tensor + 2) % 4
@@ -97,7 +98,7 @@
         return pl.ds(pl.multiple_of(b * size, size), size)
 
     bar = pltpu.get_barrier_semaphore()
-    for axis, dev in (("dp", mate), ("tensor", core_mate), ("tensor", x_mate)):
+    for axis, dev in (("dp", mate), ("dp", far), ("tensor", core_mate), ("tensor", x_mate)):
         pl.semaphore_signal(bar, inc=1, device_id={axis: dev}, device_id_type=MESH)
 
     @pl.when(z < last)
@@ -144,10 +145,17 @@
             copy.wait()
 
     start(out_load + token_load + proj_load + late_load)
-    pl.semaphore_wait(bar, 3 + (z < last).astype(jnp.int32) + (z > 0).astype(jnp.int32))
+    pl.semaphore_wait(bar, 4 + (z < last).astype(jnp.int32) + (z > 0).astype(jnp.int32))
 
     part_w = buf.at[share, wide]
-    w_x = remote(part_w, part_w, ws.at[0], wr.at[0], x_mate, "tensor")
+    quarter = 2 * (z % 2) + y
+    part_q = buf.at[pl.ds(pl.multiple_of(tensor * 256 + quarter * 64, 64), 64), wide]
+    part_y = buf.at[pl.ds(pl.multiple_of(x_mate * 256 + quarter * 64, 64), 64), wide]
+    part_z = buf.at[pl.ds(pl.multiple_of(x_mate * 256 + (z % 2) * 128, 128), 128), wide]
+    pair = base + (z + 1 - 2 * (z % 2)) * 2 + y
+    w_x = remote(part_q, part_q, ws.at[0], wr.at[0], x_mate, "tensor")
+    w_y = remote(part_y, part_y, ws.at[3], wr.at[3], mate)
+    w_z = remote(part_z, part_z, ws.at[4], wr.at[4], pair)
     w_c = remote(part_w, part_w, ws.at[1], wr.at[1], core_mate, "tensor")
     part_f = buf.at[block(x_mate), wide]
     w_f = remote(part_f, part_f, ws.at[2], wr.at[2], core_mate, "tensor")
@@ -172,8 +180,9 @@
         return remote(part, part, cs_f.at[b], cr_f.at[b], core_mate, "tensor")
 
     def rotate_t(values, cols):
-        turned = jnp.concatenate([-values[32:], values[:32]], axis=0)
-        return values * cos_t[:, cols] + turned * sin_t[:, cols]
+        one, two = values[:32], values[32:]
+        cosine, sine = cos_t[:, cols], sin_t[:, cols]
+        return jnp.concatenate([one * cosine - two * sine, two * cosine + one * sine], axis=0)
 
     def head_rows(b, carry):
         rows = block(b)
@@ -237,10 +246,22 @@
         gather_c(qb).start()
 
     wait(token_load + proj_load)
-    lax.fori_loop(0, 4, head_rows, 0)
+    head_rows(0, 0)
+    attend(0)
+    head_rows(1, 0)
+    w_x.wait_recv()
+    w_y.start()
+    attend(1)
+    head_rows(2, 0)
+    w_y.wait_recv()
+    w_z.start()
+    attend(2)
+    head_rows(3, 0)
     start(expert_load(0, 0))
-    for qb in range(4):
-        attend(qb)
+    attend(3)
+    dk_acc[...] = jnp.zeros_like(dk_acc)
+    dv_acc[...] = jnp.zeros_like(dv_acc)
+    norms[...] = jnp.zeros_like(norms)
 
     wait(late_load)
 
@@ -271,7 +292,7 @@
 
     lax.fori_loop(0, 4, mask_rows, 0)
 
-    w_x.wait_recv()
+    w_z.wait_recv()
     w_f.start()
     w_c.wait_recv()
     w_f.wait_recv()
@@ -299,48 +320,25 @@
         square = sum(jnp.sum(v * v, axis=1, keepdims=True) for v in sums)
         scale_r = lax.rsqrt(square * (1.0 / 1024.0) + EPSILON)
         for col in range(4):
-            acc[rows, 256 * col : 256 * col + 256] = sums[col]
+            buf[rows, 256 * col : 256 * col + 256] = sums[col]
             normed = sums[col] * scale_r * gain[0:1, 256 * col : 256 * col + 256]
             hbuf[rows, 256 * col : 256 * col + 256] = normed.astype(bf16)
             for half_c in range(2):
                 lhs[16 + 2 * col + half_c, :, rows] = normed[:, 128 * half_c : 128 * half_c + 128].T.astype(bf16)
         return carry
 
-    for b in range(4):
-        gather_x(b).wait_recv()
-        gather_f(b).start()
-    for b in range(4):
-        gather_c(b).wait_recv()
-        gather_f(b).wait_recv()
-        gather_f(b).wait_send()
-        gather_x(b).wait_send()
-        gather_c(b).wait_send()
-        forward_rows(b, 0)
-    w_x.wait_send()
-    w_c.wait_send()
-    w_f.wait_send()
-    keep = local(acc.at[:, wide], s_resid, iosem.at[0])
-    keep.start()
-    keep.wait()
-
-    def clear(b, carry):
-        acc[block(b, 64), :] = jnp.zeros((64, 1152), f32)
-        return carry
-
-    lax.fori_loop(0, 16, clear, 0)
-    dk_acc[...] = jnp.zeros_like(dk_acc)
-    dv_acc[...] = jnp.zeros_like(dv_acc)
-    norms[...] = jnp.zeros_like(norms)
-
-    def expert(e):
+    def expert(e, begin, count, first=False):
         s = e % 2
-        for copy in expert_load(e, s):
-            copy.wait()
-
-        @pl.when(e + 1 < EXPERTS)
-        def _():
-            for copy in expert_load(e + 1, 1 - s):
-                copy.start()
+
+        if not first:
+
+            @pl.when(begin == 0)
+            def _():
+                wait(expert_load(e, s))
+
+                @pl.when(e + 1 < EXPERTS)
+                def _():
+                    start(expert_load(e + 1, 1 - s))
 
         def rows_of(b, carry):
             rows = block(b)
@@ -357,16 +355,49 @@
             lhs[e, :, rows] = (hidden * weight).T.astype(bf16)
             inner = jnp.sum(hidden * d_raw, axis=1, keepdims=True)
             inner = jnp.where(weight > 0.0, inner, 0.0)
-            acc[rows, 1024:1152] = jnp.where(lane == e, inner, acc[rows, 1024:1152])
+            acc[rows, 1024:1152] = jnp.where(lane == e, inner, 0.0 if first else acc[rows, 1024:1152])
             d_hidden = d_raw * weight
             d_gate = (d_hidden * up * sigma * (1.0 + gate * (1.0 - sigma))).astype(bf16)
             d_up = (d_hidden * silu).astype(bf16)
             rhs[4 + e, rows, 0:LANES] = d_gate
             rhs[4 + e, rows, LANES:] = d_up
-            acc[rows, 0:1024] += dot_nt(rhs[4 + e, rows, :], wgu[s])
+            part = dot_nt(rhs[4 + e, rows, :], wgu[s])
+            acc[rows, 0:1024] = part if first else acc[rows, 0:1024] + part
             return carry
 
-        lax.fori_loop(0, 4, rows_of, 0)
+        if first:
+            rows_of(begin, 0)
+        else:
+            lax.fori_loop(begin, begin + count, rows_of, 0)
+
+    def forward_step(b, carry):
+        @pl.when(b < 4)
+        def _():
+            gather_x(b).wait_recv()
+            gather_f(b).start()
+
+        @pl.when(b > 0)
+        def _():
+            gather_c(b - 1).wait_recv()
+            gather_f(b - 1).wait_recv()
+            gather_f(b - 1).wait_send()
+            gather_x(b - 1).wait_send()
+            gather_c(b - 1).wait_send()
+            forward_rows(b - 1, 0)
+            expert(0, b - 1, 1, True)
+
+        return carry
+
+    for copy in (w_x, w_c, w_f, w_y, w_z):
+        copy.wait_send()
+    wait(expert_load(0, 0))
+    start(expert_load(1, 1))
+    lax.fori_loop(0, 5, forward_step, 0)
+    keep = local(buf.at[:, wide], s_resid, iosem.at[0])
+    keep.start()
+
+    def half_expert(u):
+        expert(u // 2 + 1, (u % 2) * 2, 2)
 
     mine = pl.ds(pl.multiple_of(core * 512, 512), 512)
     other = pl.ds(pl.multiple_of((1 - core) * 512, 512), 512)
@@ -416,6 +447,19 @@
     def sum_last(k):
         sum_c(k).wait_recv()
         sum_c(k).wait_send()
+
+    def norm_sum(step, dev):
+        return remote(norms.at[pl.ds(0, 16)], norm_in.at[step], ns.at[step], nr.at[step], dev)
+
+    partners = (mate, pair, far)
+
+    def norm_next(step):
+        if step > 0:
+            norm_sum(step - 1, partners[step - 1]).wait_recv()
+            norm_sum(step - 1, partners[step - 1]).wait_send()
+            norms[...] = norms[...] + norm_in[step - 1]
+        if step < 3:
+            norm_sum(step, partners[step]).start()
 
     def norm_back(values, scale_r, grads, which):
         inner = sum(
@@ -425,8 +469,10 @@
         outs = []
         for c, (v, g) in enumerate(zip(values, grads)):
             normed = v * scale_r
-            row = 4 * which + c
-            norms[row : row + 1, :] += jnp.sum(g * normed, axis=0, keepdims=True)
+            total = jnp.sum(g * normed, axis=0, keepdims=True)
+            row = 8 * which + 2 * c
+            norms[row : row + 1, :] += total[:, :LANES]
+            norms[row + 1 : row + 2, :] += total[:, LANES:]
             outs.append(scale_r * (g * gain[which : which + 1, 256 * c : 256 * c + 256] - normed * inner))
         return outs
 
@@ -449,8 +495,9 @@
             da2[h, rows, :] = d_head.astype(bf16)
 
     def turn_back(grad, cols):
-        sine = grad * sin_t[:, cols]
-        return grad * cos_t[:, cols] + jnp.concatenate([sine[32:], -sine[:32]], axis=0)
+        one, two = grad[:32], grad[32:]
+        cosine, sine = cos_t[:, cols], sin_t[:, cols]
+        return jnp.concatenate([one * cosine + two * sine, two * cosine - one * sine], axis=0)
 
     def attend_back(h, qb):
         keys = ROWS * (qb + 1)
@@ -534,7 +581,20 @@
     wo_load = [
         local(w_out.at[pl.ds(64 * h, 64)], wdb.at[h, pl.ds(64 * (h // 2), 64)], ld.at[8 + h]) for h in range(4)
     ]
-    dots_out = [local(acc.at[:, pl.ds(1024, LANES)], o_dots, iosem.at[7])]
+    dots_out = [local(d_pick, o_dots, iosem.at[7])]
+    norms_out = [
+        local(norms.at[pl.ds(0, 8)], o_norm0, iosem.at[2]),
+        local(norms.at[pl.ds(8, 8)], o_norm1, iosem.at[4]),
+    ]
+
+    def pick_dots():
+        for b in range(4):
+            rows = pl.ds(ROWS * b, ROWS)
+            dots = acc[rows, 1024:1152].T[:EXPERTS]
+            lane_e = lax.broadcasted_iota(jnp.int32, (EXPERTS, ROWS), 0)
+            for k in range(TOP_K):
+                mine_k = jnp.where(picks[k : k + 1, rows] == lane_e, dots, 0.0)
+                d_pick[k : k + 1, rows] = jnp.sum(mine_k, axis=0, keepdims=True)
     dres_out = [local(acc.at[:, wide], s_dres, iosem.at[8])]
     tokens_out = [local(hbuf, o_tokens, iosem.at[9])]
     result_out = [local(hbuf, o_result, iosem.at[10])]
@@ -548,11 +608,11 @@
             step()
 
     once = {
-        T_SUM1: lambda: do_all(lambda: sum_first(0), clear_wo, lambda: start(tokens_in + wo_load + proj_load)),
+        T_SUM1: lambda: do_all(keep.wait, lambda: sum_first(0), clear_wo, lambda: start(tokens_in + wo_load + proj_load)),
         T_SUM1 + 2: lambda: do_all(lambda: sum_second(0), lambda: wait(tokens_in)),
         T_MID1 - 3: lambda: sum_third(0),
         T_MID1 - 1: lambda: do_all(
-            lambda: sum_last(0), lambda: start(halves_in(s_resid) + dots_out), lambda: wait(wo_load)
+            lambda: sum_last(0), pick_dots, lambda: start(halves_in(s_resid) + dots_out), lambda: wait(wo_load)
         ),
         T_ATT: lambda: do_all(lambda: wait(dots_out), lambda: start(dres_out)),
         T_PROJ - 1: lambda: do_all(lambda: wait(dres_out), lambda: wait(proj_load)),
@@ -562,8 +622,11 @@
         T_TOK - 1: lambda: do_all(
             lambda: sum_last(1), lambda: start(halves_in(s_dres)), lambda: start([pair_load(0, 0)])
         ),
-        T_MOE: lambda: start(tokens_out),
-        T_SUM3: lambda: do_all(lambda: wait(tokens_out), lambda: sum_first(2)),
+        T_MOE: lambda: do_all(lambda: start(tokens_out), lambda: norm_next(0)),
+        T_MOE + 2: lambda: norm_next(1),
+        T_MOE + 4: lambda: norm_next(2),
+        T_MOE + 6: lambda: do_all(lambda: norm_next(3), lambda: start(norms_out)),
+        T_SUM3: lambda: do_all(lambda: wait(tokens_out + norms_out), lambda: sum_first(2)),
         T_SUM3 + 2: lambda: sum_second(2),
         T_RES - 3: lambda: sum_third(2),
         T_RES - 1: lambda: do_all(lambda: sum_last(2), lambda: start(halves_in(s_resid))),
@@ -578,7 +641,7 @@
         for when_t, src in halves_wait.items():
             pl.when(t == when_t)(lambda src=src: wait(halves_in(src)))
         for begin, count, fn in (
-            (0, EXPERTS, expert),
+            (0, 2 * EXPERTS - 2, half_expert),
             (T_MID1, 4, middle_rows),
             (T_TURN, 4, turn_rows),
             (T_PROJ, 4, project_rows),
@@ -587,9 +650,14 @@
             (T_RES, 4, result_rows),
         ):
             pl.when((t >= begin) & (t < begin + count))(lambda fn=fn, begin=begin: fn(t - begin))
-        for qb in range(4):
+        for pair_b in range(2):
             u = t - T_ATT
-            pl.when((u >= 0) & (u < 16) & (u % 4 == qb))(lambda qb=qb, u=u: attend_back(u // 4, qb))
+
+            def two(pair_b=pair_b, u=u):
+                attend_back(u // 2, pair_b)
+                attend_back(u // 2, 3 - pair_b)
+
+            pl.when((u >= 0) & (u < 8) & (u % 2 == pair_b))(two)
 
     own = pl.ds(pl.multiple_of(y * 64, 64), 64)
     oth = pl.ds(pl.multiple_of((1 - y) * 64, 64), 64)
@@ -646,13 +714,7 @@
             r_att = jnp.where(a < 16, 20 + a // 8, 22 + (a - 16) % 4)
             li = jnp.where(in_moe, l_moe, l_att)
             ri = jnp.where(in_moe, r_moe, r_att)
-            @pl.when(i < N_CLASS - 1)
-            def _():
-                pbuf[c, s] = dot_f(lhs[jnp.minimum(li, 33)], rhs[jnp.minimum(ri, 25)])
-
-            @pl.when(i == N_CLASS - 1)
-            def _():
-                pbuf[c, s] = norms[...]
+            pbuf[c, s] = dot_f(lhs[li], rhs[ri])
 
             @pl.when(kind % 2 == 0)
             def _():
@@ -792,11 +854,7 @@
                 rows = pl.ds(pl.multiple_of((a - 8) * 128, 128), 128)
                 store(s, o_k.at[rows], o_v.at[rows])
 
-            @pl.when(i == N_CLASS - 1)
-            def _():
-                store(s, o_norm.at[c, :, pl.ds(0, 128)], o_norm.at[c, :, pl.ds(128, 128)])
-
-            @pl.when((a >= 16) & (a < 24))
+            @pl.when(a >= 16)
             def _():
                 b = a - 16
                 rows = pl.ds(pl.multiple_of((b // 4) * 128, 128), 128)
@@ -874,8 +932,8 @@
 
     outs = [
         out((16, 1024, 128)), out((16, 1024, 128)), out((16, 128, 1024)),
-        out((1024, 256)), out((1024, 128)), out((1024, 128)), out((256, 1024)), out((2, 128, 256)),
-        out((1024, 1024), bf16), out((1024, 1024), bf16), out((1024, 128)),
+        out((1024, 256)), out((1024, 128)), out((1024, 128)), out((256, 1024)), out((8, 128)), out((8, 128)),
+        out((1024, 1024), bf16), out((1024, 1024), bf16), out((8, 1024)),
         out((1024, 1024)), out((1024, 1024)),
     ]
     anywhere = pl.BlockSpec(memory_space=pl.ANY)
@@ -894,23 +952,25 @@
             vmem((1024, 1024), bf16), vmem((2, 1024, 256), bf16), vmem((4, 128, 1024), bf16),
             vmem((4, 1024, 128), bf16), vmem((1024, 128), bf16), vmem((1024, 128), bf16),
             vmem((128, 1024), bf16), vmem((128, 1024), bf16),
-            vmem((8, 1024), f32), vmem((64, 1024), f32), vmem((64, 1024), f32),
+            vmem((8, 1024), f32), vmem((32, 1024), f32), vmem((32, 1024), f32),
             vmem((4, 1024, 128), bf16), vmem((1024, 128), f32), vmem((1024, 128), f32),
-            vmem((1024, 128), f32), vmem((8, 1024), f32), vmem((128, 256), f32),
+            vmem((1024, 128), f32), vmem((8, 1024), f32), vmem((16, 128), f32),
             vmem((8, 1024), jnp.int32), vmem((8, 1024), f32),
+            vmem((3, 16, 128), f32), vmem((8, 1024), f32),
             dma((18,)), dma((2, 3)), dma((11,)),
         ]
         + [dma((2, ring))] * 10
         + [dma((2, SPARE))]
         + [dma((4,))] * 6
-        + [dma((3,))] * 2
+        + [dma((5,))] * 2
         + [dma((3,))] * 6
-        + [reg((3,))] * 3,
+        + [reg((3,))] * 3
+        + [dma((3,))] * 2,
         compiler_params=pltpu.CompilerParams(
             collective_id=0, has_side_effects=True, vmem_limit_bytes=63 * 2**20
         ),
     )(*operands)
-    sums, rest = tuple(res[:8]), res[8:11]
+    sums, rest = tuple(res[:9]), res[9:12]
     if groups > 2 * nz:
         same = [
             [2 * nz * block + place for block in range(groups // (2 * nz))] for place in range(2 * nz)
@@ -957,19 +1017,17 @@
         w_key,
         w_value,
     )
-    grad_gate, grad_up, grad_down, grad_query, grad_key, grad_value, grad_out, norm_rows = sums
-    picked = chosen[:, :, None] == jnp.arange(EXPERTS, dtype=jnp.int32)[None, None, :]
-    d_gates = jnp.sum(jnp.where(picked, dots[:, None, :EXPERTS], 0.0), axis=-1)
+    grad_gate, grad_up, grad_down, grad_query, grad_key, grad_value, grad_out, grad_norm_moe, grad_norm_attn = sums
     return (
         result,
         grad_tokens,
-        d_gates,
-        norm_rows[0, 4:8].reshape(-1),
+        dots.T,
+        grad_norm_attn.reshape(-1),
         grad_query,
         grad_key,
         grad_value,
         grad_out,
-        norm_rows[0, 0:4].reshape(-1),
+        grad_norm_moe.reshape(-1),
         grad_gate,
         grad_up,
         grad_down,

time: 569 us -> 538 us (0.946)
  Pallas kernels: 541 us -> 512 us
    pallas_call x1, Pallas kernels: 541 us -> 512 us  [run_layer(): pl.pallas_call(functools.partial(layer_kernel, nz, hop, ring), out_shape=...]
    unnamed x32 -> x38, local copies, waits for them, and re-layouts: 25.2 us -> 24.2 us
where the time goes in v6:
time: 538 us; the launch traced here: 537 us
  Pallas kernels  512 us (95%)
  local copies, waits for them, and re-layouts  24.2 us (4%)
    pallas_call x1, Pallas kernels, run_layer(): pl.pallas_call(functools.partial(layer_kernel, nz, hop, ring), out_shape=...  512 us
    unnamed x38, local copies, waits for them, and re-layouts  24.2 us

profile of v6, /device:TPU:0, one launch (start us, length us, event | category | flops | bytes accessed | tf_op | source)
XLA Modules:
  0.0 537.3 jit_solution(17403242728010574381)
XLA Ops:
  1.3 511.8 %shard_map.247 = (f32[16,1024,128]{2,1,0:T(8,128)}, f32[16,1024,128]{2,1,0:T(8,128)}, f32[16,128,1024]{2,1,0:T(8,128)}, f32[1024,256]{1,0:T(8,128)}, f32[1024,12...) custom-call(s32[1]{0:T(128)S(6)} %copy.40.length, ...), custom_call_target="tpu_custom_call" | custom-call | tf_op jit(solution)/shard_map/pallas_call | solution.py:943
  513.1 0.0 copy-start.1
  513.1 0.0 copy-start.6
  513.1 0.0 copy-start.8
  513.1 0.0 copy-start.3
  513.1 0.0 copy-start.5
  513.2 0.0 copy-start.4
  513.2 0.0 copy-start.2
  513.2 3.2 copy.41
  516.4 0.0 copy-done.1
  516.4 0.0 copy-start
  516.4 1.3 copy.42
  517.7 0.0 copy-done.6
  517.7 0.0 copy-start.7
  517.7 0.6 copy.43
  518.4 0.0 copy-done.8
  518.4 0.6 copy.44
  519.0 0.0 copy-done.3
  519.0 1.0 copy.45
  519.9 0.0 copy-done.5
  519.9 0.8 copy.46
  520.7 0.0 copy-done.4
  520.7 0.0 slice-start.2
  520.7 0.8 copy.47
  521.5 0.0 copy-done.2
  521.5 1.0 copy.48
  522.5 0.0 copy-done.7
  522.5 0.6 copy.49
  523.1 0.0 copy-done
  523.1 0.0 slice-start.3
  523.1 0.0 slice-start
  523.1 4.3 copy.50
  527.4 0.0 slice-done.2
  527.4 1.0 slice-done.3
  528.3 0.0 slice-start.1
  528.3 4.3 copy.51
  532.6 0.0 slice-done
  532.6 1.4 slice-done.1
  534.0 3.4 copy.52
  (2 shorter events, 0.0 us)
Async XLA Ops:
  513.1 3.3 copy-start.1
  513.1 4.6 copy-start.6
  513.1 5.2 copy-start.8
  513.1 5.8 %copy-start.3 = (f32[1024,256]{1,0:T(8,128)S(1)}, f32[1024,256]{1,0:T(8,128)}, u32[]{:S(2)}) copy-start(f32[1024,256]{1,0:T(8,128)} %get-tuple-element.52) | copy-start | bytes 3145732
  513.1 6.8 %copy-start.5 = (f32[1024,128]{1,0:T(8,128)S(1)}, f32[1024,128]{1,0:T(8,128)}, u32[]{:S(2)}) copy-start(f32[1024,128]{1,0:T(8,128)} %get-tuple-element.53) | copy-start | bytes 1572868
  513.2 7.6 %copy-start.4 = (f32[1024,128]{1,0:T(8,128)S(1)}, f32[1024,128]{1,0:T(8,128)}, u32[]{:S(2)}) copy-start(f32[1024,128]{1,0:T(8,128)} %get-tuple-element.54) | copy-start | bytes 1572868
  513.2 8.4 %copy-start.2 = (f32[256,1024]{1,0:T(8,128)S(1)}, f32[256,1024]{1,0:T(8,128)}, u32[]{:S(2)}) copy-start(f32[256,1024]{1,0:T(8,128)} %get-tuple-element.55) | copy-start | bytes 3145732
  516.4 6.7 %copy-start = (f32[16,1024,128]{2,1,0:T(8,128)S(1)}, f32[16,1024,128]{2,1,0:T(8,128)}, u32[]{:S(2)}) copy-start(f32[16,1024,128]{2,1,0:T(8,128)} %get-tuple-element.57) | copy-start | bytes 25165828
  517.7 4.8 copy-start.7
  520.7 6.6 %slice-start.2 = ((s8[8388608]{0:T(1024)(128)(4,1)}), s8[4194304]{0:T(1024)(128)(4,1)S(1)}, s32[]{:S(2)}) async-start(s8[8388608]{0:T(1024)(128)(4,1)} %bitcast.9), calls=%async_computation.2 | async-start | bytes 8388608
  523.1 5.2 slice-start.3
  523.1 9.5 %slice-start = ((s8[8388608]{0:T(1024)(128)(4,1)}), s8[4194304]{0:T(1024)(128)(4,1)S(1)}, s32[]{:S(2)}) async-start(s8[8388608]{0:T(1024)(128)(4,1)} %bitcast.7), calls=%async_computation | async-start | bytes 8388608
  528.3 5.6 %slice-start.1 = ((s8[8388608]{0:T(1024)(128)(4,1)}), s8[4194304]{0:T(1024)(128)(4,1)S(1)}, s32[]{:S(2)}) async-start(s8[8388608]{0:T(1024)(128)(4,1)} %bitcast.7), calls=%async_computation.1 | async-start | bytes 8388608

commit v7 on v6

--- a/solution.py
+++ b/solution.py
@@ -34,19 +34,21 @@
 
 LANES = 128
 ROWS = 256
-N_CLASS = 108
+CHUNK = 64
+N_EXPERT = 96
+N_CLASS = 120
 HOP = 2
-SPARE = 3
+HALF = EXPERTS // 2
 T_SUM1 = 30
-T_MID1 = 47
-T_ATT = 51
-T_TURN = 59
-T_PROJ = 63
-T_SUM2 = 67
-T_TOK = 84
-T_MOE = 88
-T_SUM3 = 96
-T_RES = 113
+T_MID1 = 52
+T_ATT = 56
+T_TURN = 64
+T_PROJ = 68
+T_SUM2 = 72
+T_TOK = 92
+T_MOE = 96
+T_SUM3 = 104
+T_RES = 124
 
 
 def dot_nt(left, right):
@@ -66,10 +68,11 @@
     length, x_in, d_out, chosen, gates, gain_attn, gain_moe, w_gate, w_up, w_down,
     cos_in, sin_in, w_out, w_query, w_key, w_value,
     o_gate, o_up, o_down, o_q, o_k, o_v, o_out, o_norm0, o_norm1, o_result, o_tokens, o_dots, s_resid, s_dres,
-    lhs, rhs, pbuf, zbuf, ybuf, xbuf, acc, buf, hbuf, wgu, wdb, q2, k2, v2, kt2, vt2, lse, cos_t, sin_t,
-    da2, dk_acc, dv_acc, slot_w, gain, norms, picks, pick_w, norm_in, d_pick,
-    ld, wsem, iosem, ys, yr, zs, zr, fs, fr, gs, gr, os0, os1, xr,
-    cs_c, cr_c, cs_x, cr_x, cs_f, cr_f, ws, wr, s1s, s1r, s2s, s2r, s3s, s3r, ready1, ready2, ready3, ns, nr,
+    lhs, rhs, pbuf, zbuf, ybuf, acc, buf, hbuf, wgu, wdb, q2, k2, v2, kt2, vt2, lse, cos_t, sin_t,
+    da2, dk_acc, dv_acc, slot_w, gain, norms, picks, pick_w, norm_in, d_pick, kept_out, kept_in, slot_m,
+    ld, wsem, iosem, ys, yr, zs, zr, fs, fr, gs, gr, os0, os1,
+    cs_c, cr_c, cs_x, cr_x, cs_f, cr_f, ws, wr, s1s, s1r, s2s, s2r, s3s, s3r, ready1, ready2, ready3, ns, nr, go,
+    hys, hyr, hcs, hcr, hxs, hxr, hfs, hfr, dys, dyr, dcs, dcr, dxs, dxr, dfs, dfr, ks, kr,
 ):
     f32, bf16 = jnp.float32, jnp.bfloat16
     dp = lax.axis_index("dp")
@@ -123,7 +126,7 @@
         local(w_key, wgu.at[1, :, pl.ds(0, LANES)], ld.at[6]),
         local(w_value, wgu.at[1, :, pl.ds(LANES, LANES)], ld.at[7]),
     ]
-    out_load = [local(w_out.at[:, block(c)], rhs.at[22 + c, share], ld.at[8 + c]) for c in range(4)]
+    out_load = [local(w_out.at[:, block(c)], rhs.at[26 + c, share], ld.at[8 + c]) for c in range(4)]
     late_load = [local(d_out.at[:, block(c)], rhs.at[c], ld.at[12 + c]) for c in range(4)] + [
         local(chosen, picks, ld.at[16]),
         local(gates, pick_w, ld.at[17]),
@@ -161,7 +164,7 @@
     w_f = remote(part_f, part_f, ws.at[2], wr.at[2], core_mate, "tensor")
     wait(out_load)
     for c in range(4):
-        buf[share, 256 * c : 256 * c + 256] = rhs[22 + c, share, :].astype(f32)
+        buf[share, 256 * c : 256 * c + 256] = rhs[26 + c, share, :].astype(f32)
     w_x.start()
     w_c.start()
 
@@ -245,6 +248,95 @@
         gather_x(qb).start()
         gather_c(qb).start()
 
+    def mask_rows(b, carry):
+        rows = block(b)
+        pos = lax.broadcasted_iota(jnp.int32, (ROWS, 256), 0) + b * ROWS
+        for c in range(4):
+            rhs[c, rows, :] = jnp.where(pos < length[0], rhs[c, rows, :].astype(f32), 0.0).astype(bf16)
+        return carry
+
+    near_d = [2 * tensor + j for j in range(2)]
+    direct_d = [8 + 4 * core + j for j in range(4)]
+
+    def slab(k):
+        return pl.ds(pl.multiple_of(4 * k, 4), 4)
+
+    def d_copy(k, sends, recvs, dev, axis, src=None):
+        return remote((ybuf if src is None else src).at[slab(k)], ybuf.at[slab(k)], sends.at[k], recvs.at[k], dev, axis)
+
+    def d_y(k):
+        return d_copy(k, dys, dyr, mate, "dp", pbuf)
+
+    def d_c(k):
+        return d_copy(k, dcs, dcr, core_mate, "tensor")
+
+    def d_x(k):
+        return d_copy(k, dxs, dxr, x_mate, "tensor")
+
+    def d_f(k):
+        return d_copy(k, dfs, dfr, core_mate, "tensor")
+
+    def stage_d(k):
+        rows = block(k, 64)
+        for c in range(4):
+            pbuf[4 * k + c] = rhs[c, rows, :].astype(f32)
+        d_y(k).start()
+
+    def h_piece(b, t):
+        return 4 * b + t
+
+    def h_copy(b, t, sends, recvs, dev, axis):
+        part = zbuf.at[slab(h_piece(b, t))]
+        return remote(part, part, sends.at[b], recvs.at[b], dev, axis)
+
+    def h_stage(b):
+        return 2 * x_mate + b if isinstance(b, int) and b < 2 else 2 * jnp.where(b < 2, x_mate, core_mate) + b % 2
+
+    def h_y(b):
+        return remote(
+            pbuf.at[slab(h_stage(b))], zbuf.at[slab(h_piece(b, tensor))], hys.at[b], hyr.at[b], mate
+        )
+
+    def h_c(b):
+        return h_copy(b, tensor, hcs, hcr, core_mate, "tensor")
+
+    def h_x(b):
+        return h_copy(b, tensor, hxs, hxr, x_mate, "tensor")
+
+    def h_f(b):
+        return h_copy(b, x_mate, hfs, hfr, core_mate, "tensor")
+
+    def h_send(b):
+        rows = pl.ds(pl.multiple_of(b * 256 + tensor * 64, 64), 64)
+        for c in range(4):
+            pbuf[4 * h_stage(b) + c] = hbuf[rows, 256 * c : 256 * c + 256].astype(f32)
+        h_y(b).start()
+
+    def h_share(b):
+        h_y(b).wait_recv()
+        h_x(b).start()
+        h_c(b).start()
+
+    def h_forward(b):
+        h_x(b).wait_recv()
+        h_f(b).start()
+
+    def d_share(j):
+        k = near_d[j]
+        d_y(k).wait_recv()
+        d_x(k).start()
+        d_c(k).start()
+
+    def d_forward(j):
+        k = 2 * x_mate + j
+        d_x(k).wait_recv()
+        d_f(k).start()
+
+    def d_direct(j):
+        k = direct_d[j]
+        d_y(k).wait_recv()
+        d_c(k).start()
+
     wait(token_load + proj_load)
     head_rows(0, 0)
     attend(0)
@@ -255,15 +347,20 @@
     head_rows(2, 0)
     w_y.wait_recv()
     w_z.start()
+    wait(late_load)
+    lax.fori_loop(0, 4, mask_rows, 0)
+    for j in range(2):
+        stage_d(near_d[j])
+    for j in range(2):
+        stage_d(direct_d[j])
     attend(2)
     head_rows(3, 0)
-    start(expert_load(0, 0))
+    start(expert_load(8 * y, 0))
     attend(3)
     dk_acc[...] = jnp.zeros_like(dk_acc)
     dv_acc[...] = jnp.zeros_like(dv_acc)
     norms[...] = jnp.zeros_like(norms)
 
-    wait(late_load)
 
     expert_id = lax.broadcasted_iota(jnp.int32, (EXPERTS, 1024), 0)
     alive = lax.broadcasted_iota(jnp.int32, (EXPERTS, 1024), 1) < length[0]
@@ -281,16 +378,11 @@
         earlier = jnp.where(lax.broadcasted_iota(jnp.int32, (1024, ROWS), 0) < token, 1.0, 0.0).astype(bf16)
         places = dot_f(hits, earlier)
         kept = jnp.where(places < limit, weight[:, ROWS * b : ROWS * b + ROWS], 0.0)
+        kept_out[:, rows] = kept
         slot_w[rows, :] = jnp.concatenate([kept, jnp.zeros((LANES - EXPERTS, ROWS), f32)], axis=0).T
 
-    def mask_rows(b, carry):
-        rows = block(b)
-        pos = lax.broadcasted_iota(jnp.int32, (ROWS, 256), 0) + b * ROWS
-        for c in range(4):
-            rhs[c, rows, :] = jnp.where(pos < length[0], rhs[c, rows, :].astype(f32), 0.0).astype(bf16)
-        return carry
-
-    lax.fori_loop(0, 4, mask_rows, 0)
+    kept_copy = remote(kept_out, kept_in, ks.at[0], kr.at[0], mate)
+    kept_copy.start()
 
     w_z.wait_recv()
     w_f.start()
@@ -299,7 +391,7 @@
 
     def cast_out(b, carry):
         for c in range(4):
-            rhs[22 + c, block(b, 64), :] = buf[block(b, 64), 256 * c : 256 * c + 256].astype(bf16)
+            rhs[26 + c, block(b, 64), :] = buf[block(b, 64), 256 * c : 256 * c + 256].astype(bf16)
         return carry
 
     lax.fori_loop(0, 16, cast_out, 0)
@@ -310,12 +402,12 @@
             part = acc[rows, 256 * k : 256 * k + 256].astype(bf16)
             if k == 0:
                 sums = [
-                    hbuf[rows, 256 * col : 256 * col + 256].astype(f32) + dot_f(part, rhs[22 + col, 0:256, :])
+                    hbuf[rows, 256 * col : 256 * col + 256].astype(f32) + dot_f(part, rhs[26 + col, 0:256, :])
                     for col in range(4)
                 ]
             else:
                 sums = [
-                    sums[col] + dot_f(part, rhs[22 + col, 256 * k : 256 * k + 256, :]) for col in range(4)
+                    sums[col] + dot_f(part, rhs[26 + col, 256 * k : 256 * k + 256, :]) for col in range(4)
                 ]
         square = sum(jnp.sum(v * v, axis=1, keepdims=True) for v in sums)
         scale_r = lax.rsqrt(square * (1.0 / 1024.0) + EPSILON)
@@ -327,48 +419,66 @@
                 lhs[16 + 2 * col + half_c, :, rows] = normed[:, 128 * half_c : 128 * half_c + 128].T.astype(bf16)
         return carry
 
-    def expert(e, begin, count, first=False):
-        s = e % 2
-
-        if not first:
-
-            @pl.when(begin == 0)
-            def _():
-                wait(expert_load(e, s))
-
-                @pl.when(e + 1 < EXPERTS)
-                def _():
-                    start(expert_load(e + 1, 1 - s))
-
-        def rows_of(b, carry):
-            rows = block(b)
+    def expert_of(k):
+        return jnp.where(k < 16, 8 * y + k % 8, 8 * (1 - y) + k % 8)
+
+    def next_weights(k):
+        wait(expert_load(expert_of(k), k % 2))
+
+        @pl.when(k < 23)
+        def _():
+            start(expert_load(expert_of(k + 1), (k + 1) % 2))
+
+    def unit(k, b, kind):
+        rows = block(b)
+        s = k % 2
+        e = expert_of(k)
+        el = k % 8
+        if kind == "mate":
+            both = dot_f(rhs[26, rows, :], wgu[s, 0:256, :])
+            for c in range(1, 4):
+                both = both + dot_f(rhs[26 + c, rows, :], wgu[s, 256 * c : 256 * c + 256, :])
+        else:
             both = dot_f(hbuf[rows, :], wgu[s])
-            gate, up = both[:, :LANES], both[:, LANES:]
-            d_raw = dot_nt(rhs[0, rows, :], wdb[s, :, 0:256])
-            for col in range(1, 4):
-                d_raw = d_raw + dot_nt(rhs[col, rows, :], wdb[s, :, 256 * col : 256 * col + 256])
-            lane = lax.broadcasted_iota(jnp.int32, (ROWS, LANES), 1)
-            weight = jnp.sum(jnp.where(lane == e, slot_w[rows, :], 0.0), axis=1, keepdims=True)
-            sigma = 1.0 / (1.0 + jnp.exp(-gate))
-            silu = gate * sigma
-            hidden = silu * up
-            lhs[e, :, rows] = (hidden * weight).T.astype(bf16)
-            inner = jnp.sum(hidden * d_raw, axis=1, keepdims=True)
-            inner = jnp.where(weight > 0.0, inner, 0.0)
-            acc[rows, 1024:1152] = jnp.where(lane == e, inner, 0.0 if first else acc[rows, 1024:1152])
-            d_hidden = d_raw * weight
-            d_gate = (d_hidden * up * sigma * (1.0 + gate * (1.0 - sigma))).astype(bf16)
-            d_up = (d_hidden * silu).astype(bf16)
-            rhs[4 + e, rows, 0:LANES] = d_gate
-            rhs[4 + e, rows, LANES:] = d_up
-            part = dot_nt(rhs[4 + e, rows, :], wgu[s])
-            acc[rows, 0:1024] = part if first else acc[rows, 0:1024] + part
+        d_base = 12 if kind == "mate" else 0
+        gate, up = both[:, :LANES], both[:, LANES:]
+        d_raw = dot_nt(rhs[d_base, rows, :], wdb[s, :, 0:256])
+        for c in range(1, 4):
+            d_raw = d_raw + dot_nt(rhs[d_base + c, rows, :], wdb[s, :, 256 * c : 256 * c + 256])
+        lane = lax.broadcasted_iota(jnp.int32, (ROWS, LANES), 1)
+        weights = slot_m if kind == "mate" else slot_w
+        weight = jnp.sum(jnp.where(lane == e, weights[rows, :], 0.0), axis=1, keepdims=True)
+        sigma = 1.0 / (1.0 + jnp.exp(-gate))
+        silu = gate * sigma
+        hidden = silu * up
+        hidden_t = (hidden * weight).T.astype(bf16)
+        d_hidden = d_raw * weight
+        d_gate = (d_hidden * up * sigma * (1.0 + gate * (1.0 - sigma))).astype(bf16)
+        d_up = (d_hidden * silu).astype(bf16)
+        if kind == "mate":
+            lhs[42 + el, :, rows] = hidden_t
+            rhs[16 + el, rows, 0:LANES] = d_gate
+            rhs[16 + el, rows, LANES:] = d_up
+            return
+        lhs[e, :, rows] = hidden_t
+        inner = jnp.sum(hidden * d_raw, axis=1, keepdims=True)
+        inner = jnp.where(weight > 0.0, inner, 0.0)
+        is_first = kind == "first"
+        acc[rows, 1024:1152] = jnp.where(lane == e, inner, 0.0 if is_first else acc[rows, 1024:1152])
+        if kind == "other":
+            part = dot_nt(jnp.concatenate([d_gate, d_up], axis=1), wgu[s])
+        else:
+            rhs[4 + el, rows, 0:LANES] = d_gate
+            rhs[4 + el, rows, LANES:] = d_up
+            part = dot_nt(rhs[4 + el, rows, :], wgu[s])
+        acc[rows, 0:1024] = part if is_first else acc[rows, 0:1024] + part
+
+    def units(k, begin, count, kind):
+        def step(b, carry):
+            unit(k, b, kind)
             return carry
 
-        if first:
-            rows_of(begin, 0)
-        else:
-            lax.fori_loop(begin, begin + count, rows_of, 0)
+        lax.fori_loop(begin, begin + count, step, 0)
 
     def forward_step(b, carry):
         @pl.when(b < 4)
@@ -384,20 +494,133 @@
             gather_x(b - 1).wait_send()
             gather_c(b - 1).wait_send()
             forward_rows(b - 1, 0)
-            expert(0, b - 1, 1, True)
+            h_send(b - 1)
+            unit(0, b - 1, "first")
+
+        @pl.when(b == 4)
+        def _():
+            d_share(0)
+            d_share(1)
+            stage_d(direct_d[2])
+            stage_d(direct_d[3])
 
         return carry
 
     for copy in (w_x, w_c, w_f, w_y, w_z):
         copy.wait_send()
-    wait(expert_load(0, 0))
-    start(expert_load(1, 1))
+    next_weights(0)
     lax.fori_loop(0, 5, forward_step, 0)
     keep = local(buf.at[:, wide], s_resid, iosem.at[0])
     keep.start()
 
-    def half_expert(u):
-        expert(u // 2 + 1, (u % 2) * 2, 2)
+    chores = {
+        5: [(h_share, 0)],
+        8: [(d_direct, 0), (d_direct, 1)],
+        11: [(h_share, 1)],
+        13: [(h_forward, 0), (d_forward, 0)],
+        16: [(h_share, 2), (d_forward, 1)],
+        20: [(h_forward, 1)],
+        23: [(h_share, 3)],
+        26: [(h_forward, 2)],
+        29: [(d_direct, 2)],
+        31: [(h_forward, 3), (d_direct, 3)],
+    }
+
+    def own_unit(u, carry):
+        k = u // 4
+
+        @pl.when(u % 4 == 0)
+        def _():
+            next_weights(k)
+
+        unit(k, u % 4, "own")
+        for when_u, jobs in chores.items():
+
+            @pl.when(u == when_u)
+            def _(jobs=jobs):
+                for job, arg in jobs:
+                    job(arg)
+
+        return carry
+
+    lax.fori_loop(4, 32, own_unit, 0)
+
+    kept_copy.wait_recv()
+    for b in range(4):
+        rows = pl.ds(ROWS * b, ROWS)
+        slot_m[rows, :] = jnp.concatenate(
+            [kept_in[:, rows], jnp.zeros((LANES - EXPERTS, ROWS), f32)], axis=0
+        ).T
+    other_core = tensor - core + (1 - core)
+    for j in range(2):
+        d_c(2 * other_core + j).wait_recv()
+        d_f(2 * (3 - tensor) + j).wait_recv()
+    for j in range(4):
+        d_c(8 + 4 * (1 - core) + j).wait_recv()
+    for b in range(4):
+        h_c(b).wait_recv()
+        h_f(b).wait_recv()
+
+    def take_d(k, carry):
+        for c in range(4):
+            rhs[12 + c, block(k, 64), :] = ybuf[4 * k + c].astype(bf16)
+        return carry
+
+    def take_h(b, carry):
+        rows = block(b)
+        for c in range(4):
+            whole = jnp.concatenate([zbuf[4 * (4 * b + t) + c] for t in range(4)], axis=0)
+            rhs[26 + c, rows, :] = whole.astype(bf16)
+            for half_c in range(2):
+                lhs[34 + 2 * c + half_c, :, rows] = whole[:, 128 * half_c : 128 * half_c + 128].T.astype(bf16)
+        return carry
+
+    lax.fori_loop(0, 16, take_d, 0)
+    lax.fori_loop(0, 4, take_h, 0)
+    next_weights(8)
+    units(8, 0, 4, "mate")
+    kept_copy.wait_send()
+    for j in range(2):
+        d_y(near_d[j]).wait_send()
+        d_x(near_d[j]).wait_send()
+        d_c(near_d[j]).wait_send()
+        d_f(2 * x_mate + j).wait_send()
+    for j in range(4):
+        d_y(direct_d[j]).wait_send()
+        d_c(direct_d[j]).wait_send()
+    for b in range(4):
+        h_y(b).wait_send()
+        h_x(b).wait_send()
+        h_c(b).wait_send()
+        h_f(b).wait_send()
+
+    pl.semaphore_signal(go, inc=1, device_id={"dp": mate}, device_id_type=MESH)
+
+    @pl.when(z < last)
+    def _():
+        pl.semaphore_signal(go, inc=1, device_id={"dp": up_id}, device_id_type=MESH)
+
+    @pl.when(z > 0)
+    def _():
+        pl.semaphore_signal(go, inc=1, device_id={"dp": dn_id}, device_id_type=MESH)
+
+    pl.semaphore_wait(go, 1 + (z < last).astype(jnp.int32) + (z > 0).astype(jnp.int32))
+
+    def half_pass(u):
+        k = 9 + u // 2
+        begin = (u % 2) * 2
+
+        @pl.when(begin == 0)
+        def _():
+            next_weights(k)
+
+        @pl.when(k < 16)
+        def _():
+            units(k, begin, 2, "mate")
+
+        @pl.when(k >= 16)
+        def _():
+            units(k, begin, 2, "other")
 
     mine = pl.ds(pl.multiple_of(core * 512, 512), 512)
     other = pl.ds(pl.multiple_of((1 - core) * 512, 512), 512)
@@ -487,11 +710,11 @@
         for c in range(4):
             total = rhs[c, rows, :].astype(f32) + back[c]
             acc[rows, 256 * c : 256 * c + 256] = total
-            rhs[22 + c, rows, :] = total.astype(bf16)
+            rhs[26 + c, rows, :] = total.astype(bf16)
         for h in range(4):
-            d_head = dot_nt(rhs[22, rows, :], wdb[h, :, 0:256])
+            d_head = dot_nt(rhs[26, rows, :], wdb[h, :, 0:256])
             for c in range(1, 4):
-                d_head = d_head + dot_nt(rhs[22 + c, rows, :], wdb[h, :, 256 * c : 256 * c + 256])
+                d_head = d_head + dot_nt(rhs[26 + c, rows, :], wdb[h, :, 256 * c : 256 * c + 256])
             da2[h, rows, :] = d_head.astype(bf16)
 
     def turn_back(grad, cols):
@@ -516,15 +739,15 @@
 
     def turn_rows(b):
         rows = block(b)
-        rhs[20, rows, :] = buf[0:256, rows].T.astype(bf16)
+        rhs[24, rows, :] = buf[0:256, rows].T.astype(bf16)
         d_k = (dk_acc[rows, :] * scaling).T
         d_k = jnp.concatenate([turn_back(d_k[:64], rows), turn_back(d_k[64:], rows)], axis=0)
-        rhs[21, rows, 0:LANES] = d_k.T.astype(bf16)
-        rhs[21, rows, LANES:] = dv_acc[rows, :].astype(bf16)
+        rhs[25, rows, 0:LANES] = d_k.T.astype(bf16)
+        rhs[25, rows, LANES:] = dv_acc[rows, :].astype(bf16)
 
     def project_rows(b):
         rows = block(b)
-        acc[rows, 0:1024] = dot_nt(rhs[20, rows, :], wgu[0]) + dot_nt(rhs[21, rows, :], wgu[1])
+        acc[rows, 0:1024] = dot_nt(rhs[24, rows, :], wgu[0]) + dot_nt(rhs[25, rows, :], wgu[1])
 
     def token_rows(b):
         rows = block(b)
@@ -641,7 +864,7 @@
         for when_t, src in halves_wait.items():
             pl.when(t == when_t)(lambda src=src: wait(halves_in(src)))
         for begin, count, fn in (
-            (0, 2 * EXPERTS - 2, half_expert),
+            (0, 30, half_pass),
             (T_MID1, 4, middle_rows),
             (T_TURN, 4, turn_rows),
             (T_PROJ, 4, project_rows),
@@ -659,9 +882,10 @@
 
             pl.when((u >= 0) & (u < 8) & (u % 2 == pair_b))(two)
 
-    own = pl.ds(pl.multiple_of(y * 64, 64), 64)
-    oth = pl.ds(pl.multiple_of((1 - y) * 64, 64), 64)
-    half = pl.ds(0, 64)
+    own = pl.ds(pl.multiple_of(y * 32, 32), 32)
+    oth = pl.ds(pl.multiple_of((1 - y) * 32, 32), 32)
+    half = pl.ds(0, 32)
+    upper = pl.ds(32, 32)
 
     def stage(c, t):
         p = z if c == 0 else last - z
@@ -671,72 +895,75 @@
 
             @pl.when((i >= 0) & (i < N_CLASS))
             def _():
-                body(i, i % ring, i % 5)
+                s = c * ring + i % ring
+                body(i, s, i < N_EXPERT, (i >= N_EXPERT) & (i % 2 == 0), (i >= N_EXPERT) & (i % 2 == 1))
 
         def ycopy_a(s):
-            return remote(pbuf.at[c, s, oth], ybuf.at[c, s, half], ys.at[c, s], yr.at[c, s], mate)
+            return remote(pbuf.at[s, oth], ybuf.at[s, half], ys.at[s], yr.at[s], mate)
 
         def ycopy_b(s):
-            return remote(zbuf.at[c, s], ybuf.at[c, s], ys.at[c, s], yr.at[c, s], mate)
-
-        def ycopy_c(s, k):
-            return remote(zbuf.at[c, s], xbuf.at[c, k], ys.at[c, s], xr.at[c, k], mate)
-
-        def leaf_copy(s):
-            return remote(pbuf.at[c, s], ybuf.at[c, s], ys.at[c, s], yr.at[c, s], prv)
-
-        def fcopy_c(s):
-            return remote(pbuf.at[c, s], zbuf.at[c, s], gs.at[c, s], fr.at[c, s], nxt)
+            return remote(zbuf.at[s], ybuf.at[s], ys.at[s], yr.at[s], mate)
 
         def zcopy_a(s):
-            return remote(zbuf.at[c, s, half], zbuf.at[c, s, half], zs.at[c, s], zr.at[c, s], nxt)
-
-        def zcopy_b(s):
-            return remote(zbuf.at[c, s], zbuf.at[c, s], zs.at[c, s], zr.at[c, s], nxt)
+            return remote(zbuf.at[s, half], zbuf.at[s, half], zs.at[s], zr.at[s], nxt)
+
+        def zcopy(s):
+            return remote(zbuf.at[s], zbuf.at[s], zs.at[s], zr.at[s], nxt)
 
         def fcopy_a(s):
-            return remote(pbuf.at[c, s, own], pbuf.at[c, s, own], fs.at[c, s], fr.at[c, s], prv)
-
-        def fcopy_b(s):
-            return remote(pbuf.at[c, s], pbuf.at[c, s], fs.at[c, s], fr.at[c, s], prv)
+            return remote(pbuf.at[s, own], pbuf.at[s, own], fs.at[s], fr.at[s], prv)
+
+        def fcopy(s):
+            return remote(pbuf.at[s], pbuf.at[s], fs.at[s], fr.at[s], prv)
+
+        def gcopy_a(s):
+            return remote(pbuf.at[s, own], ybuf.at[s, upper], gs.at[s], gr.at[s], mate)
 
         def gcopy(s):
-            return remote(pbuf.at[c, s, own], ybuf.at[c, s, pl.ds(64, 64)], gs.at[c, s], gr.at[c, s], mate)
-
-        def first(i, s, kind):
-            g = 2 * i + c
-            expert, part = g // 12, g % 12
-            a = g - 192
-            in_moe = g < 192
-            l_moe = jnp.where(part < 4, expert, 12 + part)
-            r_moe = jnp.where(part < 4, part, 4 + expert)
-            l_att = jnp.where(a < 16, 24 + a % 8, 32 + (a - 16) // 4)
-            r_att = jnp.where(a < 16, 20 + a // 8, 22 + (a - 16) % 4)
-            li = jnp.where(in_moe, l_moe, l_att)
-            ri = jnp.where(in_moe, r_moe, r_att)
-            pbuf[c, s] = dot_f(lhs[li], rhs[ri])
-
-            @pl.when(kind % 2 == 0)
+            return remote(pbuf.at[s], ybuf.at[s], gs.at[s], gr.at[s], mate)
+
+        def first(i, s, is_e, is_a, is_b):
+            m = i // 2
+            g = 2 * m + c
+
+            @pl.when((i % 2 == 0) & is_e)
+            def _():
+                el, part = g // 12, g % 12
+                down = part < 4
+                l_one = jnp.where(down, 8 * y + el, 12 + part)
+                r_one = jnp.where(down, part, 4 + el)
+                l_two = jnp.where(down, 42 + el, 30 + part)
+                r_two = jnp.where(down, 12 + part, 16 + el)
+                total = dot_f(lhs[l_one], rhs[r_one]) + dot_f(lhs[l_two], rhs[r_two])
+                pbuf[s] = total[:CHUNK]
+                pbuf[s + 1] = total[CHUNK:]
+
+            @pl.when((i % 2 == 0) & jnp.logical_not(is_e))
+            def _():
+                a = g - N_EXPERT
+                l_one = jnp.where(a < 8, 32 + a // 4, 24 + a % 8)
+                r_one = jnp.where(a < 8, 26 + a % 4, 23 + a // 8)
+                total = dot_f(lhs[l_one], rhs[r_one])
+                pbuf[s] = total[:CHUNK]
+                pbuf[s + 1] = total[CHUNK:]
+
+            @pl.when(is_a)
             def _():
                 ycopy_a(s).start()
 
-            @pl.when((kind == 3) & (p == last))
-            def _():
-                leaf_copy(s).start()
-
-        def second(i, s, kind):
-            @pl.when(kind % 2 == 0)
+        def second(i, s, is_e, is_a, is_b):
+            @pl.when(is_a)
             def _():
                 ycopy_a(s).wait_recv()
 
                 @pl.when(p > 0)
                 def _():
                     zcopy_a(s).wait_recv()
-                    zbuf[c, s, half] = zbuf[c, s, half] + (pbuf[c, s, own] + ybuf[c, s, half])
+                    zbuf[s, half] = zbuf[s, half] + (pbuf[s, own] + ybuf[s, half])
 
                 @pl.when(p == 0)
                 def _():
-                    zbuf[c, s, half] = pbuf[c, s, own] + ybuf[c, s, half]
+                    zbuf[s, half] = pbuf[s, own] + ybuf[s, half]
 
                 @pl.when(p < last)
                 def _():
@@ -744,57 +971,46 @@
 
                 @pl.when(p == last)
                 def _():
-                    pbuf[c, s, own] = zbuf[c, s, half]
+                    pbuf[s, own] = zbuf[s, half]
                     fcopy_a(s).start()
+                    gcopy_a(s).start()
+
+            @pl.when(jnp.logical_not(is_a))
+            def _():
+                @pl.when(p > 0)
+                def _():
+                    zcopy(s).wait_recv()
+                    zbuf[s] = zbuf[s] + pbuf[s]
+
+                @pl.when(p == 0)
+                def _():
+                    zbuf[s] = pbuf[s]
+
+                @pl.when(p < last)
+                def _():
+                    zcopy(s).start()
+
+                @pl.when((p == last) & is_e)
+                def _():
+                    pbuf[s] = zbuf[s]
+                    fcopy(s).start()
                     gcopy(s).start()
 
-            @pl.when((kind % 2 == 1) & ((kind == 1) | (p < last)))
-            def _():
-                @pl.when(p > 0)
-                def _():
-                    zcopy_b(s).wait_recv()
-                    zbuf[c, s] = zbuf[c, s] + pbuf[c, s]
-
-                @pl.when(p == 0)
-                def _():
-                    zbuf[c, s] = pbuf[c, s]
-
-                @pl.when((p < last - 1) | ((kind == 1) & (p < last)))
-                def _():
-                    zcopy_b(s).start()
-
-                @pl.when((kind == 1) & (p == last))
+                @pl.when((p == last) & is_b)
                 def _():
                     ycopy_b(s).start()
 
-                @pl.when((kind == 3) & (p == last - 1))
-                def _():
-                    leaf_copy(s).wait_recv()
-                    zbuf[c, s] = zbuf[c, s] + ybuf[c, s]
-                    ycopy_c(s, (i // 5) % SPARE).start()
-
-        def third(i, s, kind):
-            @pl.when((kind == 1) & (p == last))
+        def third(i, s, is_e, is_a, is_b):
+            @pl.when(is_b & (p == last))
             def _():
                 ycopy_b(s).wait_recv()
-                pbuf[c, s] = zbuf[c, s] + ybuf[c, s]
-                fcopy_b(s).start()
-
-            @pl.when((kind == 3) & (p == last - 1))
-            def _():
-                k = (i // 5) % SPARE
-                ycopy_c(s, k).wait_recv()
-                pbuf[c, s] = zbuf[c, s] + xbuf[c, k]
-                fcopy_c(s).start()
-
-                @pl.when(p > 0)
-                def _():
-                    fcopy_b(s).start()
-
-        def fourth(i, s, kind):
+                pbuf[s] = zbuf[s] + ybuf[s]
+                fcopy(s).start()
+
+        def fourth(i, s, is_e, is_a, is_b):
             @pl.when(p < last)
             def _():
-                @pl.when(kind % 2 == 0)
+                @pl.when(is_a)
                 def _():
                     fcopy_a(s).wait_recv()
 
@@ -802,74 +1018,91 @@
                     def _():
                         fcopy_a(s).start()
 
-                    gcopy(s).start()
-
-                @pl.when((kind == 1) | ((kind == 3) & (p < last - 1)))
-                def _():
-                    fcopy_b(s).wait_recv()
+                    gcopy_a(s).start()
+
+                @pl.when(jnp.logical_not(is_a))
+                def _():
+                    fcopy(s).wait_recv()
 
                     @pl.when(p > 0)
                     def _():
-                        fcopy_b(s).start()
-
-        def store(s, dst0, dst1):
-            pltpu.make_async_copy(pbuf.at[c, s, :, pl.ds(0, 128)], dst0, os0.at[c, s]).start()
-            pltpu.make_async_copy(pbuf.at[c, s, :, pl.ds(128, 128)], dst1, os1.at[c, s]).start()
-
-        def fifth(i, s, kind):
-            @pl.when(kind % 2 == 0)
+                        fcopy(s).start()
+
+                    @pl.when(is_e)
+                    def _():
+                        gcopy(s).start()
+
+        def store(buf_s, sem, dst0, dst1):
+            local(buf_s.at[:, pl.ds(0, LANES)], dst0, sem).start()
+            local(buf_s.at[:, pl.ds(LANES, LANES)], dst1, sem).start()
+
+        def fifth(i, s, is_e, is_a, is_b):
+            @pl.when(is_a)
+            def _():
+                gcopy_a(s).wait_recv()
+                ycopy_a(s).wait_send()
+                pbuf[s, oth] = ybuf[s, upper]
+
+            @pl.when(is_e)
             def _():
                 gcopy(s).wait_recv()
-                ycopy_a(s).wait_send()
-                pbuf[c, s, oth] = ybuf[c, s, pl.ds(64, 64)]
-
-            @pl.when((kind == 3) & (p == last))
-            def _():
-                fcopy_c(s).wait_recv()
-                leaf_copy(s).wait_send()
-                pbuf[c, s] = zbuf[c, s]
-
-            g = 2 * i + c
-            expert, part = g // 12, g % 12
-            a = g - 192
-
-            @pl.when((g < 192) & (part < 4))
-            def _():
-                col = pl.multiple_of(part * 256, 128)
-                col1 = pl.multiple_of(part * 256 + 128, 128)
-                store(s, o_down.at[expert, :, pl.ds(col, 128)], o_down.at[expert, :, pl.ds(col1, 128)])
-
-            @pl.when((g < 192) & (part >= 4))
-            def _():
-                rows = pl.ds(pl.multiple_of((part - 4) * 128, 128), 128)
-                store(s, o_gate.at[expert, rows], o_up.at[expert, rows])
-
-            @pl.when((g >= 192) & (a < 8))
-            def _():
-                rows = pl.ds(pl.multiple_of(a * 128, 128), 128)
-                store(s, o_q.at[rows, pl.ds(0, 128)], o_q.at[rows, pl.ds(128, 128)])
-
-            @pl.when((a >= 8) & (a < 16))
-            def _():
-                rows = pl.ds(pl.multiple_of((a - 8) * 128, 128), 128)
-                store(s, o_k.at[rows], o_v.at[rows])
-
-            @pl.when(a >= 16)
-            def _():
-                b = a - 16
-                rows = pl.ds(pl.multiple_of((b // 4) * 128, 128), 128)
-                col = pl.multiple_of((b % 4) * 256, 128)
-                col1 = pl.multiple_of((b % 4) * 256 + 128, 128)
-                store(s, o_out.at[rows, pl.ds(col, 128)], o_out.at[rows, pl.ds(col1, 128)])
-
-        def sixth(i, s, kind):
-            pltpu.make_async_copy(pbuf.at[c, s, :, pl.ds(0, 128)], o_k.at[pl.ds(0, 128)], os0.at[c, s]).wait()
-            pltpu.make_async_copy(pbuf.at[c, s, :, pl.ds(0, 128)], o_k.at[pl.ds(0, 128)], os1.at[c, s]).wait()
-
-            @pl.when(kind % 2 == 0)
-            def _():
+
+            g = 2 * (i // 2) + c
+            el, part = g // 12, g % 12
+            a = g - N_EXPERT
+            low = CHUNK * (i % 2)
+
+            def at_rows(start_row):
+                return pl.ds(pl.multiple_of(start_row + low, CHUNK), CHUNK)
+
+            def both_rows(write):
+                write(pbuf.at[s], os0.at[s], 8 * y + el)
+                write(ybuf.at[s], os1.at[s], 8 * (1 - y) + el)
+
+            @pl.when(is_e & (part < 4))
+            def _():
+                col = pl.ds(pl.multiple_of(part * 256, LANES), LANES)
+                col1 = pl.ds(pl.multiple_of(part * 256 + LANES, LANES), LANES)
+                both_rows(
+                    lambda src, sem, e: store(
+                        src, sem, o_down.at[e, at_rows(0), col], o_down.at[e, at_rows(0), col1]
+                    )
+                )
+
+            @pl.when(is_e & (part >= 4))
+            def _():
+                rows = at_rows((part - 4) * 128)
+                both_rows(lambda src, sem, e: store(src, sem, o_gate.at[e, rows], o_up.at[e, rows]))
+
+            @pl.when(jnp.logical_not(is_e) & (a < 8))
+            def _():
+                rows = at_rows((a // 4) * 128)
+                col = pl.ds(pl.multiple_of((a % 4) * 256, LANES), LANES)
+                col1 = pl.ds(pl.multiple_of((a % 4) * 256 + LANES, LANES), LANES)
+                store(pbuf.at[s], os0.at[s], o_out.at[rows, col], o_out.at[rows, col1])
+
+            @pl.when(jnp.logical_not(is_e) & (a >= 8) & (a < 16))
+            def _():
+                rows = at_rows((a - 8) * 128)
+                store(pbuf.at[s], os0.at[s], o_q.at[rows, pl.ds(0, LANES)], o_q.at[rows, pl.ds(LANES, LANES)])
+
+            @pl.when(jnp.logical_not(is_e) & (a >= 16))
+            def _():
+                rows = at_rows((a - 16) * 128)
+                store(pbuf.at[s], os0.at[s], o_k.at[rows], o_v.at[rows])
+
+        def sixth(i, s, is_e, is_a, is_b):
+            local(pbuf.at[s], o_q.at[pl.ds(0, CHUNK)], os0.at[s]).wait()
+
+            @pl.when(is_e)
+            def _():
+                local(ybuf.at[s], o_q.at[pl.ds(0, CHUNK)], os1.at[s]).wait()
                 gcopy(s).wait_send()
 
+            @pl.when(is_a)
+            def _():
+                gcopy_a(s).wait_send()
+
                 @pl.when(p < last)
                 def _():
                     zcopy_a(s).wait_send()
@@ -878,24 +1111,19 @@
                 def _():
                     fcopy_a(s).wait_send()
 
-            @pl.when((kind == 1) | ((kind == 3) & (p < last)))
-            def _():
-                @pl.when((p < last - 1) | ((kind == 1) & (p < last)))
-                def _():
-                    zcopy_b(s).wait_send()
-
-                @pl.when((kind == 1) & (p == last))
+            @pl.when(jnp.logical_not(is_a))
+            def _():
+                @pl.when(p < last)
+                def _():
+                    zcopy(s).wait_send()
+
+                @pl.when((p == last) & is_b)
                 def _():
                     ycopy_b(s).wait_send()
 
-                @pl.when((kind == 3) & (p == last - 1))
-                def _():
-                    ycopy_c(s, 0).wait_send()
-                    fcopy_c(s).wait_send()
-
                 @pl.when(p > 0)
                 def _():
-                    fcopy_b(s).wait_send()
+                    fcopy(s).wait_send()
 
         t2 = hop * (1 + p)
         t3 = hop * (2 + last)
@@ -924,7 +1152,7 @@
     last = nz - 1
     hop = HOP
     ring = hop * (2 * last + 4) + 2
-    ring += -ring % 5
+    ring = max(32, ring + ring % 2)
     f32, bf16 = jnp.float32, jnp.bfloat16
 
     def out(shape, kind=f32):
@@ -946,9 +1174,9 @@
         in_specs=[pl.BlockSpec(memory_space=pltpu.SMEM)] + [anywhere] * (len(operands) - 1),
         out_specs=[anywhere] * len(outs),
         scratch_shapes=[
-            vmem((34, 128, 1024), bf16), vmem((26, 1024, 256), bf16),
-            vmem((2, ring, 128, 256), f32), vmem((2, ring, 128, 256), f32), vmem((2, ring, 128, 256), f32),
-            vmem((2, SPARE, 128, 256), f32), vmem((1024, 1152), f32), vmem((1024, 1152), f32),
+            vmem((50, 128, 1024), bf16), vmem((30, 1024, 256), bf16),
+            vmem((2 * ring, CHUNK, 256), f32), vmem((2 * ring, CHUNK, 256), f32), vmem((2 * ring, CHUNK, 256), f32),
+            vmem((1024, 1152), f32), vmem((1024, 1152), f32),
             vmem((1024, 1024), bf16), vmem((2, 1024, 256), bf16), vmem((4, 128, 1024), bf16),
             vmem((4, 1024, 128), bf16), vmem((1024, 128), bf16), vmem((1024, 128), bf16),
             vmem((128, 1024), bf16), vmem((128, 1024), bf16),
@@ -957,15 +1185,19 @@
             vmem((1024, 128), f32), vmem((8, 1024), f32), vmem((16, 128), f32),
             vmem((8, 1024), jnp.int32), vmem((8, 1024), f32),
             vmem((3, 16, 128), f32), vmem((8, 1024), f32),
+            vmem((EXPERTS, 1024), f32), vmem((EXPERTS, 1024), f32), vmem((1024, 128), f32),
             dma((18,)), dma((2, 3)), dma((11,)),
         ]
-        + [dma((2, ring))] * 10
-        + [dma((2, SPARE))]
+        + [dma((2 * ring,))] * 10
         + [dma((4,))] * 6
         + [dma((5,))] * 2
         + [dma((3,))] * 6
         + [reg((3,))] * 3
-        + [dma((3,))] * 2,
+        + [dma((3,))] * 2
+        + [reg]
+        + [dma((4,))] * 8
+        + [dma((16,))] * 8
+        + [dma((1,))] * 2,
         compiler_params=pltpu.CompilerParams(
             collective_id=0, has_side_effects=True, vmem_limit_bytes=63 * 2**20
         ),

time: 538 us -> 487 us (0.905)
  Pallas kernels: 512 us -> 461 us
    pallas_call x1, Pallas kernels: 512 us -> 461 us  [run_layer(): pl.pallas_call(functools.partial(layer_kernel, nz, hop, ring), out_shape=...]
where the time goes in v7:
time: 487 us
  Pallas kernels  461 us (95%)
  local copies, waits for them, and re-layouts  24.2 us (5%)
    pallas_call x1, Pallas kernels, run_layer(): pl.pallas_call(functools.partial(layer_kernel, nz, hop, ring), out_shape=...  461 us
    unnamed x38, local copies, waits for them, and re-layouts  24.2 us

profile of v7, /device:TPU:0, one launch (start us, length us, event | category | flops | bytes accessed | tf_op | source)
XLA Modules:
  0.0 486.9 jit_solution(6883315099518474886)
XLA Ops:
  1.3 461.4 %shard_map.247 = (f32[16,1024,128]{2,1,0:T(8,128)}, f32[16,1024,128]{2,1,0:T(8,128)}, f32[16,128,1024]{2,1,0:T(8,128)}, f32[1024,256]{1,0:T(8,128)}, f32[1024,12...) custom-call(s32[1]{0:T(128)S(6)} %copy.40.length, ...), custom_call_target="tpu_custom_call" | custom-call | tf_op jit(solution)/shard_map/pallas_call | solution.py:1171
  462.7 0.0 copy-start.1
  462.7 0.0 copy-start.6
  462.7 0.0 copy-start.8
  462.7 0.0 copy-start.3
  462.7 0.0 copy-start.5
  462.7 0.0 copy-start.4
  462.7 0.0 copy-start.2
  462.7 3.2 copy.41
  466.0 0.0 copy-done.1
  466.0 0.0 copy-start
  466.0 1.3 copy.42
  467.3 0.0 copy-done.6
  467.3 0.0 copy-start.7
  467.3 0.6 copy.43
  467.9 0.0 copy-done.8
  467.9 0.6 copy.44
  468.5 0.0 copy-done.3
  468.5 1.0 copy.45
  469.5 0.0 copy-done.5
  469.5 0.8 copy.46
  470.3 0.0 copy-done.4
  470.3 0.0 slice-start.2
  470.3 0.8 copy.47
  471.1 0.0 copy-done.2
  471.1 1.0 copy.48
  472.0 0.0 copy-done.7
  472.0 0.6 copy.49
  472.6 0.0 copy-done
  472.6 0.0 slice-start.3
  472.6 0.0 slice-start
  472.6 4.3 copy.50
  476.9 0.0 slice-done.2
  476.9 1.0 slice-done.3
  477.9 0.0 slice-start.1
  477.9 4.3 copy.51
  482.1 0.0 slice-done
  482.1 1.4 slice-done.1
  483.5 3.4 copy.52
  (2 shorter events, 0.0 us)
Async XLA Ops:
  462.7 3.3 copy-start.1
  462.7 4.6 copy-start.6
  462.7 5.2 %copy-start.8 = (f32[8,128]{1,0:T(8,128)S(1)}, f32[8,128]{1,0:T(8,128)}, u32[]{:S(2)}) copy-start(f32[8,128]{1,0:T(8,128)} %get-tuple-element.27) | copy-start | bytes 12292
  462.7 5.8 %copy-start.3 = (f32[1024,256]{1,0:T(8,128)S(1)}, f32[1024,256]{1,0:T(8,128)}, u32[]{:S(2)}) copy-start(f32[1024,256]{1,0:T(8,128)} %get-tuple-element.52) | copy-start | bytes 3145732
  462.7 6.8 %copy-start.5 = (f32[1024,128]{1,0:T(8,128)S(1)}, f32[1024,128]{1,0:T(8,128)}, u32[]{:S(2)}) copy-start(f32[1024,128]{1,0:T(8,128)} %get-tuple-element.53) | copy-start | bytes 1572868
  462.7 7.6 %copy-start.4 = (f32[1024,128]{1,0:T(8,128)S(1)}, f32[1024,128]{1,0:T(8,128)}, u32[]{:S(2)}) copy-start(f32[1024,128]{1,0:T(8,128)} %get-tuple-element.54) | copy-start | bytes 1572868
  462.7 8.4 %copy-start.2 = (f32[256,1024]{1,0:T(8,128)S(1)}, f32[256,1024]{1,0:T(8,128)}, u32[]{:S(2)}) copy-start(f32[256,1024]{1,0:T(8,128)} %get-tuple-element.55) | copy-start | bytes 3145732
  466.0 6.7 %copy-start = (f32[16,1024,128]{2,1,0:T(8,128)S(1)}, f32[16,1024,128]{2,1,0:T(8,128)}, u32[]{:S(2)}) copy-start(f32[16,1024,128]{2,1,0:T(8,128)} %get-tuple-element.57) | copy-start | bytes 25165828
  467.3 4.8 copy-start.7
  470.3 6.6 %slice-start.2 = ((s8[8388608]{0:T(1024)(128)(4,1)}), s8[4194304]{0:T(1024)(128)(4,1)S(1)}, s32[]{:S(2)}) async-start(s8[8388608]{0:T(1024)(128)(4,1)} %bitcast.9), calls=%async_computation.2 | async-start | bytes 8388608
  472.6 5.2 %slice-start.3 = ((s8[8388608]{0:T(1024)(128)(4,1)}), s8[4194304]{0:T(1024)(128)(4,1)S(1)}, s32[]{:S(2)}) async-start(s8[8388608]{0:T(1024)(128)(4,1)} %bitcast.9), calls=%async_computation.3 | async-start | bytes 8388608
  472.6 9.5 %slice-start = ((s8[8388608]{0:T(1024)(128)(4,1)}), s8[4194304]{0:T(1024)(128)(4,1)S(1)}, s32[]{:S(2)}) async-start(s8[8388608]{0:T(1024)(128)(4,1)} %bitcast.7), calls=%async_computation | async-start | bytes 8388608
  477.9 5.6 %slice-start.1 = ((s8[8388608]{0:T(1024)(128)(4,1)}), s8[4194304]{0:T(1024)(128)(4,1)S(1)}, s32[]{:S(2)}) async-start(s8[8388608]{0:T(1024)(128)(4,1)} %bitcast.7), calls=%async_computation.1 | async-start | bytes 8388608

commit v8 on v7

--- a/solution.py
+++ b/solution.py
@@ -40,15 +40,15 @@
 HOP = 2
 HALF = EXPERTS // 2
 T_SUM1 = 30
-T_MID1 = 52
-T_ATT = 56
-T_TURN = 64
-T_PROJ = 68
+T_MID1 = 56
+T_ATT = 60
+T_TURN = 68
+T_PROJ = 70
 T_SUM2 = 72
-T_TOK = 92
-T_MOE = 96
-T_SUM3 = 104
-T_RES = 124
+T_TOK = 96
+T_MOE = 98
+T_SUM3 = 102
+T_RES = 126
 
 
 def dot_nt(left, right):
@@ -845,14 +845,17 @@
         T_TOK - 1: lambda: do_all(
             lambda: sum_last(1), lambda: start(halves_in(s_dres)), lambda: start([pair_load(0, 0)])
         ),
-        T_MOE: lambda: do_all(lambda: start(tokens_out), lambda: norm_next(0)),
-        T_MOE + 2: lambda: norm_next(1),
-        T_MOE + 4: lambda: norm_next(2),
-        T_MOE + 6: lambda: do_all(lambda: norm_next(3), lambda: start(norms_out)),
-        T_SUM3: lambda: do_all(lambda: wait(tokens_out + norms_out), lambda: sum_first(2)),
+        T_MOE: lambda: start(tokens_out),
+        T_SUM3 + 5: lambda: norm_next(0),
+        T_SUM3 + 7: lambda: norm_next(1),
+        T_SUM3 + 9: lambda: norm_next(2),
+        T_SUM3 + 11: lambda: do_all(lambda: norm_next(3), lambda: start(norms_out)),
+        T_SUM3: lambda: sum_first(2),
         T_SUM3 + 2: lambda: sum_second(2),
         T_RES - 3: lambda: sum_third(2),
-        T_RES - 1: lambda: do_all(lambda: sum_last(2), lambda: start(halves_in(s_resid))),
+        T_RES - 1: lambda: do_all(
+            lambda: sum_last(2), lambda: wait(tokens_out + norms_out), lambda: start(halves_in(s_resid))
+        ),
         T_RES + 4: lambda: start(result_out),
         T_RES + 8: lambda: wait(result_out),
     }
@@ -866,10 +869,10 @@
         for begin, count, fn in (
             (0, 30, half_pass),
             (T_MID1, 4, middle_rows),
-            (T_TURN, 4, turn_rows),
-            (T_PROJ, 4, project_rows),
-            (T_TOK, 4, token_rows),
-            (T_MOE, EXPERTS // 2, moe_pair),
+            (T_TURN, 2, lambda u: do_all(lambda: turn_rows(2 * u), lambda: turn_rows(2 * u + 1))),
+            (T_PROJ, 2, lambda u: do_all(lambda: project_rows(2 * u), lambda: project_rows(2 * u + 1))),
+            (T_TOK, 2, lambda u: do_all(lambda: token_rows(2 * u), lambda: token_rows(2 * u + 1))),
+            (T_MOE, EXPERTS // 4, lambda u: do_all(lambda: moe_pair(2 * u), lambda: moe_pair(2 * u + 1))),
             (T_RES, 4, result_rows),
         ):
             pl.when((t >= begin) & (t < begin + count))(lambda fn=fn, begin=begin: fn(t - begin))
@@ -891,7 +894,7 @@
         p = z if c == 0 else last - z
         nxt, prv = (up_id, dn_id) if c == 0 else (dn_id, up_id)
         def at(delay, body):
-            i = t - delay
+            i = t - delay - c
 
             @pl.when((i >= 0) & (i < N_CLASS))
             def _():
@@ -1142,7 +1145,7 @@
                 at(delay, fn)
         return carry
 
-    total = N_CLASS + hop * (2 * last + 4) + 1
+    total = N_CLASS + hop * (2 * last + 4) + 2
     lax.fori_loop(0, total, body, 0)
 
 

time: 487 us -> 480 us (0.986)
  Pallas kernels: 461 us -> 454 us
    pallas_call x1, Pallas kernels: 461 us -> 454 us  [run_layer(): pl.pallas_call(functools.partial(layer_kernel, nz, hop, ring), out_shape=...]
where the time goes in v8:
time: 480 us
  Pallas kernels  454 us (95%)
  local copies, waits for them, and re-layouts  24.2 us (5%)
    pallas_call x1, Pallas kernels, run_layer(): pl.pallas_call(functools.partial(layer_kernel, nz, hop, ring), out_shape=...  454 us
    unnamed x38, local copies, waits for them, and re-layouts  24.2 us

profile of v8, /device:TPU:0, one launch (start us, length us, event | category | flops | bytes accessed | tf_op | source)
XLA Modules:
  0.0 479.7 jit_solution(16945067340663244212)
XLA Ops:
  1.3 454.1 %shard_map.247 = (f32[16,1024,128]{2,1,0:T(8,128)}, f32[16,1024,128]{2,1,0:T(8,128)}, f32[16,128,1024]{2,1,0:T(8,128)}, f32[1024,256]{1,0:T(8,128)}, f32[1024,12...) custom-call(s32[1]{0:T(128)S(6)} %copy.40.length, ...), custom_call_target="tpu_custom_call" | custom-call | tf_op jit(solution)/shard_map/pallas_call | solution.py:1174
  455.4 0.0 copy-start.1
  455.4 0.0 copy-start.6
  455.4 0.0 copy-start.8
  455.4 0.0 copy-start.3
  455.5 0.0 copy-start.5
  455.5 0.0 copy-start.4
  455.5 0.0 copy-start.2
  455.5 3.2 copy.41
  458.7 0.0 copy-done.1
  458.7 0.0 copy-start
  458.7 1.3 copy.42
  460.1 0.0 copy-done.6
  460.1 0.0 copy-start.7
  460.1 0.6 copy.43
  460.7 0.0 copy-done.8
  460.7 0.6 copy.44
  461.3 0.0 copy-done.3
  461.3 1.0 copy.45
  462.2 0.0 copy-done.5
  462.2 0.8 copy.46
  463.0 0.0 copy-done.4
  463.0 0.0 slice-start.2
  463.0 0.8 copy.47
  463.8 0.0 copy-done.2
  463.8 1.0 copy.48
  464.8 0.0 copy-done.7
  464.8 0.6 copy.49
  465.4 0.0 copy-done
  465.4 0.0 slice-start.3
  465.4 0.0 slice-start
  465.4 4.3 copy.50
  469.7 0.0 slice-done.2
  469.7 1.0 slice-done.3
  470.7 0.0 slice-start.1
  470.7 4.3 copy.51
  474.9 0.0 slice-done
  474.9 1.4 slice-done.1
  476.3 3.4 copy.52
  (2 shorter events, 0.0 us)
Async XLA Ops:
  455.4 3.3 copy-start.1
  455.4 4.6 copy-start.6
  455.4 5.2 %copy-start.8 = (f32[8,128]{1,0:T(8,128)S(1)}, f32[8,128]{1,0:T(8,128)}, u32[]{:S(2)}) copy-start(f32[8,128]{1,0:T(8,128)} %get-tuple-element.27) | copy-start | bytes 12292
  455.4 5.8 %copy-start.3 = (f32[1024,256]{1,0:T(8,128)S(1)}, f32[1024,256]{1,0:T(8,128)}, u32[]{:S(2)}) copy-start(f32[1024,256]{1,0:T(8,128)} %get-tuple-element.52) | copy-start | bytes 3145732
  455.5 6.8 %copy-start.5 = (f32[1024,128]{1,0:T(8,128)S(1)}, f32[1024,128]{1,0:T(8,128)}, u32[]{:S(2)}) copy-start(f32[1024,128]{1,0:T(8,128)} %get-tuple-element.53) | copy-start | bytes 1572868
  455.5 7.6 %copy-start.4 = (f32[1024,128]{1,0:T(8,128)S(1)}, f32[1024,128]{1,0:T(8,128)}, u32[]{:S(2)}) copy-start(f32[1024,128]{1,0:T(8,128)} %get-tuple-element.54) | copy-start | bytes 1572868
  455.5 8.4 %copy-start.2 = (f32[256,1024]{1,0:T(8,128)S(1)}, f32[256,1024]{1,0:T(8,128)}, u32[]{:S(2)}) copy-start(f32[256,1024]{1,0:T(8,128)} %get-tuple-element.55) | copy-start | bytes 3145732
  458.7 6.7 %copy-start = (f32[16,1024,128]{2,1,0:T(8,128)S(1)}, f32[16,1024,128]{2,1,0:T(8,128)}, u32[]{:S(2)}) copy-start(f32[16,1024,128]{2,1,0:T(8,128)} %get-tuple-element.57) | copy-start | bytes 25165828
  460.1 4.8 copy-start.7
  463.0 6.6 %slice-start.2 = ((s8[8388608]{0:T(1024)(128)(4,1)}), s8[4194304]{0:T(1024)(128)(4,1)S(1)}, s32[]{:S(2)}) async-start(s8[8388608]{0:T(1024)(128)(4,1)} %bitcast.9), calls=%async_computation.2 | async-start | bytes 8388608
  465.4 5.2 %slice-start.3 = ((s8[8388608]{0:T(1024)(128)(4,1)}), s8[4194304]{0:T(1024)(128)(4,1)S(1)}, s32[]{:S(2)}) async-start(s8[8388608]{0:T(1024)(128)(4,1)} %bitcast.9), calls=%async_computation.3 | async-start | bytes 8388608
  465.4 9.5 %slice-start = ((s8[8388608]{0:T(1024)(128)(4,1)}), s8[4194304]{0:T(1024)(128)(4,1)S(1)}, s32[]{:S(2)}) async-start(s8[8388608]{0:T(1024)(128)(4,1)} %bitcast.7), calls=%async_computation | async-start | bytes 8388608
  470.7 5.6 %slice-start.1 = ((s8[8388608]{0:T(1024)(128)(4,1)}), s8[4194304]{0:T(1024)(128)(4,1)S(1)}, s32[]{:S(2)}) async-start(s8[8388608]{0:T(1024)(128)(4,1)} %bitcast.7), calls=%async_computation.1 | async-start | bytes 8388608

commit v9 on v8

--- a/solution.py
+++ b/solution.py
@@ -38,17 +38,17 @@
 N_EXPERT = 96
 N_CLASS = 120
 HOP = 2
-HALF = EXPERTS // 2
-T_SUM1 = 30
-T_MID1 = 56
-T_ATT = 60
-T_TURN = 68
-T_PROJ = 70
-T_SUM2 = 72
-T_TOK = 96
-T_MOE = 98
-T_SUM3 = 102
-T_RES = 126
+EARLY = 7
+T_SUM1 = 32
+T_MID1 = 58
+T_ATT = 62
+T_TURN = 70
+T_PROJ = 72
+T_SUM2 = 74
+T_TOK = 98
+T_MOE = 100
+T_SUM3 = 104
+T_RES = 128
 
 
 def dot_nt(left, right):
@@ -256,7 +256,7 @@
         return carry
 
     near_d = [2 * tensor + j for j in range(2)]
-    direct_d = [8 + 4 * core + j for j in range(4)]
+    direct_d = [8 + 2 * core, 9 + 2 * core, 12 + 2 * core, 13 + 2 * core]
 
     def slab(k):
         return pl.ds(pl.multiple_of(4 * k, 4), 4)
@@ -278,8 +278,9 @@
 
     def stage_d(k):
         rows = block(k, 64)
+        live = lax.broadcasted_iota(jnp.int32, (64, 256), 0) + k * 64 < length[0]
         for c in range(4):
-            pbuf[4 * k + c] = rhs[c, rows, :].astype(f32)
+            pbuf[4 * k + c] = jnp.where(live, rhs[c, rows, :].astype(f32), 0.0)
         d_y(k).start()
 
     def h_piece(b, t):
@@ -337,6 +338,8 @@
         d_y(k).wait_recv()
         d_c(k).start()
 
+    wait(late_load)
+    stage_d(near_d[0])
     wait(token_load + proj_load)
     head_rows(0, 0)
     attend(0)
@@ -345,18 +348,16 @@
     w_y.start()
     attend(1)
     head_rows(2, 0)
+    attend(2)
     w_y.wait_recv()
     w_z.start()
-    wait(late_load)
-    lax.fori_loop(0, 4, mask_rows, 0)
-    for j in range(2):
-        stage_d(near_d[j])
-    for j in range(2):
-        stage_d(direct_d[j])
-    attend(2)
+    stage_d(near_d[1])
     head_rows(3, 0)
     start(expert_load(8 * y, 0))
     attend(3)
+    lax.fori_loop(0, 4, mask_rows, 0)
+    for j in range(2):
+        stage_d(direct_d[j])
     dk_acc[...] = jnp.zeros_like(dk_acc)
     dv_acc[...] = jnp.zeros_like(dv_acc)
     norms[...] = jnp.zeros_like(norms)
@@ -419,8 +420,15 @@
                 lhs[16 + 2 * col + half_c, :, rows] = normed[:, 128 * half_c : 128 * half_c + 128].T.astype(bf16)
         return carry
 
+    def place_of(k):
+        paired = EARLY + (k - 2 * EARLY) // 2
+        return jnp.where(k < EARLY, k, jnp.where(k < 2 * EARLY, k - EARLY, jnp.where(k < 16, paired, k - 16)))
+
+    def is_mate(k):
+        return ((k >= EARLY) & (k < 2 * EARLY)) | ((k >= 2 * EARLY) & (k < 16) & ((k - 2 * EARLY) % 2 == 1))
+
     def expert_of(k):
-        return jnp.where(k < 16, 8 * y + k % 8, 8 * (1 - y) + k % 8)
+        return jnp.where(k < 16, 8 * y + place_of(k), 8 * (1 - y) + place_of(k))
 
     def next_weights(k):
         wait(expert_load(expert_of(k), k % 2))
@@ -429,11 +437,11 @@
         def _():
             start(expert_load(expert_of(k + 1), (k + 1) % 2))
 
-    def unit(k, b, kind):
-        rows = block(b)
+    def unit(k, b, kind, size=ROWS):
+        rows = block(b, size)
         s = k % 2
         e = expert_of(k)
-        el = k % 8
+        el = place_of(k)
         if kind == "mate":
             both = dot_f(rhs[26, rows, :], wgu[s, 0:256, :])
             for c in range(1, 4):
@@ -445,7 +453,7 @@
         d_raw = dot_nt(rhs[d_base, rows, :], wdb[s, :, 0:256])
         for c in range(1, 4):
             d_raw = d_raw + dot_nt(rhs[d_base + c, rows, :], wdb[s, :, 256 * c : 256 * c + 256])
-        lane = lax.broadcasted_iota(jnp.int32, (ROWS, LANES), 1)
+        lane = lax.broadcasted_iota(jnp.int32, (size, LANES), 1)
         weights = slot_m if kind == "mate" else slot_w
         weight = jnp.sum(jnp.where(lane == e, weights[rows, :], 0.0), axis=1, keepdims=True)
         sigma = 1.0 / (1.0 + jnp.exp(-gate))
@@ -473,18 +481,16 @@
             part = dot_nt(rhs[4 + el, rows, :], wgu[s])
         acc[rows, 0:1024] = part if is_first else acc[rows, 0:1024] + part
 
-    def units(k, begin, count, kind):
-        def step(b, carry):
-            unit(k, b, kind)
-            return carry
-
-        lax.fori_loop(begin, begin + count, step, 0)
-
     def forward_step(b, carry):
         @pl.when(b < 4)
         def _():
             gather_x(b).wait_recv()
             gather_f(b).start()
+
+        @pl.when(b == 3)
+        def _():
+            d_share(0)
+            d_share(1)
 
         @pl.when(b > 0)
         def _():
@@ -499,8 +505,6 @@
 
         @pl.when(b == 4)
         def _():
-            d_share(0)
-            d_share(1)
             stage_d(direct_d[2])
             stage_d(direct_d[3])
 
@@ -514,16 +518,16 @@
     keep.start()
 
     chores = {
-        5: [(h_share, 0)],
-        8: [(d_direct, 0), (d_direct, 1)],
-        11: [(h_share, 1)],
-        13: [(h_forward, 0), (d_forward, 0)],
-        16: [(h_share, 2), (d_forward, 1)],
-        20: [(h_forward, 1)],
-        23: [(h_share, 3)],
-        26: [(h_forward, 2)],
-        29: [(d_direct, 2)],
-        31: [(h_forward, 3), (d_direct, 3)],
+        4: [(d_direct, 0), (d_direct, 1), (h_share, 0)],
+        7: [(h_share, 1)],
+        9: [(d_forward, 0)],
+        11: [(h_share, 2)],
+        13: [(d_forward, 1)],
+        15: [(h_share, 3)],
+        17: [(h_forward, 0)],
+        22: [(h_forward, 1)],
+        24: [(d_direct, 2)],
+        27: [(h_forward, 2)],
     }
 
     def own_unit(u, carry):
@@ -533,7 +537,10 @@
         def _():
             next_weights(k)
 
-        unit(k, u % 4, "own")
+        @pl.when(u % 2 == 0)
+        def _():
+            unit(k, (u % 4) // 2, "own", 2 * ROWS)
+
         for when_u, jobs in chores.items():
 
             @pl.when(u == when_u)
@@ -543,7 +550,7 @@
 
         return carry
 
-    lax.fori_loop(4, 32, own_unit, 0)
+    lax.fori_loop(4, 4 * EARLY, own_unit, 0)
 
     kept_copy.wait_recv()
     for b in range(4):
@@ -551,34 +558,34 @@
         slot_m[rows, :] = jnp.concatenate(
             [kept_in[:, rows], jnp.zeros((LANES - EXPERTS, ROWS), f32)], axis=0
         ).T
-    other_core = tensor - core + (1 - core)
-    for j in range(2):
-        d_c(2 * other_core + j).wait_recv()
-        d_f(2 * (3 - tensor) + j).wait_recv()
-    for j in range(4):
-        d_c(8 + 4 * (1 - core) + j).wait_recv()
-    for b in range(4):
+
+    def take(b):
+        rows = pl.ds(ROWS * b, ROWS)
         h_c(b).wait_recv()
         h_f(b).wait_recv()
-
-    def take_d(k, carry):
         for c in range(4):
-            rhs[12 + c, block(k, 64), :] = ybuf[4 * k + c].astype(bf16)
-        return carry
-
-    def take_h(b, carry):
-        rows = block(b)
-        for c in range(4):
-            whole = jnp.concatenate([zbuf[4 * (4 * b + t) + c] for t in range(4)], axis=0)
+            whole = jnp.concatenate([ybuf[4 * (4 * b + j) + c] for j in range(4)], axis=0)
+            rhs[12 + c, rows, :] = whole.astype(bf16)
+            whole = jnp.concatenate([zbuf[4 * (4 * b + j) + c] for j in range(4)], axis=0)
             rhs[26 + c, rows, :] = whole.astype(bf16)
             for half_c in range(2):
                 lhs[34 + 2 * c + half_c, :, rows] = whole[:, 128 * half_c : 128 * half_c + 128].T.astype(bf16)
-        return carry
-
-    lax.fori_loop(0, 16, take_d, 0)
-    lax.fori_loop(0, 4, take_h, 0)
-    next_weights(8)
-    units(8, 0, 4, "mate")
+        unit(EARLY, b, "mate")
+
+    next_weights(EARLY)
+    for j in range(2):
+        d_c(2 * core_mate + j).wait_recv()
+        d_f(2 * (3 - tensor) + j).wait_recv()
+    take(0)
+    take(1)
+    for j in range(2):
+        d_c(8 + 2 * (1 - core) + j).wait_recv()
+    take(2)
+    d_direct(3)
+    h_forward(3)
+    for j in range(2):
+        d_c(12 + 2 * (1 - core) + j).wait_recv()
+    take(3)
     kept_copy.wait_send()
     for j in range(2):
         d_y(near_d[j]).wait_send()
@@ -607,20 +614,23 @@
     pl.semaphore_wait(go, 1 + (z < last).astype(jnp.int32) + (z > 0).astype(jnp.int32))
 
     def half_pass(u):
-        k = 9 + u // 2
-        begin = (u % 2) * 2
-
-        @pl.when(begin == 0)
+        k = EARLY + 1 + u // 2
+
+        @pl.when(u % 2 == 0)
         def _():
             next_weights(k)
 
-        @pl.when(k < 16)
+        @pl.when(is_mate(k))
         def _():
-            units(k, begin, 2, "mate")
+            unit(k, u % 2, "mate", 2 * ROWS)
+
+        @pl.when((k < 16) & jnp.logical_not(is_mate(k)))
+        def _():
+            unit(k, u % 2, "own", 2 * ROWS)
 
         @pl.when(k >= 16)
         def _():
-            units(k, begin, 2, "other")
+            unit(k, u % 2, "other", 2 * ROWS)
 
     mine = pl.ds(pl.multiple_of(core * 512, 512), 512)
     other = pl.ds(pl.multiple_of((1 - core) * 512, 512), 512)
@@ -867,7 +877,7 @@
         for when_t, src in halves_wait.items():
             pl.when(t == when_t)(lambda src=src: wait(halves_in(src)))
         for begin, count, fn in (
-            (0, 30, half_pass),
+            (0, 2 * (23 - EARLY), half_pass),
             (T_MID1, 4, middle_rows),
             (T_TURN, 2, lambda u: do_all(lambda: turn_rows(2 * u), lambda: turn_rows(2 * u + 1))),
             (T_PROJ, 2, lambda u: do_all(lambda: project_rows(2 * u), lambda: project_rows(2 * u + 1))),

time: 480 us -> 472 us (0.983)
  Pallas kernels: 454 us -> 446 us
    pallas_call x1, Pallas kernels: 454 us -> 446 us  [run_layer(): pl.pallas_call(functools.partial(layer_kernel, nz, hop, ring), out_shape=...]
where the time goes in v9:
time: 472 us
  Pallas kernels  446 us (94%)
  local copies, waits for them, and re-layouts  24.2 us (5%)
    pallas_call x1, Pallas kernels, run_layer(): pl.pallas_call(functools.partial(layer_kernel, nz, hop, ring), out_shape=...  446 us
    unnamed x38, local copies, waits for them, and re-layouts  24.2 us

profile of v9, /device:TPU:0, one launch (start us, length us, event | category | flops | bytes accessed | tf_op | source)
XLA Modules:
  0.0 471.7 jit_solution(5621400734128111270)
XLA Ops:
  1.3 446.2 %shard_map.247 = (f32[16,1024,128]{2,1,0:T(8,128)}, f32[16,1024,128]{2,1,0:T(8,128)}, f32[16,128,1024]{2,1,0:T(8,128)}, f32[1024,256]{1,0:T(8,128)}, f32[1024,12...) custom-call(s32[1]{0:T(128)S(6)} %copy.40.length, ...), custom_call_target="tpu_custom_call" | custom-call | tf_op jit(solution)/shard_map/pallas_call | solution.py:1184
  447.5 0.0 copy-start.1
  447.5 0.0 copy-start.6
  447.5 0.0 copy-start.8
  447.5 0.0 copy-start.3
  447.5 0.0 copy-start.5
  447.5 0.0 copy-start.4
  447.5 0.0 copy-start.2
  447.5 3.2 copy.41
  450.8 0.0 copy-done.1
  450.8 0.0 copy-start
  450.8 1.3 copy.42
  452.1 0.0 copy-done.6
  452.1 0.0 copy-start.7
  452.1 0.6 copy.43
  452.7 0.0 copy-done.8
  452.7 0.6 copy.44
  453.3 0.0 copy-done.3
  453.3 1.0 copy.45
  454.3 0.0 copy-done.5
  454.3 0.8 copy.46
  455.1 0.0 copy-done.4
  455.1 0.0 slice-start.2
  455.1 0.8 copy.47
  455.9 0.0 copy-done.2
  455.9 1.0 copy.48
  456.9 0.0 copy-done.7
  456.9 0.6 copy.49
  457.5 0.0 copy-done
  457.5 0.0 slice-start.3
  457.5 0.0 slice-start
  457.5 4.3 copy.50
  461.7 0.0 slice-done.2
  461.7 1.0 slice-done.3
  462.7 0.0 slice-start.1
  462.7 4.3 copy.51
  467.0 0.0 slice-done
  467.0 1.4 slice-done.1
  468.3 3.4 copy.52
  (2 shorter events, 0.0 us)
Async XLA Ops:
  447.5 3.3 copy-start.1
  447.5 4.6 copy-start.6
  447.5 5.2 %copy-start.8 = (f32[8,128]{1,0:T(8,128)S(1)}, f32[8,128]{1,0:T(8,128)}, u32[]{:S(2)}) copy-start(f32[8,128]{1,0:T(8,128)} %get-tuple-element.27) | copy-start | bytes 12292
  447.5 5.8 %copy-start.3 = (f32[1024,256]{1,0:T(8,128)S(1)}, f32[1024,256]{1,0:T(8,128)}, u32[]{:S(2)}) copy-start(f32[1024,256]{1,0:T(8,128)} %get-tuple-element.52) | copy-start | bytes 3145732
  447.5 6.8 %copy-start.5 = (f32[1024,128]{1,0:T(8,128)S(1)}, f32[1024,128]{1,0:T(8,128)}, u32[]{:S(2)}) copy-start(f32[1024,128]{1,0:T(8,128)} %get-tuple-element.53) | copy-start | bytes 1572868
  447.5 7.6 %copy-start.4 = (f32[1024,128]{1,0:T(8,128)S(1)}, f32[1024,128]{1,0:T(8,128)}, u32[]{:S(2)}) copy-start(f32[1024,128]{1,0:T(8,128)} %get-tuple-element.54) | copy-start | bytes 1572868
  447.5 8.4 %copy-start.2 = (f32[256,1024]{1,0:T(8,128)S(1)}, f32[256,1024]{1,0:T(8,128)}, u32[]{:S(2)}) copy-start(f32[256,1024]{1,0:T(8,128)} %get-tuple-element.55) | copy-start | bytes 3145732
  450.8 6.7 %copy-start = (f32[16,1024,128]{2,1,0:T(8,128)S(1)}, f32[16,1024,128]{2,1,0:T(8,128)}, u32[]{:S(2)}) copy-start(f32[16,1024,128]{2,1,0:T(8,128)} %get-tuple-element.57) | copy-start | bytes 25165828
  452.1 4.8 %copy-start.7 = (f32[8,128]{1,0:T(8,128)S(1)}, f32[8,128]{1,0:T(8,128)}, u32[]{:S(2)}) copy-start(f32[8,128]{1,0:T(8,128)} %get-tuple-element.32) | copy-start | bytes 12292
  455.1 6.6 %slice-start.2 = ((s8[8388608]{0:T(1024)(128)(4,1)}), s8[4194304]{0:T(1024)(128)(4,1)S(1)}, s32[]{:S(2)}) async-start(s8[8388608]{0:T(1024)(128)(4,1)} %bitcast.9), calls=%async_computation.2 | async-start | bytes 8388608
  457.5 5.2 %slice-start.3 = ((s8[8388608]{0:T(1024)(128)(4,1)}), s8[4194304]{0:T(1024)(128)(4,1)S(1)}, s32[]{:S(2)}) async-start(s8[8388608]{0:T(1024)(128)(4,1)} %bitcast.9), calls=%async_computation.3 | async-start | bytes 8388608
  457.5 9.5 %slice-start = ((s8[8388608]{0:T(1024)(128)(4,1)}), s8[4194304]{0:T(1024)(128)(4,1)S(1)}, s32[]{:S(2)}) async-start(s8[8388608]{0:T(1024)(128)(4,1)} %bitcast.7), calls=%async_computation | async-start | bytes 8388608
  462.7 5.6 %slice-start.1 = ((s8[8388608]{0:T(1024)(128)(4,1)}), s8[4194304]{0:T(1024)(128)(4,1)S(1)}, s32[]{:S(2)}) async-start(s8[8388608]{0:T(1024)(128)(4,1)} %bitcast.7), calls=%async_computation.1 | async-start | bytes 8388608

commit v10 on v9

--- a/solution.py
+++ b/solution.py
@@ -154,11 +154,13 @@
     quarter = 2 * (z % 2) + y
     part_q = buf.at[pl.ds(pl.multiple_of(tensor * 256 + quarter * 64, 64), 64), wide]
     part_y = buf.at[pl.ds(pl.multiple_of(x_mate * 256 + quarter * 64, 64), 64), wide]
-    part_z = buf.at[pl.ds(pl.multiple_of(x_mate * 256 + (z % 2) * 128, 128), 128), wide]
+    near_q = 2 * (z % 2) + 1 - y
+    part_z = buf.at[pl.ds(pl.multiple_of(x_mate * 256 + near_q * 64, 64), 64), wide]
     pair = base + (z + 1 - 2 * (z % 2)) * 2 + y
     w_x = remote(part_q, part_q, ws.at[0], wr.at[0], x_mate, "tensor")
     w_y = remote(part_y, part_y, ws.at[3], wr.at[3], mate)
     w_z = remote(part_z, part_z, ws.at[4], wr.at[4], pair)
+    w_p = remote(part_y, part_y, ws.at[5], wr.at[5], pair)
     w_c = remote(part_w, part_w, ws.at[1], wr.at[1], core_mate, "tensor")
     part_f = buf.at[block(x_mate), wide]
     w_f = remote(part_f, part_f, ws.at[2], wr.at[2], core_mate, "tensor")
@@ -346,6 +348,7 @@
     head_rows(1, 0)
     w_x.wait_recv()
     w_y.start()
+    w_p.start()
     attend(1)
     head_rows(2, 0)
     attend(2)
@@ -355,9 +358,8 @@
     head_rows(3, 0)
     start(expert_load(8 * y, 0))
     attend(3)
+    stage_d(direct_d[0])
     lax.fori_loop(0, 4, mask_rows, 0)
-    for j in range(2):
-        stage_d(direct_d[j])
     dk_acc[...] = jnp.zeros_like(dk_acc)
     dv_acc[...] = jnp.zeros_like(dv_acc)
     norms[...] = jnp.zeros_like(norms)
@@ -386,6 +388,7 @@
     kept_copy.start()
 
     w_z.wait_recv()
+    w_p.wait_recv()
     w_f.start()
     w_c.wait_recv()
     w_f.wait_recv()
@@ -505,28 +508,28 @@
 
         @pl.when(b == 4)
         def _():
-            stage_d(direct_d[2])
-            stage_d(direct_d[3])
+            stage_d(direct_d[1])
 
         return carry
 
-    for copy in (w_x, w_c, w_f, w_y, w_z):
+    for copy in (w_x, w_c, w_f, w_y, w_z, w_p):
         copy.wait_send()
     next_weights(0)
     lax.fori_loop(0, 5, forward_step, 0)
     keep = local(buf.at[:, wide], s_resid, iosem.at[0])
     keep.start()
 
+    def d_late(j):
+        stage_d(direct_d[j])
+
     chores = {
-        4: [(d_direct, 0), (d_direct, 1), (h_share, 0)],
-        7: [(h_share, 1)],
-        9: [(d_forward, 0)],
-        11: [(h_share, 2)],
-        13: [(d_forward, 1)],
-        15: [(h_share, 3)],
-        17: [(h_forward, 0)],
+        4: [(h_share, 0), (h_share, 1)],
+        8: [(d_forward, 0)],
+        10: [(h_share, 2), (d_late, 2), (d_late, 3)],
+        14: [(h_share, 3)],
+        16: [(d_direct, 0), (h_forward, 0)],
+        18: [(d_forward, 1), (d_direct, 1)],
         22: [(h_forward, 1)],
-        24: [(d_direct, 2)],
         27: [(h_forward, 2)],
     }
 
@@ -581,6 +584,7 @@
     for j in range(2):
         d_c(8 + 2 * (1 - core) + j).wait_recv()
     take(2)
+    d_direct(2)
     d_direct(3)
     h_forward(3)
     for j in range(2):
@@ -610,8 +614,6 @@
     @pl.when(z > 0)
     def _():
         pl.semaphore_signal(go, inc=1, device_id={"dp": dn_id}, device_id_type=MESH)
-
-    pl.semaphore_wait(go, 1 + (z < last).astype(jnp.int32) + (z > 0).astype(jnp.int32))
 
     def half_pass(u):
         k = EARLY + 1 + u // 2
@@ -1146,6 +1148,10 @@
         return [(0, first, at), (t2, second, at), (t3, third, at), (t4, fourth, at), (t5, fifth, at), (t6, sixth, at)]
 
     def body(t, carry):
+        @pl.when(t == 1)
+        def _():
+            pl.semaphore_wait(go, 1 + (z < last).astype(jnp.int32) + (z > 0).astype(jnp.int32))
+
         both = [stage(0, t), stage(1, t)]
         for k in (1, 2, 3, 4, 5, 0):
             if k == 0:
@@ -1203,7 +1209,7 @@
         ]
         + [dma((2 * ring,))] * 10
         + [dma((4,))] * 6
-        + [dma((5,))] * 2
+        + [dma((6,))] * 2
         + [dma((3,))] * 6
         + [reg((3,))] * 3
         + [dma((3,))] * 2

time: 472 us -> 469 us (level)
  no operation moved by 1% of the time
where the time goes in v10:
time: 469 us
  Pallas kernels  443 us (94%)
  local copies, waits for them, and re-layouts  24.2 us (5%)
    pallas_call x1, Pallas kernels, run_layer(): pl.pallas_call(functools.partial(layer_kernel, nz, hop, ring), out_shape=...  443 us
    unnamed x38, local copies, waits for them, and re-layouts  24.2 us

profile of v10, /device:TPU:0, one launch (start us, length us, event | category | flops | bytes accessed | tf_op | source)
XLA Modules:
  0.0 468.9 jit_solution(10944344143299113767)
XLA Ops:
  1.3 443.3 %shard_map.247 = (f32[16,1024,128]{2,1,0:T(8,128)}, f32[16,1024,128]{2,1,0:T(8,128)}, f32[16,128,1024]{2,1,0:T(8,128)}, f32[1024,256]{1,0:T(8,128)}, f32[1024,12...) custom-call(s32[1]{0:T(128)S(6)} %copy.40.length, ...), custom_call_target="tpu_custom_call" | custom-call | tf_op jit(solution)/shard_map/pallas_call | solution.py:1190
  444.6 0.0 copy-start.1
  444.6 0.0 copy-start.6
  444.7 0.0 copy-start.8
  444.7 0.0 copy-start.3
  444.7 0.0 copy-start.5
  444.7 0.0 copy-start.4
  444.7 0.0 copy-start.2
  444.7 3.2 copy.41
  447.9 0.0 copy-done.1
  447.9 0.0 copy-start
  448.0 1.3 copy.42
  449.3 0.0 copy-done.6
  449.3 0.0 copy-start.7
  449.3 0.6 copy.43
  449.9 0.0 copy-done.8
  449.9 0.6 copy.44
  450.5 0.0 copy-done.3
  450.5 1.0 copy.45
  451.5 0.0 copy-done.5
  451.5 0.8 copy.46
  452.3 0.0 copy-done.4
  452.3 0.0 slice-start.2
  452.3 0.8 copy.47
  453.1 0.0 copy-done.2
  453.1 1.0 copy.48
  454.0 0.0 copy-done.7
  454.0 0.6 copy.49
  454.6 0.0 copy-done
  454.6 0.0 slice-start.3
  454.6 0.0 slice-start
  454.6 4.3 copy.50
  458.9 0.0 slice-done.2
  458.9 1.0 slice-done.3
  459.9 0.0 slice-start.1
  459.9 4.3 copy.51
  464.1 0.0 slice-done
  464.1 1.4 slice-done.1
  465.5 3.4 copy.52
  (2 shorter events, 0.0 us)
Async XLA Ops:
  444.6 3.3 copy-start.1
  444.6 4.6 copy-start.6
  444.7 5.2 %copy-start.8 = (f32[8,128]{1,0:T(8,128)S(1)}, f32[8,128]{1,0:T(8,128)}, u32[]{:S(2)}) copy-start(f32[8,128]{1,0:T(8,128)} %get-tuple-element.27) | copy-start | bytes 12292
  444.7 5.8 %copy-start.3 = (f32[1024,256]{1,0:T(8,128)S(1)}, f32[1024,256]{1,0:T(8,128)}, u32[]{:S(2)}) copy-start(f32[1024,256]{1,0:T(8,128)} %get-tuple-element.52) | copy-start | bytes 3145732
  444.7 6.8 %copy-start.5 = (f32[1024,128]{1,0:T(8,128)S(1)}, f32[1024,128]{1,0:T(8,128)}, u32[]{:S(2)}) copy-start(f32[1024,128]{1,0:T(8,128)} %get-tuple-element.53) | copy-start | bytes 1572868
  444.7 7.6 %copy-start.4 = (f32[1024,128]{1,0:T(8,128)S(1)}, f32[1024,128]{1,0:T(8,128)}, u32[]{:S(2)}) copy-start(f32[1024,128]{1,0:T(8,128)} %get-tuple-element.54) | copy-start | bytes 1572868
  444.7 8.4 %copy-start.2 = (f32[256,1024]{1,0:T(8,128)S(1)}, f32[256,1024]{1,0:T(8,128)}, u32[]{:S(2)}) copy-start(f32[256,1024]{1,0:T(8,128)} %get-tuple-element.55) | copy-start | bytes 3145732
  447.9 6.7 %copy-start = (f32[16,1024,128]{2,1,0:T(8,128)S(1)}, f32[16,1024,128]{2,1,0:T(8,128)}, u32[]{:S(2)}) copy-start(f32[16,1024,128]{2,1,0:T(8,128)} %get-tuple-element.57) | copy-start | bytes 25165828
  449.3 4.8 %copy-start.7 = (f32[8,128]{1,0:T(8,128)S(1)}, f32[8,128]{1,0:T(8,128)}, u32[]{:S(2)}) copy-start(f32[8,128]{1,0:T(8,128)} %get-tuple-element.32) | copy-start | bytes 12292
  452.3 6.6 %slice-start.2 = ((s8[8388608]{0:T(1024)(128)(4,1)}), s8[4194304]{0:T(1024)(128)(4,1)S(1)}, s32[]{:S(2)}) async-start(s8[8388608]{0:T(1024)(128)(4,1)} %bitcast.9), calls=%async_computation.2 | async-start | bytes 8388608
  454.6 5.2 %slice-start.3 = ((s8[8388608]{0:T(1024)(128)(4,1)}), s8[4194304]{0:T(1024)(128)(4,1)S(1)}, s32[]{:S(2)}) async-start(s8[8388608]{0:T(1024)(128)(4,1)} %bitcast.9), calls=%async_computation.3 | async-start | bytes 8388608
  454.6 9.5 %slice-start = ((s8[8388608]{0:T(1024)(128)(4,1)}), s8[4194304]{0:T(1024)(128)(4,1)S(1)}, s32[]{:S(2)}) async-start(s8[8388608]{0:T(1024)(128)(4,1)} %bitcast.7), calls=%async_computation | async-start | bytes 8388608
  459.9 5.6 %slice-start.1 = ((s8[8388608]{0:T(1024)(128)(4,1)}), s8[4194304]{0:T(1024)(128)(4,1)S(1)}, s32[]{:S(2)}) async-start(s8[8388608]{0:T(1024)(128)(4,1)} %bitcast.7), calls=%async_computation.1 | async-start | bytes 8388608

commit v11 on v10

--- a/solution.py
+++ b/solution.py
@@ -197,9 +197,9 @@
         query, key_value = 0.0, 0.0
         for col in range(4):
             normed = vals[col] * scale_r * gain[1:2, 256 * col : 256 * col + 256]
+            normed = normed.astype(bf16)
             for half_c in range(2):
-                lhs[24 + 2 * col + half_c, :, rows] = normed[:, 128 * half_c : 128 * half_c + 128].T.astype(bf16)
-            normed = normed.astype(bf16)
+                lhs[24 + 2 * col + half_c, :, rows] = normed[:, 128 * half_c : 128 * half_c + 128].T
             query = query + dot_f(normed, wgu[0, 256 * col : 256 * col + 256, :])
             key_value = key_value + dot_f(normed, wgu[1, 256 * col : 256 * col + 256, :])
         query = query.T
@@ -418,9 +418,10 @@
         for col in range(4):
             buf[rows, 256 * col : 256 * col + 256] = sums[col]
             normed = sums[col] * scale_r * gain[0:1, 256 * col : 256 * col + 256]
-            hbuf[rows, 256 * col : 256 * col + 256] = normed.astype(bf16)
+            normed = normed.astype(bf16)
+            hbuf[rows, 256 * col : 256 * col + 256] = normed
             for half_c in range(2):
-                lhs[16 + 2 * col + half_c, :, rows] = normed[:, 128 * half_c : 128 * half_c + 128].T.astype(bf16)
+                lhs[16 + 2 * col + half_c, :, rows] = normed[:, 128 * half_c : 128 * half_c + 128].T
         return carry
 
     def place_of(k):
@@ -462,7 +463,7 @@
         sigma = 1.0 / (1.0 + jnp.exp(-gate))
         silu = gate * sigma
         hidden = silu * up
-        hidden_t = (hidden * weight).T.astype(bf16)
+        hidden_t = (hidden * weight).astype(bf16).T
         d_hidden = d_raw * weight
         d_gate = (d_hidden * up * sigma * (1.0 + gate * (1.0 - sigma))).astype(bf16)
         d_up = (d_hidden * silu).astype(bf16)
@@ -523,9 +524,9 @@
         stage_d(direct_d[j])
 
     chores = {
-        4: [(h_share, 0), (h_share, 1)],
+        4: [(h_share, 0), (h_share, 1), (d_late, 2), (d_late, 3)],
         8: [(d_forward, 0)],
-        10: [(h_share, 2), (d_late, 2), (d_late, 3)],
+        10: [(h_share, 2)],
         14: [(h_share, 3)],
         16: [(d_direct, 0), (h_forward, 0)],
         18: [(d_forward, 1), (d_direct, 1)],
@@ -570,9 +571,10 @@
             whole = jnp.concatenate([ybuf[4 * (4 * b + j) + c] for j in range(4)], axis=0)
             rhs[12 + c, rows, :] = whole.astype(bf16)
             whole = jnp.concatenate([zbuf[4 * (4 * b + j) + c] for j in range(4)], axis=0)
-            rhs[26 + c, rows, :] = whole.astype(bf16)
+            whole = whole.astype(bf16)
+            rhs[26 + c, rows, :] = whole
             for half_c in range(2):
-                lhs[34 + 2 * c + half_c, :, rows] = whole[:, 128 * half_c : 128 * half_c + 128].T.astype(bf16)
+                lhs[34 + 2 * c + half_c, :, rows] = whole[:, 128 * half_c : 128 * half_c + 128].T
         unit(EARLY, b, "mate")
 
     next_weights(EARLY)

time: 469 us -> 469 us (level)
  no operation moved by 1% of the time
where the time goes in v11:
time: 469 us
  Pallas kernels  443 us (94%)
  local copies, waits for them, and re-layouts  24.2 us (5%)
    pallas_call x1, Pallas kernels, run_layer(): pl.pallas_call(functools.partial(layer_kernel, nz, hop, ring), out_shape=...  443 us
    unnamed x38, local copies, waits for them, and re-layouts  24.2 us

profile of v11, /device:TPU:0, one launch (start us, length us, event | category | flops | bytes accessed | tf_op | source)
XLA Modules:
  0.0 468.8 jit_solution(2459036421429470027)
XLA Ops:
  1.3 443.3 %shard_map.247 = (f32[16,1024,128]{2,1,0:T(8,128)}, f32[16,1024,128]{2,1,0:T(8,128)}, f32[16,128,1024]{2,1,0:T(8,128)}, f32[1024,256]{1,0:T(8,128)}, f32[1024,12...) custom-call(s32[1]{0:T(128)S(6)} %copy.40.length, ...), custom_call_target="tpu_custom_call" | custom-call | tf_op jit(solution)/shard_map/pallas_call | solution.py:1192
  444.6 0.0 copy-start.1
  444.6 0.0 copy-start.6
  444.6 0.0 copy-start.8
  444.6 0.0 copy-start.3
  444.6 0.0 copy-start.5
  444.6 0.0 copy-start.4
  444.6 0.0 copy-start.2
  444.6 3.2 copy.41
  447.9 0.0 copy-done.1
  447.9 0.0 copy-start
  447.9 1.3 copy.42
  449.2 0.0 copy-done.6
  449.2 0.0 copy-start.7
  449.2 0.6 copy.43
  449.8 0.0 copy-done.8
  449.8 0.6 copy.44
  450.4 0.0 copy-done.3
  450.4 1.0 copy.45
  451.4 0.0 copy-done.5
  451.4 0.8 copy.46
  452.2 0.0 copy-done.4
  452.2 0.0 slice-start.2
  452.2 0.8 copy.47
  453.0 0.0 copy-done.2
  453.0 1.0 copy.48
  454.0 0.0 copy-done.7
  454.0 0.6 copy.49
  454.6 0.0 copy-done
  454.6 0.0 slice-start.3
  454.6 0.0 slice-start
  454.6 4.3 copy.50
  458.8 0.0 slice-done.2
  458.8 1.0 slice-done.3
  459.8 0.0 slice-start.1
  459.8 4.3 copy.51
  464.1 0.0 slice-done
  464.1 1.4 slice-done.1
  465.4 3.4 copy.52
  (2 shorter events, 0.0 us)
Async XLA Ops:
  444.6 3.3 copy-start.1
  444.6 4.6 copy-start.6
  444.6 5.2 %copy-start.8 = (f32[8,128]{1,0:T(8,128)S(1)}, f32[8,128]{1,0:T(8,128)}, u32[]{:S(2)}) copy-start(f32[8,128]{1,0:T(8,128)} %get-tuple-element.27) | copy-start | bytes 12292
  444.6 5.8 %copy-start.3 = (f32[1024,256]{1,0:T(8,128)S(1)}, f32[1024,256]{1,0:T(8,128)}, u32[]{:S(2)}) copy-start(f32[1024,256]{1,0:T(8,128)} %get-tuple-element.52) | copy-start | bytes 3145732
  444.6 6.8 %copy-start.5 = (f32[1024,128]{1,0:T(8,128)S(1)}, f32[1024,128]{1,0:T(8,128)}, u32[]{:S(2)}) copy-start(f32[1024,128]{1,0:T(8,128)} %get-tuple-element.53) | copy-start | bytes 1572868
  444.6 7.6 %copy-start.4 = (f32[1024,128]{1,0:T(8,128)S(1)}, f32[1024,128]{1,0:T(8,128)}, u32[]{:S(2)}) copy-start(f32[1024,128]{1,0:T(8,128)} %get-tuple-element.54) | copy-start | bytes 1572868
  444.6 8.4 %copy-start.2 = (f32[256,1024]{1,0:T(8,128)S(1)}, f32[256,1024]{1,0:T(8,128)}, u32[]{:S(2)}) copy-start(f32[256,1024]{1,0:T(8,128)} %get-tuple-element.55) | copy-start | bytes 3145732
  447.9 6.7 %copy-start = (f32[16,1024,128]{2,1,0:T(8,128)S(1)}, f32[16,1024,128]{2,1,0:T(8,128)}, u32[]{:S(2)}) copy-start(f32[16,1024,128]{2,1,0:T(8,128)} %get-tuple-element.57) | copy-start | bytes 25165828
  449.2 4.8 %copy-start.7 = (f32[8,128]{1,0:T(8,128)S(1)}, f32[8,128]{1,0:T(8,128)}, u32[]{:S(2)}) copy-start(f32[8,128]{1,0:T(8,128)} %get-tuple-element.32) | copy-start | bytes 12292
  452.2 6.6 %slice-start.2 = ((s8[8388608]{0:T(1024)(128)(4,1)}), s8[4194304]{0:T(1024)(128)(4,1)S(1)}, s32[]{:S(2)}) async-start(s8[8388608]{0:T(1024)(128)(4,1)} %bitcast.9), calls=%async_computation.2 | async-start | bytes 8388608
  454.6 5.2 %slice-start.3 = ((s8[8388608]{0:T(1024)(128)(4,1)}), s8[4194304]{0:T(1024)(128)(4,1)S(1)}, s32[]{:S(2)}) async-start(s8[8388608]{0:T(1024)(128)(4,1)} %bitcast.9), calls=%async_computation.3 | async-start | bytes 8388608
  454.6 9.5 %slice-start = ((s8[8388608]{0:T(1024)(128)(4,1)}), s8[4194304]{0:T(1024)(128)(4,1)S(1)}, s32[]{:S(2)}) async-start(s8[8388608]{0:T(1024)(128)(4,1)} %bitcast.7), calls=%async_computation | async-start | bytes 8388608
  459.8 5.6 %slice-start.1 = ((s8[8388608]{0:T(1024)(128)(4,1)}), s8[4194304]{0:T(1024)(128)(4,1)S(1)}, s32[]{:S(2)}) async-start(s8[8388608]{0:T(1024)(128)(4,1)} %bitcast.7), calls=%async_computation.1 | async-start | bytes 8388608
